TPU v7x, 32 devices: a whole 2x2x4 slice. The times are simulated.
32 devices in a mesh: wide: 16 (over z, y, x), narrow: 2 (over core).
Axes of the slice: x: 2, y: 2, z: 4, core: 2. Of those that a mesh axis runs over, the one named last changes fastest.
Arguments:
- factor: bfloat16 [4, 2048, 4, 2048], P(None, 'wide', None, 'narrow'), may hold values from -0.0625 to 0.0625
- diag_inverse: float32 [4, 2048, 2048], P(None, 'wide', 'narrow'), as said below
- parent: int32 [15], replicated, may hold values from -1 to 14, as said below
- tile_node: int32 [4, 8], replicated, may hold values from 0 to 14, as said below
- structure: int32 [15, 4, 8], replicated, may hold values from 0 to 1, as said below
Outputs:
- selected_inverse: float32 [4, 2048, 4, 2048], P(None, 'wide', None, 'narrow')
Inputs may be any that keep to these rules, and one draw needn't show every extreme that they name: The tree is a complete binary tree of 4 levels; the root's entry is -1, every other supernode's entry is its parent. `tile_node`: level k holds the 2 ** k supernodes at depth k of the tree, each owning 8 / 2 ** k of the level's tile positions. `structure`: an entry is 1 only where the tile's supernode is a strict ancestor of supernode i (dimension 0). `diag_inverse`: Symmetric; each supernode's diagonal block is positive definite.
All inputs are finite; a program needn't handle non-finite values.
Results may differ from a plain program's by a relative error of at most 0.0016.
Values may be sent and summed in bfloat16 or wider, within the bound.
No kernel may reach another device: no remote copies, remote signals or barrier semaphores. Data moves between devices by JAX's collectives and lax.ppermute only.
A program may use at most 192 MiB of HBM per device.

v0:
```python
import jax
import jax.numpy as jnp
from jax import lax
from jax.sharding import PartitionSpec as P

LEV = 4
TILE = 256
LT = 8
M = 15


def spread_2(block, axis, source):
    block = jnp.where(lax.axis_index(axis) == source, block, jnp.zeros_like(block))
    return lax.psum(block, axis)


def ancestors(parent):
    node_ids = jnp.arange(M, dtype=jnp.int32)
    step_mat = (parent[:, None] == node_ids[None, :]).astype(jnp.float32)
    power_mat = step_mat
    reach = step_mat
    for hop_count in range(LEV - 2):
        power_mat = jnp.dot(power_mat, step_mat, precision=lax.Precision.HIGHEST)
        reach = reach + power_mat
    return reach


def spread(mask_tile):
    return jnp.repeat(mask_tile, TILE, axis=-1)


def fetch_panel(piece, col_id, group_size, col_count):
    row_block = lax.all_gather(piece, "narrow", axis=2, tiled=True)
    copies = [
        spread_2(row_block, "wide", col_id * group_size + member) for member in range(group_size)
    ]
    joined = jnp.concatenate(copies, axis=1)
    return joined.reshape(piece.shape[0] * col_count, LT * TILE)


def local(factor, diag_inverse, parent, tile_node, structure):
    wide_size = lax.axis_size("wide")
    narrow_size = lax.axis_size("narrow")
    group_size = wide_size // narrow_size
    row_count = factor.shape[1]
    col_count = factor.shape[3]
    col_tiles = col_count // TILE
    row_id = lax.axis_index("wide")
    col_id = lax.axis_index("narrow")
    high = lax.Precision.HIGHEST
    reach = ancestors(parent)
    node_hot = (tile_node[:, :, None] == jnp.arange(M, dtype=jnp.int32)[None, None, :]).astype(
        jnp.float32
    )
    row_pos = row_id * row_count // TILE
    pos_hot = (jnp.arange(LT, dtype=jnp.int32) == row_pos).astype(jnp.float32)
    row_hot = jnp.einsum("t,ltm->lm", pos_hot, node_hot, precision=high)
    col_sel = (
        jnp.arange(LT, dtype=jnp.int32)[None, :]
        == (col_id * col_tiles + jnp.arange(col_tiles, dtype=jnp.int32))[:, None]
    ).astype(jnp.float32)
    col_hot = jnp.einsum("jt,ltm->ljm", col_sel, node_hot, precision=high)
    tile_above = jnp.einsum("ra,ba,cjb->rcj", row_hot, reach, col_hot, precision=high)
    tile_same = jnp.einsum("lm,ljm->lj", row_hot, col_hot, precision=high)
    struct_row = jnp.einsum("mlt,t->ml", structure.astype(jnp.float32), pos_hot, precision=high)
    tile_struct = jnp.einsum("cjm,mr->rcj", col_hot, struct_row, precision=high)
    masked = factor * spread(tile_struct)[:, None, :, :].astype(jnp.bfloat16)
    sigma_loc = jnp.zeros((LEV, row_count, LEV, col_count), jnp.float32)
    sigma_loc = sigma_loc.at[0, :, 0, :].set(spread(tile_same[0])[None, :] * diag_inverse[0])
    for level_no in range(1, LEV):
        panel_mat = fetch_panel(masked[:level_no, :, level_no, :], col_id, group_size, col_count)
        known_bf = (
            sigma_loc[:level_no, :, :level_no, :]
            .reshape(level_no * row_count, level_no * col_count)
            .astype(jnp.bfloat16)
        )
        partial_value = jnp.dot(known_bf, panel_mat, preferred_element_type=jnp.float32)
        summed = lax.psum_scatter(partial_value, "narrow", scatter_dimension=1, tiled=True)
        above_mask = spread(tile_above[:level_no, level_no])[:, None, :]
        column = -(summed.reshape(level_no, row_count, col_count) * above_mask)
        sigma_loc = sigma_loc.at[:level_no, :, level_no, :].set(column)
        block_size = level_no * row_count * row_count
        pieces = column.reshape(level_no, row_count, group_size, row_count).transpose(2, 0, 3, 1)
        pieces = pieces.reshape(group_size, block_size)
        outgoing = lax.dynamic_update_slice(
            jnp.zeros((wide_size, pieces.shape[1]), jnp.float32), pieces, (col_id * group_size, 0)
        )
        arrived = lax.all_to_all(
            lax.all_to_all(outgoing, "wide", split_axis=0, concat_axis=0, tiled=True),
            "narrow",
            split_axis=0,
            concat_axis=0,
            tiled=True,
        )
        chosen = lax.dynamic_slice_in_dim(arrived, row_id // group_size * group_size, group_size, 0)
        mirror = (
            chosen.reshape(group_size, level_no, row_count, row_count)
            .transpose(2, 1, 0, 3)
            .reshape(row_count, level_no, col_count)
        )
        sigma_loc = sigma_loc.at[level_no, :, :level_no, :].set(mirror)
        mirror_bf = mirror.reshape(row_count, level_no * col_count).astype(jnp.bfloat16)
        inner_sum = jnp.dot(mirror_bf, panel_mat, preferred_element_type=jnp.float32)
        diag_sum = lax.psum_scatter(inner_sum, "narrow", scatter_dimension=1, tiled=True)
        same_mask = spread(tile_same[level_no])[None, :]
        sigma_loc = sigma_loc.at[level_no, :, level_no, :].set(
            same_mask * (diag_inverse[level_no] - diag_sum)
        )
    return sigma_loc


def solution(mesh):
    return jax.shard_map(
        local,
        mesh=mesh,
        in_specs=(P(None, "wide", None, "narrow"), P(None, "wide", "narrow"), P(), P(), P()),
        out_specs=P(None, "wide", None, "narrow"),
        check_vma=False,
    )
```

profile of v0, /device:TPU:0, one launch (start us, length us, event | category | flops | bytes accessed | tf_op | source)
XLA Modules:
  0.0 1540.6 jit_solution(12667376722272616793)
XLA Ops:
  8.7 4.6 copy_multiply_fusion
  13.4 2.0 copy-done.3
  16.3 2.1 slice.386
  19.4 2.3 all-gather
  21.7 2.0 select_bitcast_fusion.4
  23.7 4.4 all-gather.6.cloned.1.call-done
  28.1 2.7 select_bitcast_fusion.2
  30.8 4.0 fusion.15
  34.8 5.8 all-gather.8.cloned.1.call-done
  40.7 5.3 fusion.9
  46.0 1.9 select_bitcast_fusion
  49.0 1144.2 %all-reduce.4.cloned.1.call-done = (bf16[1,128,2048]{2,1,0:T(8,128)(2,1)}, bf16[1,128,2048]{2,1,0:T(8,128)(2,1)}, bf16[1,128,2048]{2,1,0:T(8,128)(2,1)}, bf16[1,...) async-done(((bf16[1,128,2048]{2,1,0:T(8,128)(2,1)}, ...) | async-done | bytes 25165840 | tf_op jit(solution)/shard_map/psum | solution.py:14
  1193.2 1.2 constant_dynamic-update-slice_fusion.7
  1194.4 1.2 constant_dynamic-update-slice_fusion.6
  1198.1 2.0 copy-done.1
  1200.1 1.7 fusion.2
  1203.5 4.3 scatter.34
  1207.8 1.4 and_reduce_fusion.2
  1209.2 3.8 reduce-scatter.7.cloned.1.call-done
  1213.0 3.3 fusion.17
  1216.5 1.9 all_to_all.48
  1219.2 6.8 all-to-all-start
  1226.0 24.6 %all-to-all-done = f32[16,1,16384]{2,1,0:T(1,128)S(1)} async-done(((f32[16,1,16384]{2,1,0:T(1,128)}), f32[16,1,16384]{2,1,0:T(1,128)S(1)}, u32[]{:S(2)}, u32[]{:S(2)}) %all-to-all-start) | async-done | bytes 1048608 | tf_op jit(solution)/shard_map/all_to_all | solution.py:89
  1251.2 4.7 all_to_all.72
  1256.0 1.7 fusion
  1258.0 2.5 constant_dynamic-update-slice_fusion.15
  1260.5 2.4 constant_dynamic-update-slice_fusion.14
  1270.0 1.9 bitcast_dynamic-update-slice_fusion.2
  1272.0 1.7 slice.406
  1275.1 7.1 fusion.52
  1282.3 10.7 reduce-scatter.11.cloned.1.call-done
  1293.0 1.4 copy.164
  1295.0 3.1 all_to_all.54
  1299.2 6.8 all-to-all-start.2
  1306.8 1.9 and_reduce_fusion.1
  1308.7 2.8 constant_dynamic-update-slice_fusion.23
  1311.5 37.7 %all-to-all-done.2 = f32[16,1,32768]{2,1,0:T(1,128)S(1)} async-done(((f32[16,1,32768]{2,1,0:T(1,128)}), f32[16,1,32768]{2,1,0:T(1,128)S(1)}, u32[]{:S(2)}, u32[]{:S(2)}) %all-to-all-start.2) | async-done | bytes 2097184 | tf_op jit(solution)/shard_map/all_to_all | solution.py:89
  1349.2 1.2 copy.183
  1350.5 5.4 all_to_all.73
  1356.5 5.7 fusion.53
  1362.4 2.9 constant_dynamic-update-slice_fusion.22
  1365.4 1.2 constant_dynamic-update-slice_fusion.21
  1366.6 1.3 constant_dynamic-update-slice_fusion.20
  1367.9 1.3 constant_dynamic-update-slice_fusion.19
  1369.2 1.3 constant_dynamic-update-slice_fusion.18
  1370.5 1.3 constant_dynamic-update-slice_fusion.17
  1371.8 1.2 constant_dynamic-update-slice_fusion.16
  1373.0 4.3 select_dynamic-update-slice_fusion.1
  1378.6 2.1 bitcast_dynamic-update-slice_fusion.1
  1380.6 2.9 slice.405
  1383.5 2.1 copy.129
  1386.8 6.8 fusion.54
  1393.8 15.6 %reduce-scatter.15.cloned.1.call-done = f32[384,1024]{1,0:T(8,128)} async-done(((f32[384,2048]{1,0:T(8,128)}), f32[384,1024]{1,0:T(8,128)}) %reduce-scatter.15.cloned.1.call-update) | async-done | bytes 1572880 | tf_op jit(solution)/shard_map/reduce_scatter | solution.py:78
  1409.4 1.7 copy.169
  1411.9 2.4 all_to_all.60
  1414.5 78.2 %all_to_all.74 = f32[16,1,49152]{2,1,0:T(1,128)S(1)} all-to-all(f32[16,1,49152]{2,1,0:T(1,128)S(1)} %constant_dynamic-update-slice_fusion.25), channel_id=1, replica_groups=mesh['wide'=16,'narrow'=2] {'wide'}, dimensions={0} | all-to-all | bytes 6291456 | tf_op jit(solution)/shard_map/all_to_all | solution.py:89
  1492.7 1.8 copy.182
  1494.6 6.3 all_to_all.75
  1502.4 7.7 fusion.55
  1510.9 2.0 and_reduce_fusion
  1513.0 4.9 select_dynamic-update-slice_fusion
  1518.1 1.3 constant_dynamic-update-slice_fusion.24
  1519.4 2.1 bitcast_dynamic-update-slice_fusion
  1521.4 12.2 copy.147
  (156 shorter events, 29.1 us)
Async XLA Ops:
  6.5 21.6 %all-gather.6.cloned.1.call-start = ((), (), s32[]{:S(2)}) async-start(), calls=%async_computation.18 | async-start | bytes 1572864 | tf_op jit(solution)/shard_map/all_gather | solution.py:33
  13.3 2.0 copy-start.3
  16.2 24.4 %all-gather.8.cloned.1.call-start = ((), (), s32[]{:S(2)}) async-start(), calls=%async_computation.19 | async-start | bytes 2359296 | tf_op jit(solution)/shard_map/all_gather | solution.py:33
  18.4 1174.8 %all-reduce.4.cloned.1.call-start = ((), (), s32[]{:S(2)}) async-start(), calls=%async_computation.20 | async-start | bytes 50331648 | tf_op jit(solution)/shard_map/psum | solution.py:14
  40.7 5.3 copy-start.4
  47.9 0.7 copy-start.27
  47.9 1165.1 %reduce-scatter.7.cloned.1.call-start = ((), (), s32[]{:S(2)}) async-start(), calls=%async_computation.12 | async-start | bytes 1572864 | tf_op jit(solution)/shard_map/reduce_scatter | solution.py:78
  1193.2 4.7 copy-start.23
  1193.2 4.7 copy-start.22
  1193.2 4.8 copy-start.21
  1193.2 4.9 copy-start.20
  1193.2 6.9 copy-start.7
  1198.0 3.8 copy-start.28
  1198.1 2.0 copy-start.1
  1203.5 4.3 copy-start.26
  1219.2 31.4 %all-to-all-start = ((f32[16,1,16384]{2,1,0:T(1,128)}), f32[16,1,16384]{2,1,0:T(1,128)S(1)}, u32[]{:S(2)}, u32[]{:S(2)}) async-start(f32[16,1,16384]{2,1,0:T(1,128)} %constant_dynamic-update-slice_fusion.29), calls=%async_computation.1 | async-start | bytes 2097152 | tf_op jit(solution)/shard_map/all_to_all | solution.py:89
  1225.9 44.1 %reduce-scatter.9.cloned.1.call-start = ((), (), s32[]{:S(2)}) async-start(), calls=%async_computation.13 | async-start | bytes 1572864 | tf_op jit(solution)/shard_map/reduce_scatter | solution.py:104
  1250.6 5.4 copy-start.2
  1257.7 35.3 %reduce-scatter.11.cloned.1.call-start = ((), (), s32[]{:S(2)}) async-start(), calls=%async_computation.14 | async-start | bytes 3145728 | tf_op jit(solution)/shard_map/reduce_scatter | solution.py:78
  1258.0 4.9 copy-start.19
  1258.0 5.9 copy-start.18
  1258.0 6.9 copy-start.17
  1260.5 5.5 copy-start.16
  1262.9 4.2 copy-start.15
  1263.9 4.2 copy-start.14
  1295.0 11.8 copy-start.25
  1299.2 50.0 %all-to-all-start.2 = ((f32[16,1,32768]{2,1,0:T(1,128)}), f32[16,1,32768]{2,1,0:T(1,128)S(1)}, u32[]{:S(2)}, u32[]{:S(2)}) async-start(f32[16,1,32768]{2,1,0:T(1,128)} %constant_dynamic-update-slice_fusion.27), calls=%async_computation.5 | async-start | bytes 4194304 | tf_op jit(solution)/shard_map/all_to_all | solution.py:89
  1306.0 72.5 %reduce-scatter.13.cloned.1.call-start = ((), (), s32[]{:S(2)}) async-start(), calls=%async_computation.15 | async-start | bytes 1572864 | tf_op jit(solution)/shard_map/reduce_scatter | solution.py:104
  1362.1 4.5 copy-start.12
  1362.2 47.2 %reduce-scatter.15.cloned.1.call-start = ((), (), s32[]{:S(2)}) async-start(), calls=%async_computation.16 | async-start | bytes 4718592 | tf_op jit(solution)/shard_map/reduce_scatter | solution.py:78
  1362.4 3.0 copy-start.13
  1362.4 5.5 copy-start.11
  1365.4 3.8 copy-start.10
  1366.6 3.8 copy-start.9
  1367.9 3.9 copy-start.8
  1369.2 3.8 copy-start.6
  1380.6 6.1 copy-start
  1393.6 125.7 %reduce-scatter.17.cloned.1.call-start = ((), (), s32[]{:S(2)}) async-start(), calls=%async_computation.17 | async-start | bytes 1572864 | tf_op jit(solution)/shard_map/reduce_scatter | solution.py:104
  1502.4 8.5 copy-start.24
  1502.4 10.6 copy-start.5
Sparse Core Ops, SparseCore 0:
  16.3 11.7 all-gather.5
  29.7 10.9 all-gather.7
  48.0 1145.0 all-reduce.3
  1202.0 10.9 reduce-scatter.6
  1257.9 9.5 reduce-scatter.8
  1282.4 10.6 reduce-scatter.10
  1362.3 13.2 reduce-scatter.12
  1393.7 15.5 reduce-scatter.14
  1510.3 6.9 reduce-scatter.16
where the time goes:
time: 1550 us; the launch traced here: 1540 us
  waiting for transfers between devices  1250 us (81%)
  blocking collectives  96.9 us (6%)
  local copies, waits for them, and re-layouts  89.4 us (6%)
  other arithmetic  44.9 us (3%)
  matrix products  34 us (2%)
    psum x1, waiting for transfers between devices, spread_2(): return lax.psum(block, axis)  1140 us
    all_to_all x1, blocking collectives, local(): lax.all_to_all(outgoing, 'wide', split_axis=0, concat_axis=0, tiled=True)  78.2 us
    all_to_all x2, waiting for transfers between devices, local(): lax.all_to_all(outgoing, 'wide', split_axis=0, concat_axis=0, tiled=True)  62.3 us
    unnamed x103, local copies, waits for them, and re-layouts  41.1 us
  transfers between devices with their start and end apart: 11, of which 8 were waited for; matrix products, arithmetic and copies ran while one was open for 4% of the time, Pallas kernels for 0%

commit v1 on v0

v1 whole, which is shorter than its diff:
```python
import jax
import jax.numpy as jnp
from jax import lax
from jax.sharding import PartitionSpec as P

LEV = 4
TILE = 256
LT = 8
M = 15
BF = jnp.bfloat16
F32 = jnp.float32


def ancestors(parent):
    node_ids = jnp.arange(M, dtype=jnp.int32)
    step_mat = (parent[:, None] == node_ids[None, :]).astype(jnp.float32)
    power_mat = step_mat
    reach = step_mat
    for hop_count in range(LEV - 2):
        power_mat = jnp.dot(power_mat, step_mat, precision=lax.Precision.HIGHEST)
        reach = reach + power_mat
    return reach


def spread(mask_tile):
    return jnp.repeat(mask_tile, TILE, axis=-1)


def narrow_all(x, axis):
    size = lax.axis_size("narrow")
    mine = lax.axis_index("narrow")
    if size == 2:
        other = lax.ppermute(x, "narrow", [(0, 1), (1, 0)])
        first = mine == 0
        return jnp.concatenate([jnp.where(first, x, other), jnp.where(first, other, x)], axis=axis)
    shape = list(x.shape)
    width = shape[axis]
    shape[axis] = width * size
    out = jnp.zeros(shape, x.dtype)
    for hop in range(size):
        got = x if hop == 0 else lax.ppermute(x, "narrow", [(i, (i + hop) % size) for i in range(size)])
        out = lax.dynamic_update_slice_in_dim(out, got, (mine - hop) % size * width, axis)
    return out


def wide_all(x):
    wide = lax.axis_size("wide")
    narrow = lax.axis_size("narrow")
    row_id = lax.axis_index("wide")
    depth = wide // 4
    z, y_id, x_id = row_id // 4, row_id // 2 % 2, row_id % 2
    l, r, c = x.shape
    line = jnp.zeros((l, depth, r, c), x.dtype)
    for hop in range(depth):
        got = x
        if hop:
            got = lax.ppermute(x, "wide", [(i, (i + 4 * hop) % wide) for i in range(wide)])
        line = lax.dynamic_update_slice(line, got[:, None], (0, (z - hop) % depth, 0, 0))

    def swap(value, turn):
        pairs = []
        for i in range(wide):
            for j in range(narrow):
                pairs.append((i * narrow + j, (i ^ (1 if (j + turn) % 2 == 0 else 2)) * narrow + j))
        return lax.ppermute(value, ("wide", "narrow"), pairs)

    even = lax.axis_index("narrow") % 2 == 0
    near = swap(line, 0)
    far = swap(jnp.stack([line, near]), 1)
    out = jnp.zeros((l, depth, 2, 2, r, c), x.dtype)
    near_y, near_x = jnp.where(even, y_id, 1 - y_id), jnp.where(even, 1 - x_id, x_id)
    far_y, far_x = jnp.where(even, 1 - y_id, y_id), jnp.where(even, x_id, 1 - x_id)
    for piece, yy, xx in (
        (line, y_id, x_id),
        (near, near_y, near_x),
        (far[0], far_y, far_x),
        (far[1], 1 - y_id, 1 - x_id),
    ):
        out = lax.dynamic_update_slice(out, piece[:, :, None, None], (0, 0, yy, xx, 0, 0))
    return out.reshape(l, wide * r, c)


def mirrored(full):
    wide = lax.axis_size("wide")
    narrow = lax.axis_size("narrow")
    l, r, cols = full.shape
    part = r // narrow
    mine = lax.dynamic_slice_in_dim(full, lax.axis_index("narrow") * part, part, 1)
    slots = mine.reshape(l, part, wide, r).transpose(2, 0, 1, 3)
    got = lax.all_to_all(slots, "wide", split_axis=0, concat_axis=0, tiled=True)
    whole = narrow_all(got, 2)
    return whole.transpose(3, 1, 0, 2).reshape(r, l, cols)


def local(factor, diag_inverse, parent, tile_node, structure):
    row_count = factor.shape[1]
    col_count = factor.shape[3]
    col_tiles = col_count // TILE
    row_id = lax.axis_index("wide")
    col_id = lax.axis_index("narrow")
    high = lax.Precision.HIGHEST
    reach = ancestors(parent)
    node_hot = (tile_node[:, :, None] == jnp.arange(M, dtype=jnp.int32)[None, None, :]).astype(
        jnp.float32
    )
    row_pos = row_id * row_count // TILE
    pos_hot = (jnp.arange(LT, dtype=jnp.int32) == row_pos).astype(jnp.float32)
    row_hot = jnp.einsum("t,ltm->lm", pos_hot, node_hot, precision=high)
    col_sel = (
        jnp.arange(LT, dtype=jnp.int32)[None, :]
        == (col_id * col_tiles + jnp.arange(col_tiles, dtype=jnp.int32))[:, None]
    ).astype(jnp.float32)
    col_hot = jnp.einsum("jt,ltm->ljm", col_sel, node_hot, precision=high)
    tile_above = jnp.einsum("ra,ba,cjb->rcj", row_hot, reach, col_hot, precision=high)
    tile_same = jnp.einsum("lm,ljm->lj", row_hot, col_hot, precision=high)
    struct_row = jnp.einsum("mlt,t->ml", structure.astype(jnp.float32), pos_hot, precision=high)
    tile_struct = jnp.einsum("cjm,mr->rcj", col_hot, struct_row, precision=high)

    panels = {}
    for level in range(1, LEV):
        mask = spread(tile_struct[:level, level])[:, None, :].astype(BF)
        panels[level] = wide_all(factor[:level, :, level, :] * mask)

    blocks = {(0, 0): spread(tile_same[0])[None, :] * diag_inverse[0]}
    rows = {0: [narrow_all(blocks[0, 0].astype(BF), 1)]}
    for level in range(1, LEV):
        panel = panels[level].reshape(level * LT * TILE, col_count)
        known = jnp.concatenate([jnp.concatenate(rows[k], axis=1) for k in range(level)], axis=0)
        product = jnp.dot(known, panel, preferred_element_type=F32)
        above = spread(tile_above[:level, level])[:, None, :]
        column = -(product.reshape(level, row_count, col_count) * above)
        for k in range(level):
            blocks[k, level] = column[k]
        full = narrow_all(column.astype(BF), 2)
        for k in range(level):
            rows[k].append(full[k])
        mirror = mirrored(full)
        here = lax.dynamic_slice_in_dim(mirror, col_id * col_count, col_count, 2).astype(F32)
        for k in range(level):
            blocks[level, k] = here[:, k]
        inner = jnp.dot(
            mirror.reshape(row_count, level * LT * TILE), panel, preferred_element_type=F32
        )
        blocks[level, level] = spread(tile_same[level])[None, :] * (diag_inverse[level] - inner)
        if level < LEV - 1:
            rows[level] = [mirror[:, k] for k in range(level)]
            rows[level].append(narrow_all(blocks[level, level].astype(BF), 1))
    return jnp.stack(
        [jnp.stack([blocks[k, m] for m in range(LEV)], axis=1) for k in range(LEV)], axis=0
    )


def solution(mesh):
    return jax.shard_map(
        local,
        mesh=mesh,
        in_specs=(P(None, "wide", None, "narrow"), P(None, "wide", "narrow"), P(), P(), P()),
        out_specs=P(None, "wide", None, "narrow"),
        check_vma=False,
    )
```

time: 1550 us -> 474 us (0.31)
  waiting for transfers between devices: 1250 us -> 168 us
  blocking collectives: 96.9 us -> 0 us
  starting transfers between devices: 14.3 us -> 78.8 us
  other arithmetic: 44.9 us -> 82.3 us
    psum x1 -> x0, waiting for transfers between devices: 1140 us -> none  [spread_2(): return lax.psum(block, axis)]
    all_to_all x4 -> x0, blocking collectives: 94.6 us -> none  [the longest x1 78.2 us: local(): lax.all_to_all(outgoing, 'wide', split_axis=0, concat_axis=0, tiled=True)]
    ppermute x0 -> x24, waiting for transfers between devices: none -> 83 us  [the longest x9 73.1 us: wide_all(): lax.ppermute(x, 'wide', [(i, (i + 4 * hop) % wide) for i in range(wide)])]
    concatenate x0 -> x7, other arithmetic: none -> 41.8 us  [the longest x2 41.5 us: local(): jnp.concatenate([jnp.concatenate(rows[k], axis=1) for k in range(level)],...]
    dynamic_update_slice x3 -> x21, local copies, waits for them, and re-layouts: 2.12 us -> 39 us  [the longest x12 28.9 us: wide_all(): lax.dynamic_update_slice(out, piece[:, :, None, None], (0, 0, yy, xx, 0, 0))]
    all_to_all x2 -> x3, starting transfers between devices: 13.5 us -> 50 us  [mirrored(): got = lax.all_to_all(slots, 'wide', split_axis=0, concat_axis=0, tiled=True)]
    reduce_scatter x6 -> x0, waiting for transfers between devices: 30.1 us -> none  [the longest x3 30 us: local(): lax.psum_scatter(partial_value, 'narrow', scatter_dimension=1, tiled=True)]
    ppermute x0 -> x24, starting transfers between devices: none -> 28.9 us  [the longest x9 18.8 us: wide_all(): lax.ppermute(x, 'wide', [(i, (i + 4 * hop) % wide) for i in range(wide)])]
  transfers between devices with their start and end apart: 11 -> 27, of which waited for: 8 -> 12; matrix products, arithmetic and copies ran while one was open for 4% -> 34% of each run, Pallas kernels for 0% -> 0%
where the time goes in v1:
time: 474 us; the launch traced here: 464 us
  waiting for transfers between devices  168 us (35%)
  local copies, waits for them, and re-layouts  98 us (21%)
  other arithmetic  82.3 us (17%)
  starting transfers between devices  78.8 us (17%)
  matrix products  35.3 us (7%)
    all_to_all x3, waiting for transfers between devices, mirrored(): got = lax.all_to_all(slots, 'wide', split_axis=0, concat_axis=0, tiled=True)  85.4 us
    ppermute x9, waiting for transfers between devices, wide_all(): lax.ppermute(x, 'wide', [(i, (i + 4 * hop) % wide) for i in range(wide)])  73.1 us
    all_to_all x3, starting transfers between devices, mirrored(): got = lax.all_to_all(slots, 'wide', split_axis=0, concat_axis=0, tiled=True)  50 us
    concatenate x2, other arithmetic, local(): jnp.concatenate([jnp.concatenate(rows[k], axis=1) for k in range(level)],...  41.5 us
    dynamic_update_slice x12, local copies, waits for them, and re-layouts, wide_all(): lax.dynamic_update_slice(out, piece[:, :, None, None], (0, 0, yy, xx, 0, 0))  28.9 us
    ppermute x9, starting transfers between devices, wide_all(): lax.ppermute(x, 'wide', [(i, (i + 4 * hop) % wide) for i in range(wide)])  18.8 us
    dot_general x3, matrix products, local(): product = jnp.dot(known, panel, preferred_element_type=F32)  17.2 us
    dot_general x3, matrix products, local(): jnp.dot(mirror.reshape(row_count, level * LT * TILE), panel, preferred_el...  15 us
  transfers between devices with their start and end apart: 27, of which 12 were waited for; matrix products, arithmetic and copies ran while one was open for 34% of the time, Pallas kernels for 0%

profile of v1, /device:TPU:0, one launch (start us, length us, event | category | flops | bytes accessed | tf_op | source)
XLA Modules:
  0.0 464.2 jit_solution(6313150707411796554)
XLA Ops:
  2.2 2.7 slice.115
  5.8 3.0 collective-permute-start.9
  8.9 2.6 collective-permute-start.10
  11.5 1.3 collective-permute-start.11
  12.8 1.8 slice.108
  16.5 3.6 slice.127
  20.4 1.6 broadcast_in_dim.117
  26.3 25.9 %collective-permute-done.1 = bf16[1,128,1024]{2,1,0:T(8,128)(2,1)} collective-permute-done((bf16[1,128,1024]{2,1,0:T(8,128)(2,1)}, bf16[1,128,1024]{2,1,0:T(8,128)(2,1)}, u32[]{:S(2)}, u32[]{:S(2)}) %collective-permute-start.1) | collective-permute-done | bytes 262176 | tf_op jit(solution)/shard_map/ppermute | solution.py:57
  53.2 20.6 %collective-permute-done.2 = bf16[1,128,1024]{2,1,0:T(8,128)(2,1)} collective-permute-done((bf16[1,128,1024]{2,1,0:T(8,128)(2,1)}, bf16[1,128,1024]{2,1,0:T(8,128)(2,1)}, u32[]{:S(2)}, u32[]{:S(2)}) %collective-permute-start.2) | collective-permute-done | bytes 262176 | tf_op jit(solution)/shard_map/ppermute | solution.py:57
  73.8 4.5 collective-permute-start.17
  79.4 1.6 collective-permute-start.4
  81.3 3.4 collective-permute-start.18
  84.7 1.9 bitcast_dynamic-update-slice_fusion.12
  86.6 1.9 bitcast_dynamic-update-slice_fusion.11
  88.5 1.9 bitcast_dynamic-update-slice_fusion.10
  90.9 3.4 collective-permute-done.4
  95.2 1.5 pad_maximum_fusion.3
  96.7 1.5 collective-permute-start.5
  98.7 1.8 bitcast_dynamic-update-slice_fusion.9
  100.5 2.9 collective-permute-start.19
  106.6 25.8 %collective-permute-done.18 = bf16[3,128,1024]{2,1,0:T(8,128)(2,1)} collective-permute-done((bf16[3,128,1024]{2,1,0:T(8,128)(2,1)}, bf16[3,128,1024]{2,1,0:T(8,128)(2,1)}, u32[]{:S(2)}, u32[]{:S(2)}) %collective-permute-start.18) | collective-permute-done | bytes 786464 | tf_op jit(solution)/shard_map/ppermute | solution.py:57
  136.1 4.6 pad_maximum_fusion.2
  140.7 1.7 collective-permute-start.13
  145.1 2.1 copy-done
  149.5 1.9 collective-permute-done.6
  154.2 16.7 %all-to-all-start = ((bf16[16,1,64,128]{3,2,1,0:T(8,128)(2,1)}), bf16[16,1,64,128]{3,2,1,0:T(8,128)(2,1)}, u32[]{:S(2)}, u32[]{:S(2)}) async-start(bf16[16,1,64,128]{3,2,1,0:T(8,128)(2,1)} %copy.42), calls=%async_computation | async-start | bytes 524288 | tf_op jit(solution)/shard_map/all_to_all | solution.py:90
  170.9 4.5 broadcast_in_dim.116
  175.4 3.1 bitcast_dynamic-update-slice_fusion.3
  178.5 41.5 %all-to-all-done = bf16[16,1,64,128]{3,2,1,0:T(8,128)(2,1)} async-done(((bf16[16,1,64,128]{3,2,1,0:T(8,128)(2,1)}), bf16[16,1,64,128]{3,2,1,0:T(8,128)(2,1)}, u32[]{:S(2)}, u32[]{:S(2)}) %all-to-all-start) | async-done | bytes 262176 | tf_op jit(solution)/shard_map/all_to_all | solution.py:90
  220.0 1.4 collective-permute-start.7
  221.4 3.1 bitcast_dynamic-update-slice_fusion.2
  224.4 1.9 fusion.13
  227.4 2.9 fusion.47
  230.4 5.2 %pad_maximum_fusion.1 = bf16[2,3,4,128,1024]{4,3,2,1,0:T(8,128)(2,1)} fusion(bf16[1,3,4,128,1024]{4,3,2,1,0:T(8,128)(2,1)} %bitcast.94, bf16[1,3,4,128,1024]{4,3,2,1,0:T(8,128)(2,1)S(1)} %bitcast.313), kind=kLoop, calls=%fused_computation.1 | loop fusion | flops 3145728 | bytes 12582912 | tf_op jit(solution)/shard_map/stack | solution.py:69
  236.5 2.1 copy.78
  239.6 1.6 maximum_maximum_fusion.1
  241.3 3.1 fusion.3
  244.4 3.1 fusion.2
  247.5 6.8 %fusion.48 = (bf16[2,128,1024]{2,1,0:T(8,128)(2,1)S(1)}, f32[2,128,1024]{2,1,0:T(8,128)}) fusion(f32[2,1024]{1,0:T(2,128)S(1)} %bitcast.351, bf16[2,128,4096]{2,1,0:T(8,128)(2,1)S(1)} %bitcast.330, bf16[4096,1024,1]{1,0,2:T(8,128)(2,1)} %bitcast.64), kind=kOutput, calls=%fused_computation.166 | convolution fusion | flops 2148270080 | bytes 12066816 | tf_op jit(solution)/shard_map/dot_general | solution.py:129
  255.1 1.5 collective-permute-done.14
  258.9 16.7 %all-to-all-start.1 = ((bf16[16,2,64,128]{3,2,1,0:T(8,128)(2,1)}), bf16[16,2,64,128]{3,2,1,0:T(8,128)(2,1)}, u32[]{:S(2)}, u32[]{:S(2)}) async-start(bf16[16,2,64,128]{3,2,1,0:T(8,128)(2,1)} %copy.53), calls=%async_computation.1 | async-start | bytes 1048576 | tf_op jit(solution)/shard_map/all_to_all | solution.py:90
  275.8 6.2 %broadcast_in_dim.126 = bf16[3,4,2,2,128,1024]{5,4,3,2,1,0:T(8,128)(2,1)} broadcast(bf16[]{:T(256)} %constant.134.clone.1), dimensions={} | broadcast | bytes 12582914 | tf_op jit(solution)/shard_map/broadcast_in_dim | solution.py:70
  282.0 2.2 bitcast_dynamic-update-slice_fusion.1
  284.2 28.3 %all-to-all-done.1 = bf16[16,2,64,128]{3,2,1,0:T(8,128)(2,1)} async-done(((bf16[16,2,64,128]{3,2,1,0:T(8,128)(2,1)}), bf16[16,2,64,128]{3,2,1,0:T(8,128)(2,1)}, u32[]{:S(2)}, u32[]{:S(2)}) %all-to-all-start.1) | async-done | bytes 524320 | tf_op jit(solution)/shard_map/all_to_all | solution.py:90
  313.7 3.8 bitcast_dynamic-update-slice_fusion
  319.8 5.5 %fusion.49 = (bf16[128,1024]{1,0:T(8,128)(2,1)S(1)}, f32[128,1024]{1,0:T(8,128)}) fusion(bf16[128,4096]{0,1:T(8,128)(2,1)S(1)} %bitcast.314, bf16[4096,1024]{1,0:T(8,128)(2,1)} %bitcast.63, f32[4,128,1024]{2,1,0:T(8,128)} %param.6, f32[1024]{0:T(1024)S(1)} %bitcast.347), kind=kOutput, calls=%fused_computation.167 | convolution fusion | flops 1074135040 | bytes 10752000 | tf_op jit(solution)/shard_map/dot_general | solution.py:141
  326.9 2.0 copy.84
  329.0 2.0 copy.85
  332.1 39.8 %maximum_maximum_fusion = bf16[384,6144]{1,0:T(8,128)(2,1)S(1)} fusion(bf16[128,1024]{1,0:T(8,128)(2,1)S(1)} %get-tuple-element.23, bf16[128,1024]{1,0:T(8,128)(2,1)S(1)} %get-tuple-element.22, bf16[128,2048]{1,0:T(8,128)(2,1)} %bitcast.329, bf16[128,2048]{1,0:T(8,128)(2,1)} %bitcast.328, bf16[128,2048]{1,0:T(8,128)(2,1)} %get-tuple-element.15, ...), kind=kLoop, calls=%fused_computation.2 | loop fusion | flops 56623104 | bytes 9437184 | tf_op jit(solution)/shard_map/concatenate | solution.py:128
  371.9 3.9 fusion.1
  375.8 3.8 fusion
  379.6 9.6 %fusion.50 = (bf16[3,128,1024]{2,1,0:T(8,128)(2,1)S(1)}, f32[3,128,1024]{2,1,0:T(8,128)}) fusion(f32[3,1024]{1,0:T(4,128)S(1)} %bitcast.348, bf16[3,128,6144]{2,1,0:T(8,128)(2,1)S(1)} %bitcast.324, bf16[6144,1024,1]{1,0,2:T(8,128)(2,1)} %bitcast.309), kind=kOutput, calls=%fused_computation.168 | convolution fusion | flops 4833017856 | bytes 19673088 | tf_op jit(solution)/shard_map/dot_general | solution.py:129
  389.3 2.3 collective-permute-done.22
  393.1 16.5 %all-to-all-start.2 = ((bf16[16,3,64,128]{3,2,1,0:T(8,128)(2,1)}), bf16[16,3,64,128]{3,2,1,0:T(8,128)(2,1)S(1)}, u32[]{:S(2)}, u32[]{:S(2)}) async-start(bf16[16,3,64,128]{3,2,1,0:T(8,128)(2,1)} %copy.68), calls=%async_computation.2 | async-start | bytes 1572864 | tf_op jit(solution)/shard_map/all_to_all | solution.py:90
  409.7 1.9 bitcast_multiply_fusion.5
  411.8 2.3 slice_bitcast_fusion.10
  414.2 15.6 %all-to-all-done.2 = bf16[16,3,64,128]{3,2,1,0:T(8,128)(2,1)S(1)} async-done(((bf16[16,3,64,128]{3,2,1,0:T(8,128)(2,1)}), bf16[16,3,64,128]{3,2,1,0:T(8,128)(2,1)S(1)}, u32[]{:S(2)}, u32[]{:S(2)}) %all-to-all-start.2) | async-done | bytes 786464 | tf_op jit(solution)/shard_map/all_to_all | solution.py:90
  431.1 1.6 slice_bitcast_fusion.9
  432.7 1.5 maximum_bitcast_fusion.2
  434.2 1.5 maximum_bitcast_fusion
  435.7 1.5 maximum_bitcast_fusion.1
  439.1 6.6 %fusion.8 = f32[128,1,1024]{2,0,1:T(8,128)S(1)} fusion(bf16[128,6144]{0,1:T(8,128)(2,1)S(1)} %bitcast.318, bf16[6144,1024]{1,0:T(8,128)(2,1)} %bitcast.310, f32[4,128,1024]{2,1,0:T(8,128)} %param.6, f32[1024]{0:T(1024)S(1)} %bitcast.345), kind=kOutput, calls=%fused_computation.40 | convolution fusion | flops 1610874880 | bytes 15208448 | tf_op jit(solution)/shard_map/dot_general | solution.py:141
  447.9 3.6 pad_maximum_fusion
  451.6 12.2 %copy.73 = f32[4,128,4,1024]{3,2,1,0:T(4,128)} copy(f32[4,128,4,1024]{3,1,2,0:T(8,128)} %pad_maximum_fusion) | data formatting | bytes 16777216 | tf_op jit(solution)/shard_map/stack | solution.py:148
  (194 shorter events, 48.0 us)
Async XLA Ops:
  2.1 18.0 %copy-start.33 = (s32[4,8]{1,0:T(4,128)S(1)}, s32[4,8]{1,0:T(4,128)}, u32[]{:S(2)}) copy-start(s32[4,8]{1,0:T(4,128)} %param.8) | copy-start | bytes 388
  5.8 75.4 %collective-permute-start.9 = (bf16[2,128,1024]{2,1,0:T(8,128)(2,1)}, bf16[2,128,1024]{2,1,0:T(8,128)(2,1)}, u32[]{:S(2)}, u32[]{:S(2)}) collective-permute-start(bf16[2,128,1024]{2,1,0:T(8,128)(2,1)} %bitcast_multiply_fusion.2), channel_id=1, source_target_pairs={{0,8},{2,10},{4,12},{6,14},{8,16},{10,18},{12,20},{14,22},{16,24},... | collective-permute-start | bytes 1572872 | tf_op jit(solution)/shard_map/ppermute | solution.py:57
  8.9 77.7 %collective-permute-start.10 = (bf16[2,128,1024]{2,1,0:T(8,128)(2,1)}, bf16[2,128,1024]{2,1,0:T(8,128)(2,1)}, u32[]{:S(2)}, u32[]{:S(2)}) collective-permute-start(bf16[2,128,1024]{2,1,0:T(8,128)(2,1)} %bitcast_multiply_fusion.2), channel_id=1, source_target_pairs={{0,16},{2,18},{4,20},{6,22},{8,24},{10,26},{12,28},{14,30},{16,0},... | collective-permute-start | bytes 1572872 | tf_op jit(solution)/shard_map/ppermute | solution.py:57
  11.5 77.0 %collective-permute-start.11 = (bf16[2,128,1024]{2,1,0:T(8,128)(2,1)}, bf16[2,128,1024]{2,1,0:T(8,128)(2,1)}, u32[]{:S(2)}, u32[]{:S(2)}) collective-permute-start(bf16[2,128,1024]{2,1,0:T(8,128)(2,1)} %bitcast_multiply_fusion.2), channel_id=1, source_target_pairs={{0,24},{2,26},{4,28},{6,30},{8,0},{10,2},{12,4},{14,6},{16,8},{18,... | collective-permute-start | bytes 1572872 | tf_op jit(solution)/shard_map/ppermute | solution.py:57
  15.5 36.7 %collective-permute-start.1 = (bf16[1,128,1024]{2,1,0:T(8,128)(2,1)}, bf16[1,128,1024]{2,1,0:T(8,128)(2,1)}, u32[]{:S(2)}, u32[]{:S(2)}) collective-permute-start(bf16[1,128,1024]{2,1,0:T(8,128)(2,1)} %bitcast_multiply_fusion.6), channel_id=1, source_target_pairs={{0,8},{2,10},{4,12},{6,14},{8,16},{10,18},{12,20},{14,22},{16,24},... | collective-permute-start | bytes 786440 | tf_op jit(solution)/shard_map/ppermute | solution.py:57
  16.2 57.6 %collective-permute-start.2 = (bf16[1,128,1024]{2,1,0:T(8,128)(2,1)}, bf16[1,128,1024]{2,1,0:T(8,128)(2,1)}, u32[]{:S(2)}, u32[]{:S(2)}) collective-permute-start(bf16[1,128,1024]{2,1,0:T(8,128)(2,1)} %bitcast_multiply_fusion.6), channel_id=1, source_target_pairs={{0,16},{2,18},{4,20},{6,22},{8,24},{10,26},{12,28},{14,30},{16,0},... | collective-permute-start | bytes 786440 | tf_op jit(solution)/shard_map/ppermute | solution.py:57
  16.5 7.0 %copy-start.34 = (s32[15]{0:T(128)S(1)}, s32[15]{0:T(128)}, u32[]{:S(2)}) copy-start(s32[15]{0:T(128)} %param.7) | copy-start | bytes 184
  20.1 5.8 %copy-start.2 = (bf16[3,128,1,1024]{3,2,1,0:T(2,128)(2,1)}, bf16[3,128,1,1024]{3,2,1,0:T(2,128)(2,1)S(1)}, u32[]{:S(2)}) copy-start(bf16[3,128,1,1024]{3,2,1,0:T(2,128)(2,1)S(1)} %slice.127) | copy-start | bytes 2359300
  52.2 27.1 %collective-permute-start.3 = (bf16[1,128,1024]{2,1,0:T(8,128)(2,1)}, bf16[1,128,1024]{2,1,0:T(8,128)(2,1)S(1)}, u32[]{:S(2)}, u32[]{:S(2)}) collective-permute-start(bf16[1,128,1024]{2,1,0:T(8,128)(2,1)} %bitcast_multiply_fusion.6), channel_id=1, source_target_pairs={{0,24},{2,26},{4,28},{6,30},{8,0},{10,2},{12,4},{14,6},{16,8},{18,... | collective-permute-start | bytes 786440 | tf_op jit(solution)/shard_map/ppermute | solution.py:57
  73.8 31.5 %collective-permute-start.17 = (bf16[3,128,1024]{2,1,0:T(8,128)(2,1)}, bf16[3,128,1024]{2,1,0:T(8,128)(2,1)}, u32[]{:S(2)}, u32[]{:S(2)}) collective-permute-start(bf16[3,128,1024]{2,1,0:T(8,128)(2,1)} %bitcast_multiply_fusion), channel_id=1, source_target_pairs={{0,8},{2,10},{4,12},{6,14},{8,16},{10,18},{12,20},{14,22},{16,24},... | collective-permute-start | bytes 2359304 | tf_op jit(solution)/shard_map/ppermute | solution.py:57
  79.4 19.0 %copy-start.3 = (bf16[1,4,128,1024]{3,2,1,0:T(8,128)(2,1)}, bf16[1,4,128,1024]{3,2,1,0:T(8,128)(2,1)S(1)}, u32[]{:S(2)}) copy-start(bf16[1,4,128,1024]{3,2,1,0:T(8,128)(2,1)S(1)} %bitcast_dynamic-update-slice_fusion.14) | copy-start | bytes 3145732
  79.4 14.9 %collective-permute-start.4 = (bf16[1,4,128,1024]{3,2,1,0:T(8,128)(2,1)S(1)}, bf16[1,4,128,1024]{3,2,1,0:T(8,128)(2,1)S(1)}, u32[]{:S(2)}, u32[]{:S(2)}) collective-permute-start(bf16[1,4,128,1024]{3,2,1,0:T(8,128)(2,1)S(1)} %bitcast_dynamic-update-slice_fusion.14), channel_id=1, source_target_pairs={{0,2},{1,5},{2,0},{3,7},{4,6},{5,1},{6,4},{7,3},{8,10},{9,13},{10,... | collective-permute-start | bytes 3145736 | tf_op jit(solution)/shard_map/ppermute | solution.py:65
  81.3 51.1 %collective-permute-start.18 = (bf16[3,128,1024]{2,1,0:T(8,128)(2,1)}, bf16[3,128,1024]{2,1,0:T(8,128)(2,1)}, u32[]{:S(2)}, u32[]{:S(2)}) collective-permute-start(bf16[3,128,1024]{2,1,0:T(8,128)(2,1)} %bitcast_multiply_fusion), channel_id=1, source_target_pairs={{0,16},{2,18},{4,20},{6,22},{8,24},{10,26},{12,28},{14,30},{16,0},... | collective-permute-start | bytes 2359304 | tf_op jit(solution)/shard_map/ppermute | solution.py:57
  86.6 13.9 %collective-permute-start = (bf16[128,1024]{1,0:T(8,128)(2,1)S(1)}, bf16[128,1024]{1,0:T(8,128)(2,1)}, u32[]{:S(2)}, u32[]{:S(2)}) collective-permute-start(bf16[128,1024]{1,0:T(8,128)(2,1)S(1)} %fusion.22), channel_id=1, source_target_pairs={{0,1},{1,0},{2,3},{3,2},{4,5},{5,4},{6,7},{7,6},{8,9},{9,8},{10,11... | collective-permute-start | bytes 786440 | tf_op jit(solution)/shard_map/ppermute | solution.py:33
  90.3 45.8 %collective-permute-start.12 = (bf16[2,4,128,1024]{3,2,1,0:T(8,128)(2,1)}, bf16[2,4,128,1024]{3,2,1,0:T(8,128)(2,1)}, u32[]{:S(2)}, u32[]{:S(2)}) collective-permute-start(bf16[2,4,128,1024]{3,2,1,0:T(8,128)(2,1)} %bitcast_dynamic-update-slice_fusion.10), channel_id=1, source_target_pairs={{0,2},{1,5},{2,0},{3,7},{4,6},{5,1},{6,4},{7,3},{8,10},{9,13},{10,... | collective-permute-start | bytes 6291464 | tf_op jit(solution)/shard_map/ppermute | solution.py:65
  94.3 1.0 copy-start.20
  96.7 45.7 %collective-permute-start.5 = (bf16[2,1,4,128,1024]{4,3,2,1,0:T(8,128)(2,1)}, bf16[2,1,4,128,1024]{4,3,2,1,0:T(8,128)(2,1)}, u32[]{:S(2)}, u32[]{:S(2)}) collective-permute-start(bf16[2,1,4,128,1024]{4,3,2,1,0:T(8,128)(2,1)} %pad_maximum_fusion.3), channel_id=1, source_target_pairs={{0,4},{1,3},{2,6},{3,1},{4,0},{5,7},{6,2},{7,5},{8,12},{9,11},{10,... | collective-permute-start | bytes 6291464 | tf_op jit(solution)/shard_map/ppermute | solution.py:65
  98.3 5.6 %copy-start.4 = (bf16[1,4,128,1024]{3,2,1,0:T(8,128)(2,1)S(1)}, bf16[1,4,128,1024]{3,2,1,0:T(8,128)(2,1)}, u32[]{:S(2)}) copy-start(bf16[1,4,128,1024]{3,2,1,0:T(8,128)(2,1)} %copy-done.3) | copy-start | bytes 3145732
  100.5 33.8 %collective-permute-start.19 = (bf16[3,128,1024]{2,1,0:T(8,128)(2,1)}, bf16[3,128,1024]{2,1,0:T(8,128)(2,1)S(1)}, u32[]{:S(2)}, u32[]{:S(2)}) collective-permute-start(bf16[3,128,1024]{2,1,0:T(8,128)(2,1)} %bitcast_multiply_fusion), channel_id=1, source_target_pairs={{0,24},{2,26},{4,28},{6,30},{8,0},{10,2},{12,4},{14,6},{16,8},{18,... | collective-permute-start | bytes 2359304 | tf_op jit(solution)/shard_map/ppermute | solution.py:57
  103.9 31.3 %copy-start.21 = (bf16[1,4,128,1024]{3,2,1,0:T(8,128)(2,1)S(1)}, bf16[1,4,128,1024]{3,2,1,0:T(8,128)(2,1)}, u32[]{:S(2)}) copy-start(bf16[1,4,128,1024]{3,2,1,0:T(8,128)(2,1)} %copy-done.20) | copy-start | bytes 3145732
  105.3 39.8 %copy-start.18 = (bf16[128,1024]{1,0:T(8,128)(2,1)}, bf16[128,1024]{1,0:T(8,128)(2,1)S(1)}, u32[]{:S(2)}) copy-start(bf16[128,1024]{1,0:T(8,128)(2,1)S(1)} %get-tuple-element.31) | copy-start | bytes 786436
  134.4 96.0 %collective-permute-start.20 = (bf16[3,4,128,1024]{3,2,1,0:T(8,128)(2,1)S(1)}, bf16[3,4,128,1024]{3,2,1,0:T(8,128)(2,1)}, u32[]{:S(2)}, u32[]{:S(2)}) collective-permute-start(bf16[3,4,128,1024]{3,2,1,0:T(8,128)(2,1)S(1)} %bitcast_dynamic-update-slice_fusion.6), channel_id=1, source_target_pairs={{0,2},{1,5},{2,0},{3,7},{4,6},{5,1},{6,4},{7,3},{8,10},{9,13},{10,... | collective-permute-start | bytes 9437192 | tf_op jit(solution)/shard_map/ppermute | solution.py:65
  140.7 100.6 %collective-permute-start.13 = (bf16[2,2,4,128,1024]{4,3,2,1,0:T(8,128)(2,1)}, bf16[2,2,4,128,1024]{4,3,2,1,0:T(8,128)(2,1)}, u32[]{:S(2)}, u32[]{:S(2)}) collective-permute-start(bf16[2,2,4,128,1024]{4,3,2,1,0:T(8,128)(2,1)} %pad_maximum_fusion.2), channel_id=1, source_target_pairs={{0,4},{1,3},{2,6},{3,1},{4,0},{5,7},{6,2},{7,5},{8,12},{9,11},{10,... | collective-permute-start | bytes 12582920 | tf_op jit(solution)/shard_map/ppermute | solution.py:65
  145.1 2.1 copy-start
  147.9 0.8 copy-start.5
  149.4 1.9 collective-permute-start.6
  152.5 0.7 copy-start.26
  152.5 0.8 copy-start.27
  154.2 65.8 %all-to-all-start = ((bf16[16,1,64,128]{3,2,1,0:T(8,128)(2,1)}), bf16[16,1,64,128]{3,2,1,0:T(8,128)(2,1)}, u32[]{:S(2)}, u32[]{:S(2)}) async-start(bf16[16,1,64,128]{3,2,1,0:T(8,128)(2,1)} %copy.42), calls=%async_computation | async-start | bytes 524288 | tf_op jit(solution)/shard_map/all_to_all | solution.py:90
  220.0 7.4 %copy-start.1 = (bf16[1,4,2,2,128,1024]{5,4,3,2,1,0:T(8,128)(2,1)S(1)}, bf16[1,4,2,2,128,1024]{5,4,3,2,1,0:T(8,128)(2,1)}, u32[]{:S(2)}) copy-start(bf16[1,4,2,2,128,1024]{5,4,3,2,1,0:T(8,128)(2,1)} %copy-done) | copy-start | bytes 12582916
  220.0 6.4 %collective-permute-start.7 = (bf16[16,1,64,128]{3,2,1,0:T(8,128)(2,1)}, bf16[16,1,64,128]{3,2,1,0:T(8,128)(2,1)S(1)}, u32[]{:S(2)}, u32[]{:S(2)}) collective-permute-start(bf16[16,1,64,128]{3,2,1,0:T(8,128)(2,1)} %all-to-all-done), channel_id=1, source_target_pairs={{0,1},{1,0},{2,3},{3,2},{4,5},{5,4},{6,7},{7,6},{8,9},{9,8},{10,11... | collective-permute-start | bytes 786440 | tf_op jit(solution)/shard_map/ppermute | solution.py:33
  227.4 3.1 copy-start.10
  230.3 8.3 %collective-permute-start.8 = (bf16[128,1024]{1,0:T(8,128)(2,1)}, bf16[128,1024]{1,0:T(8,128)(2,1)}, u32[]{:S(2)}, u32[]{:S(2)}) collective-permute-start(bf16[128,1024]{1,0:T(8,128)(2,1)} %get-tuple-element.36), channel_id=1, source_target_pairs={{0,1},{1,0},{2,3},{3,2},{4,5},{5,4},{6,7},{7,6},{8,9},{9,8},{10,11... | collective-permute-start | bytes 786440 | tf_op jit(solution)/shard_map/ppermute | solution.py:33
  235.6 136.3 %collective-permute-start.21 = (bf16[2,3,4,128,1024]{4,3,2,1,0:T(8,128)(2,1)}, bf16[2,3,4,128,1024]{4,3,2,1,0:T(8,128)(2,1)}, u32[]{:S(2)}, u32[]{:S(2)}) collective-permute-start(bf16[2,3,4,128,1024]{4,3,2,1,0:T(8,128)(2,1)} %pad_maximum_fusion.1), channel_id=1, source_target_pairs={{0,4},{1,3},{2,6},{3,1},{4,0},{5,7},{6,2},{7,5},{8,12},{9,11},{10,... | collective-permute-start | bytes 18874376 | tf_op jit(solution)/shard_map/ppermute | solution.py:65
  239.6 4.8 %copy-start.22 = (bf16[128,1024]{1,0:T(8,128)(2,1)}, bf16[128,1024]{1,0:T(8,128)(2,1)S(1)}, u32[]{:S(2)}) copy-start(bf16[128,1024]{1,0:T(8,128)(2,1)S(1)} %get-tuple-element.24) | copy-start | bytes 786436
  239.6 4.8 %copy-start.24 = (bf16[128,1024]{1,0:T(8,128)(2,1)}, bf16[128,1024]{1,0:T(8,128)(2,1)S(1)}, u32[]{:S(2)}) copy-start(bf16[128,1024]{1,0:T(8,128)(2,1)S(1)} %get-tuple-element.25) | copy-start | bytes 786436
  254.3 2.4 collective-permute-start.14
  256.8 0.8 copy-start.12
  256.8 0.9 copy-start.14
  258.9 53.7 %all-to-all-start.1 = ((bf16[16,2,64,128]{3,2,1,0:T(8,128)(2,1)}), bf16[16,2,64,128]{3,2,1,0:T(8,128)(2,1)}, u32[]{:S(2)}, u32[]{:S(2)}) async-start(bf16[16,2,64,128]{3,2,1,0:T(8,128)(2,1)} %copy.53), calls=%async_computation.1 | async-start | bytes 1048576 | tf_op jit(solution)/shard_map/all_to_all | solution.py:90
  284.2 33.3 %copy-start.13 = (bf16[2,128,1024]{2,1,0:T(8,128)(2,1)S(1)}, bf16[2,128,1024]{2,1,0:T(8,128)(2,1)}, u32[]{:S(2)}) copy-start(bf16[2,128,1024]{2,1,0:T(8,128)(2,1)} %copy-done.12) | copy-start | bytes 1572868
  284.2 33.3 %copy-start.15 = (bf16[2,128,1024]{2,1,0:T(8,128)(2,1)S(1)}, bf16[2,128,1024]{2,1,0:T(8,128)(2,1)}, u32[]{:S(2)}) copy-start(bf16[2,128,1024]{2,1,0:T(8,128)(2,1)} %copy-done.14) | copy-start | bytes 1572868
  313.6 5.0 %collective-permute-start.15 = (bf16[16,2,64,128]{3,2,0,1:T(8,128)(2,1)S(1)}, bf16[16,2,64,128]{3,2,0,1:T(8,128)(2,1)S(1)}, u32[]{:S(2)}, u32[]{:S(2)}) collective-permute-start(bf16[16,2,64,128]{3,2,0,1:T(8,128)(2,1)S(1)} %copy.55), channel_id=1, source_target_pairs={{0,1},{1,0},{2,3},{3,2},{4,5},{5,4},{6,7},{7,6},{8,9},{9,8},{10,11... | collective-permute-start | bytes 1572872 | tf_op jit(solution)/shard_map/ppermute | solution.py:33
  325.3 6.7 %copy-start.16 = (bf16[128,2048]{1,0:T(8,128)(2,1)S(1)}, bf16[128,2048]{1,0:T(8,128)(2,1)}, u32[]{:S(2)}) copy-start(bf16[128,2048]{1,0:T(8,128)(2,1)} %fusion.13) | copy-start | bytes 1572868
  325.3 6.7 %copy-start.17 = (bf16[128,2048]{1,0:T(8,128)(2,1)S(1)}, bf16[128,2048]{1,0:T(8,128)(2,1)}, u32[]{:S(2)}) copy-start(bf16[128,2048]{1,0:T(8,128)(2,1)} %copy.78) | copy-start | bytes 1572868
  325.3 6.7 %copy-start.19 = (bf16[128,1024]{1,0:T(8,128)(2,1)S(1)}, bf16[128,1024]{1,0:T(8,128)(2,1)}, u32[]{:S(2)}) copy-start(bf16[128,1024]{1,0:T(8,128)(2,1)} %copy-done.18) | copy-start | bytes 786436
  325.3 6.7 %copy-start.23 = (bf16[128,1024]{1,0:T(8,128)(2,1)S(1)}, bf16[128,1024]{1,0:T(8,128)(2,1)}, u32[]{:S(2)}) copy-start(bf16[128,1024]{1,0:T(8,128)(2,1)} %copy-done.22) | copy-start | bytes 786436
  325.3 6.8 %copy-start.25 = (bf16[128,1024]{1,0:T(8,128)(2,1)S(1)}, bf16[128,1024]{1,0:T(8,128)(2,1)}, u32[]{:S(2)}) copy-start(bf16[128,1024]{1,0:T(8,128)(2,1)} %copy-done.24) | copy-start | bytes 786436
  325.3 5.7 %collective-permute-start.16 = (bf16[128,1024]{1,0:T(8,128)(2,1)S(1)}, bf16[128,1024]{1,0:T(8,128)(2,1)}, u32[]{:S(2)}, u32[]{:S(2)}) collective-permute-start(bf16[128,1024]{1,0:T(8,128)(2,1)S(1)} %get-tuple-element.40), channel_id=1, source_target_pairs={{0,1},{1,0},{2,3},{3,2},{4,5},{5,4},{6,7},{7,6},{8,9},{9,8},{10,11... | collective-permute-start | bytes 786440 | tf_op jit(solution)/shard_map/ppermute | solution.py:33
  389.3 2.3 collective-permute-start.22
  391.7 19.9 %copy-start.11 = (bf16[16,1,128,128]{3,2,1,0:T(8,128)(2,1)S(1)}, bf16[16,1,128,128]{3,2,1,0:T(8,128)(2,1)}, u32[]{:S(2)}) copy-start(bf16[16,1,128,128]{3,2,1,0:T(8,128)(2,1)} %copy-done.10) | copy-start | bytes 1572868
  393.1 36.6 %all-to-all-start.2 = ((bf16[16,3,64,128]{3,2,1,0:T(8,128)(2,1)}), bf16[16,3,64,128]{3,2,1,0:T(8,128)(2,1)S(1)}, u32[]{:S(2)}, u32[]{:S(2)}) async-start(bf16[16,3,64,128]{3,2,1,0:T(8,128)(2,1)} %copy.68), calls=%async_computation.2 | async-start | bytes 1572864 | tf_op jit(solution)/shard_map/all_to_all | solution.py:90
  414.2 18.5 %copy-start.29 = (f32[128,1024]{1,0:T(8,128)S(1)}, f32[128,1024]{1,0:T(8,128)}, u32[]{:S(2)}) copy-start(f32[128,1024]{1,0:T(8,128)} %get-tuple-element.41) | copy-start | bytes 1572868
  430.7 6.5 %collective-permute-start.23 = (bf16[16,3,64,128]{3,2,0,1:T(8,128)(2,1)}, bf16[16,3,64,128]{3,2,0,1:T(8,128)(2,1)}, u32[]{:S(2)}, u32[]{:S(2)}) collective-permute-start(bf16[16,3,64,128]{3,2,0,1:T(8,128)(2,1)} %copy.70), channel_id=1, source_target_pairs={{0,1},{1,0},{2,3},{3,2},{4,5},{5,4},{6,7},{7,6},{8,9},{9,8},{10,11... | collective-permute-start | bytes 2359304 | tf_op jit(solution)/shard_map/ppermute | solution.py:33
  431.0 3.2 copy-start.6
  431.0 3.2 copy-start.30
  431.0 3.2 copy-start.32
  432.7 3.0 copy-start.28
  432.7 3.0 copy-start.31
  439.1 6.9 %copy-start.9 = (f32[1,128,4,1024]{3,1,2,0:T(8,128)S(1)}, f32[1,128,4,1024]{3,1,2,0:T(8,128)}, u32[]{:S(2)}) copy-start(f32[1,128,4,1024]{3,1,2,0:T(8,128)} %maximum_bitcast_fusion.1) | copy-start | bytes 6291460
  445.7 1.6 copy-start.7
  445.7 2.2 copy-start.8

commit v2 on v1

v2 whole, which is shorter than its diff:
```python
import functools

import jax
import jax.numpy as jnp
from jax import lax
from jax.experimental import pallas as pl
from jax.experimental.pallas import tpu as pltpu
from jax.sharding import PartitionSpec as P

LEV = 4
TILE = 256
LT = 8
M = 15
BF = jnp.bfloat16
F32 = jnp.float32
VMEM = 56 * 1024 * 1024


def ancestors(parent):
    node_ids = jnp.arange(M, dtype=jnp.int32)
    step_mat = (parent[:, None] == node_ids[None, :]).astype(jnp.float32)
    power_mat = step_mat
    reach = step_mat
    for hop_count in range(LEV - 2):
        power_mat = jnp.dot(power_mat, step_mat, precision=lax.Precision.HIGHEST)
        reach = reach + power_mat
    return reach


def spread(mask_tile):
    return jnp.repeat(mask_tile, TILE, axis=-1)


def after(value, *others):
    return lax.optimization_barrier((value,) + others)[0]


def narrow_all(x, axis):
    size = lax.axis_size("narrow")
    mine = lax.axis_index("narrow")
    if size == 2:
        other = lax.ppermute(x, "narrow", [(0, 1), (1, 0)])
        first = mine == 0
        return jnp.concatenate([jnp.where(first, x, other), jnp.where(first, other, x)], axis=axis)
    shape = list(x.shape)
    width = shape[axis]
    shape[axis] = width * size
    out = jnp.zeros(shape, x.dtype)
    for hop in range(size):
        got = x if hop == 0 else lax.ppermute(x, "narrow", [(i, (i + hop) % size) for i in range(size)])
        out = lax.dynamic_update_slice_in_dim(out, got, (mine - hop) % size * width, axis)
    return out


def swap(value, turn):
    wide = lax.axis_size("wide")
    narrow = lax.axis_size("narrow")
    pairs = []
    for i in range(wide):
        for j in range(narrow):
            pairs.append((i * narrow + j, (i ^ (1 if (j + turn) % 2 == 0 else 2)) * narrow + j))
    return lax.ppermute(value, ("wide", "narrow"), pairs)


def shifts(value):
    wide = lax.axis_size("wide")
    return [value] + [
        lax.ppermute(value, "wide", [(i, (i + 4 * hop) % wide) for i in range(wide)])
        for hop in range(1, wide // 4)
    ]


def positions(z_last):
    wide = lax.axis_size("wide")
    depth = wide // 4
    row_id = lax.axis_index("wide")
    odd = lax.axis_index("narrow") % 2
    z = (row_id // 4 - jnp.arange(depth, dtype=jnp.int32)) % depth
    flips = jnp.stack([0 * odd, 1 + odd, 2 - odd, 3 + 0 * odd])
    near = (row_id % 4) ^ flips
    if z_last:
        return (z[:, None] * 4 + near[None, :]).reshape(-1).astype(jnp.int32)
    return (z[None, :] * 4 + near[:, None]).reshape(-1).astype(jnp.int32)


def along_z(x, gate):
    return shifts(x if gate is None else after(x, gate))


def along_xy(pieces, gate):
    if gate is not None:
        held = lax.optimization_barrier(tuple(pieces) + (gate,))
        pieces = held[:-1]
    line = jnp.stack(pieces)
    return [line, swap(line, 0), swap(line, 1)]


def along_both(arrays, gate):
    near = arrays[1]
    return arrays + [swap(near if gate is None else after(near, gate), 1)]


def product_body(plan, rows_n, steps_n, finish, *refs):
    place_ref, mask_ref = refs[0], refs[1]
    refs = refs[2:]
    row_refs = [refs[q * steps_n : (q + 1) * steps_n] for q in range(rows_n)]
    refs = refs[rows_n * steps_n :]
    count = sum(arrays for _, arrays, _ in plan)
    piece_refs, refs = refs[:count], refs[count:]
    if finish:
        diag_ref, out_ref, low_ref, lhs = refs
    else:
        out_ref, lhs = refs
    r = row_refs[0][0].shape[0]
    width = piece_refs[0].shape[-1]

    @pl.when(pl.program_id(0) == 0)
    def _():
        at = 0
        for g, (levels, arrays, each) in enumerate(plan):
            for i in range(arrays * each):
                start = pl.multiple_of(place_ref[g, i] * r, r)
                for j in levels:
                    for q in range(rows_n):
                        lhs[q * r : (q + 1) * r, at : at + r] = row_refs[q][j][:, pl.ds(start, r)]
                    at += r

    total = None
    at, base = 0, 0
    for levels, arrays, each in plan:
        depth = each * len(levels) * r
        for a in range(arrays):
            part = jnp.dot(
                lhs[:, at : at + depth],
                piece_refs[base + a][...].reshape(depth, width),
                preferred_element_type=F32,
            )
            total = part if total is None else total + part
            at += depth
        base += arrays
    here = pl.program_id(0)
    for q in range(rows_n):
        for t in range(width // TILE):
            keep = mask_ref[q, here * (width // TILE) + t] > 0
            cols = slice(t * TILE, (t + 1) * TILE)
            value = total[q * r : (q + 1) * r, cols]
            if finish:
                value = diag_ref[0, :, cols] - value
            else:
                value = -value
            value = jnp.where(keep, value, 0.0)
            if finish:
                out_ref[:, cols] = value
                low_ref[:, cols] = value.astype(BF)
            else:
                out_ref[q, :, cols] = value.astype(BF)


def product(rows, groups, mask, diag=None, shift=0):
    r = rows[0][0].shape[0]
    c = groups[0][2][0].shape[-1]
    rows_n, steps_n = len(rows), len(rows[0])
    if r % 128:
        total = 0.0
        for levels, place, arrays in groups:
            at = 0
            for array in arrays:
                each = array.shape[0]
                here = place[at : at + each]
                lhs = jnp.concatenate(
                    [
                        jnp.stack(
                            [jnp.take(row[j].reshape(r, -1, r), here, axis=1) for j in levels], axis=2
                        ).reshape(r, -1)
                        for row in rows
                    ],
                    axis=0,
                )
                total += jnp.dot(lhs, array.reshape(-1, c), preferred_element_type=F32)
                at += each
        total = total.reshape(rows_n, r, c)
        keep = jnp.repeat(mask, TILE, axis=1)[:, None, :] > 0
        if diag is None:
            return jnp.where(keep, -total, 0.0).astype(BF)
        level = diag[1]
        value = jnp.where(keep[0], diag[0][level, :, shift : shift + c] - total[0], 0.0)
        return value, value.astype(BF)
    width = TILE
    plan = tuple((tuple(levels), len(arrays), arrays[0].shape[0]) for levels, _, arrays in groups)
    place = jnp.stack([p for _, p, _ in groups])
    whole = pl.BlockSpec(memory_space=pltpu.VMEM)
    scalar = pl.BlockSpec(memory_space=pltpu.SMEM)
    pieces = [a for _, _, arrays in groups for a in arrays]
    piece_specs = [pl.BlockSpec(a.shape[:3] + (width,), lambda i: (0, 0, 0, i)) for a in pieces]
    flat = [x for row in rows for x in row]
    operands = [place, mask] + flat + pieces
    specs = [scalar, scalar] + [whole] * len(flat) + piece_specs
    if diag is None:
        outs = jax.ShapeDtypeStruct((rows_n, r, c), BF)
        out_specs = pl.BlockSpec((rows_n, r, width), lambda i: (0, 0, i))
    else:
        level = diag[1]
        skip = shift // width
        operands.append(diag[0])
        specs.append(pl.BlockSpec((1, r, width), lambda i: (level, 0, skip + i)))
        outs = (jax.ShapeDtypeStruct((r, c), F32), jax.ShapeDtypeStruct((r, c), BF))
        out_specs = (pl.BlockSpec((r, width), lambda i: (0, i)),) * 2
    deep = sum(len(levels) * arrays * each for levels, arrays, each in plan) * r
    return pl.pallas_call(
        functools.partial(product_body, plan, rows_n, steps_n, diag is not None),
        grid=(c // width,),
        in_specs=specs,
        out_specs=out_specs,
        out_shape=outs,
        scratch_shapes=[pltpu.VMEM((rows_n * r, deep), BF)],
        compiler_params=pltpu.CompilerParams(vmem_limit_bytes=VMEM),
        cost_estimate=pl.CostEstimate(
            flops=1, bytes_accessed=1, transcendentals=0
        ),
    )(*operands)


def slots_body(levels, wide, id_ref, own_ref, other_ref, slots_ref, full_ref):
    r, c = own_ref.shape[1:]
    part = r // 2
    half = wide // 2
    for n in range(2):

        @pl.when(id_ref[0] == n)
        def _():
            for h in range(2):
                ref = own_ref if h == n else other_ref
                for k in range(levels):
                    full_ref[k, :, h * c : (h + 1) * c] = ref[k]
                    for i in range(half):
                        slots_ref[h * half + i, k] = ref[k, n * part : (n + 1) * part, i * r : (i + 1) * r]


def make_slots(value):
    wide = lax.axis_size("wide")
    narrow = lax.axis_size("narrow")
    l, r, c = value.shape
    if narrow != 2 or r % 128:
        full = narrow_all(value, 2)
        part = r // narrow
        mine = lax.dynamic_slice_in_dim(full, lax.axis_index("narrow") * part, part, 1)
        return mine.reshape(l, part, wide, r).transpose(2, 0, 1, 3), full
    other = lax.ppermute(value, "narrow", [(0, 1), (1, 0)])
    whole = pl.BlockSpec(memory_space=pltpu.VMEM)
    return pl.pallas_call(
        functools.partial(slots_body, l, wide),
        in_specs=[pl.BlockSpec(memory_space=pltpu.SMEM), whole, whole],
        out_specs=(whole, whole),
        out_shape=(
            jax.ShapeDtypeStruct((wide, l, r // 2, r), BF),
            jax.ShapeDtypeStruct((l, r, 2 * c), BF),
        ),
        compiler_params=pltpu.CompilerParams(vmem_limit_bytes=VMEM),
        cost_estimate=pl.CostEstimate(flops=1, bytes_accessed=1, transcendentals=0),
    )(lax.axis_index("narrow").astype(jnp.int32).reshape(1), value, other)


def turn_body(levels, wide, id_ref, own_ref, other_ref, out_ref):
    r = out_ref.shape[1]
    for n in range(2):

        @pl.when(id_ref[0] == n)
        def _():
            first, second = (own_ref, other_ref) if n == 0 else (other_ref, own_ref)
            for k in range(levels):
                for w in range(wide):
                    block = jnp.concatenate([first[w, k], second[w, k]], axis=0)
                    out_ref[k, :, w * r : (w + 1) * r] = block.T


def mirrored(got, full):
    wide = lax.axis_size("wide")
    narrow = lax.axis_size("narrow")
    l, r, cols = full.shape
    if narrow != 2 or r % 128:
        return narrow_all(got, 2).transpose(1, 3, 0, 2).reshape(l, r, cols)
    other = lax.ppermute(got, "narrow", [(0, 1), (1, 0)])
    whole = pl.BlockSpec(memory_space=pltpu.VMEM)
    return pl.pallas_call(
        functools.partial(turn_body, l, wide),
        in_specs=[pl.BlockSpec(memory_space=pltpu.SMEM), whole, whole],
        out_specs=whole,
        out_shape=jax.ShapeDtypeStruct((l, r, cols), BF),
        compiler_params=pltpu.CompilerParams(vmem_limit_bytes=VMEM),
        cost_estimate=pl.CostEstimate(flops=1, bytes_accessed=1, transcendentals=0),
    )(lax.axis_index("narrow").astype(jnp.int32).reshape(1), got, other)


def upper_body(id_ref, first_ref, *refs):
    news, turns, diags, out_ref = refs[0:3], refs[3:5], refs[5:7], refs[7]
    for k in range(LEV - 1):
        for m in range(LEV):
            if m == k:
                value = first_ref[0] if k == 0 else diags[k - 1][...]
            elif m > k:
                value = news[m - 1][k].astype(F32)
            else:
                value = turns[k - 1][m].astype(F32)
            out_ref[k, :, m, :] = value


def lower_body(id_ref, turn_ref, diag_ref, held_ref, out_ref):
    for m in range(LEV - 1):
        out_ref[0, :, m, :] = turn_ref[m].astype(F32)
    out_ref[0, :, LEV - 1, :] = diag_ref[...]


def upper_rows(diag_inverse, news, turns, diags):
    r, c = diag_inverse.shape[1:]
    step = min(r, 32)
    shape = jax.ShapeDtypeStruct((LEV, r, LEV, c), F32)
    specs = [pl.BlockSpec((1, step, c), lambda i, n: (0, i, 0))]
    specs += [pl.BlockSpec((m, step, c), lambda i, n: (0, i, 0)) for m in range(1, LEV)]
    specs += [pl.BlockSpec((k, step, c), lambda i, n: (0, i, n[0])) for k in range(1, LEV - 1)]
    specs += [pl.BlockSpec((step, c), lambda i, n: (i, 0)) for k in range(1, LEV - 1)]
    return pl.pallas_call(
        upper_body,
        grid_spec=pltpu.PrefetchScalarGridSpec(
            num_scalar_prefetch=1,
            grid=(r // step,),
            in_specs=specs,
            out_specs=pl.BlockSpec((LEV - 1, step, LEV, c), lambda i, n: (0, i, 0, 0)),
        ),
        out_shape=shape,
        compiler_params=pltpu.CompilerParams(vmem_limit_bytes=VMEM),
        cost_estimate=pl.CostEstimate(flops=0, bytes_accessed=1, transcendentals=0),
    )(lax.axis_index("narrow").astype(jnp.int32).reshape(1), diag_inverse, *news, *turns, *diags)


def lower_rows(turn, diag, held):
    r, c = diag.shape
    step = min(r, 32)
    return pl.pallas_call(
        lower_body,
        grid_spec=pltpu.PrefetchScalarGridSpec(
            num_scalar_prefetch=1,
            grid=(r // step,),
            in_specs=[
                pl.BlockSpec((LEV - 1, step, c), lambda i, n: (0, i, n[0])),
                pl.BlockSpec((step, c), lambda i, n: (i, 0)),
                pl.BlockSpec(memory_space=pl.ANY),
            ],
            out_specs=pl.BlockSpec((1, step, LEV, c), lambda i, n: (LEV - 1, i, 0, 0)),
        ),
        out_shape=jax.ShapeDtypeStruct(held.shape, F32),
        input_output_aliases={3: 0},
        compiler_params=pltpu.CompilerParams(vmem_limit_bytes=VMEM),
        cost_estimate=pl.CostEstimate(flops=0, bytes_accessed=1, transcendentals=0),
    )(lax.axis_index("narrow").astype(jnp.int32).reshape(1), turn, diag, held)


def local(factor, diag_inverse, parent, tile_node, structure):
    row_count = factor.shape[1]
    col_count = factor.shape[3]
    col_tiles = col_count // TILE
    row_id = lax.axis_index("wide")
    col_id = lax.axis_index("narrow")
    high = lax.Precision.HIGHEST
    reach = ancestors(parent)
    node_hot = (tile_node[:, :, None] == jnp.arange(M, dtype=jnp.int32)[None, None, :]).astype(
        jnp.float32
    )
    row_pos = row_id * row_count // TILE
    pos_hot = (jnp.arange(LT, dtype=jnp.int32) == row_pos).astype(jnp.float32)
    row_hot = jnp.einsum("t,ltm->lm", pos_hot, node_hot, precision=high)
    col_sel = (
        jnp.arange(LT, dtype=jnp.int32)[None, :]
        == (col_id * col_tiles + jnp.arange(col_tiles, dtype=jnp.int32))[:, None]
    ).astype(jnp.float32)
    col_hot = jnp.einsum("jt,ltm->ljm", col_sel, node_hot, precision=high)
    tile_above = jnp.einsum("ra,ba,cjb->rcj", row_hot, reach, col_hot, precision=high)
    tile_same = jnp.einsum("lm,ljm->lj", row_hot, col_hot, precision=high)
    struct_row = jnp.einsum("mlt,t->ml", structure.astype(jnp.float32), pos_hot, precision=high)
    tile_struct = jnp.einsum("cjm,mr->rcj", col_hot, struct_row, precision=high)
    above = (tile_above > 0.5).astype(jnp.int32)
    same = (tile_same > 0.5).astype(jnp.int32)

    def masked(k, m):
        return (factor[k, :, m, :] * spread(tile_struct[k, m])[None, :].astype(BF))[None]

    place = positions(False)

    def panel_of(level):
        return jnp.concatenate([masked(k, level) for k in range(level)], axis=0)

    wide = lax.axis_size("wide")
    whole_place = jnp.arange(wide, dtype=jnp.int32)
    last = lax.all_gather(panel_of(3), "wide", axis=0)
    first = along_z(panel_of(1), None)
    gathered_two = lax.all_gather(panel_of(2), "wide", axis=0)
    gathered = {1: along_both(along_xy(first, None), None)}
    gathered[3] = [last]
    gathered[2] = [gathered_two]

    rows = {0: [narrow_all(diag_inverse[0].astype(BF), 1)]}
    news, turns, diags = [], [], []
    for level in range(1, LEV):
        arrays = gathered[level]
        known = [rows[k] for k in range(level)]
        groups = [(tuple(range(level)), place if level == 1 else whole_place, arrays)]
        value = product(known, groups, above[:level, level])
        news.append(value)
        if level == 1:
            pass
        slots, full = make_slots(value)
        for k in range(level):
            rows[k].append(full[k])
        if level == LEV - 1:
            out = upper_rows(diag_inverse, news, turns, diags)
        got = lax.all_to_all(slots, "wide", split_axis=0, concat_axis=0, tiled=True)
        turn = mirrored(got, full)
        turns.append(turn)
        rows[level] = [turn[k] for k in range(level)]
        done, low = product([rows[level]], groups, same[level : level + 1], (diag_inverse, level))
        diags.append(done)
        if level < LEV - 1:
            rows[level].append(narrow_all(low, 1))
    return lower_rows(turns[-1], diags[-1], out)


def solution(mesh):
    return jax.shard_map(
        local,
        mesh=mesh,
        in_specs=(P(None, "wide", None, "narrow"), P(None, "wide", "narrow"), P(), P(), P()),
        out_specs=P(None, "wide", None, "narrow"),
        check_vma=False,
    )
```

time: 474 us -> 405 us (0.85); the launches traced: 464 us -> 403 us
  local copies, waits for them, and re-layouts: 98 us -> 23.6 us
  other arithmetic: 82.3 us -> 8.49 us
  Pallas kernels: 0 us -> 69.3 us
  starting transfers between devices: 78.8 us -> 17.8 us
  blocking collectives: 0 us -> 52.8 us
  waiting for transfers between devices: 168 us -> 215 us
  matrix products: 35.3 us -> 3.24 us
  between operations: 1.23 us -> 13.6 us
    all_gather x0 -> x2, waiting for transfers between devices: none -> 115 us  [the longest x1 105 us: local(): last = lax.all_gather(panel_of(3), 'wide', axis=0)]
    all_to_all x3 -> x1, waiting for transfers between devices: 85.4 us -> 14.5 us  [local(): got = lax.all_to_all(slots, 'wide', split_axis=0, concat_axis=0, tiled=True)]
    pallas_call x0 -> x14, Pallas kernels: none -> 69.3 us  [the longest x6 44 us: product(): pl.pallas_call(functools.partial(product_body, plan, rows_n, steps_n, dia...]
    all_to_all x0 -> x2, blocking collectives: none -> 52.8 us  [local(): got = lax.all_to_all(slots, 'wide', split_axis=0, concat_axis=0, tiled=True)]
    all_to_all x3 -> x1, starting transfers between devices: 50 us -> 6.61 us  [local(): got = lax.all_to_all(slots, 'wide', split_axis=0, concat_axis=0, tiled=True)]
    concatenate x2, other arithmetic: 41.5 us -> 1.87 us  [panel_of(): return jnp.concatenate([masked(k, level) for k in range(level)], axis=0)]
    dynamic_update_slice x21 -> x0, local copies, waits for them, and re-layouts: 39 us -> none  [the longest x12 28.9 us: wide_all(): lax.dynamic_update_slice(out, piece[:, :, None, None], (0, 0, yy, xx, 0, 0))]
    ppermute x6 -> x3, waiting for transfers between devices: 4.2 us -> 42.4 us  [swap(): return lax.ppermute(value, ('wide', 'narrow'), pairs)]
  transfers between devices with their start and end apart: 27 -> 18, of which waited for: 12 -> 14; matrix products, arithmetic and copies ran while one was open for 34% -> 4% of each run, Pallas kernels for 0% -> 10%
where the time goes in v2:
time: 405 us; the launch traced here: 403 us
  waiting for transfers between devices  215 us (53%)
  Pallas kernels  69.3 us (17%)
  blocking collectives  52.8 us (13%)
  local copies, waits for them, and re-layouts  23.6 us (6%)
  starting transfers between devices  17.8 us (4%)
  between operations  13.6 us (3%)
  other arithmetic  8.49 us (2%)
    all_gather x1, waiting for transfers between devices, local(): last = lax.all_gather(panel_of(3), 'wide', axis=0)  105 us
    all_to_all x2, blocking collectives, local(): got = lax.all_to_all(slots, 'wide', split_axis=0, concat_axis=0, tiled=True)  52.8 us
    pallas_call x6, Pallas kernels, product(): pl.pallas_call(functools.partial(product_body, plan, rows_n, steps_n, dia...  44 us
    ppermute x3, waiting for transfers between devices, swap(): return lax.ppermute(value, ('wide', 'narrow'), pairs)  42.4 us
    ppermute x3, waiting for transfers between devices, shifts(): lax.ppermute(value, 'wide', [(i, (i + 4 * hop) % wide) for i in range(wid...  32.4 us
    all_to_all x1, waiting for transfers between devices, local(): got = lax.all_to_all(slots, 'wide', split_axis=0, concat_axis=0, tiled=True)  14.5 us
    all_gather x1, waiting for transfers between devices, local(): gathered_two = lax.all_gather(panel_of(2), 'wide', axis=0)  10.4 us
  transfers between devices with their start and end apart: 18, of which 14 were waited for; matrix products, arithmetic and copies ran while one was open for 4% of the time, Pallas kernels for 10%

profile of v2, /device:TPU:0, one launch (start us, length us, event | category | flops | bytes accessed | tf_op | source)
XLA Modules:
  0.0 403.4 jit_solution(16123860537313835402)
XLA Ops:
  6.5 0.9 fusion.9
  7.4 0.8 fusion.7
  8.6 6.0 %fusion.27 = (bf16[1,128,1,1024]{3,2,1,0:T(2,128)(2,1)S(1)}, bf16[1,128,1,1024]{3,2,1,0:T(2,128)(2,1)S(1)}, bf16[1,128,1,1024]{3,2,1,0:T(2,128)(2,1)S(1)}, bf16[...) fusion(bf16[4,128,4,1024]{3,2,1,0:T(4,128)(2,1)} %param.5), kind=kLoop, calls=%fused_computation.83 | loop fusion | bytes 3145728 | tf_op jit(solution)/shard_map/slice | solution.py:384
  14.9 0.8 pad_maximum_fusion.4
  16.3 1.0 pad_maximum_fusion.1
  17.4 5.1 %collective-permute-start.3 = (bf16[1,128,1024]{2,1,0:T(8,128)(2,1)S(1)}, bf16[1,128,1024]{2,1,0:T(8,128)(2,1)S(1)}, u32[]{:S(2)}, u32[]{:S(2)}) collective-permute-start(bf16[1,128,1024]{2,1,0:T(8,128)(2,1)S(1)} %bitcast_multiply_fusion), channel_id=1, source_target_pairs={{0,24},{2,26},{4,28},{6,30},{8,0},{10,2},{12,4},{14,6},{16,8},{18,... | collective-permute-start | bytes 786440 | tf_op jit(solution)/shard_map/ppermute | solution.py:68
  22.5 1.0 collective-permute-start.1
  23.6 6.6 %collective-permute-done.3 = bf16[1,128,1024]{2,1,0:T(8,128)(2,1)S(1)} collective-permute-done((bf16[1,128,1024]{2,1,0:T(8,128)(2,1)S(1)}, bf16[1,128,1024]{2,1,0:T(8,128)(2,1)S(1)}, u32[]{:S(2)}, u32[]{:S(2)}) %collective-permute-start.3) | collective-permute-done | bytes 262176 | tf_op jit(solution)/shard_map/ppermute | solution.py:68
  30.3 25.7 %collective-permute-done.2 = bf16[1,128,1024]{2,1,0:T(8,128)(2,1)S(1)} collective-permute-done((bf16[1,128,1024]{2,1,0:T(8,128)(2,1)S(1)}, bf16[1,128,1024]{2,1,0:T(8,128)(2,1)S(1)}, u32[]{:S(2)}, u32[]{:S(2)}) %collective-permute-start.2) | collective-permute-done | bytes 262176 | tf_op jit(solution)/shard_map/ppermute | solution.py:68
  56.2 1.6 collective-permute-start.4
  57.7 1.1 fusion.1
  60.0 1.5 collective-permute-start.5
  61.5 32.4 %collective-permute-done.4.refs_4_ = bf16[4,1,128,1024]{3,2,1,0:T(8,128)(2,1)S(1)} collective-permute-done((bf16[4,1,128,1024]{3,2,1,0:T(8,128)(2,1)S(1)}, bf16[4,1,128,1024]{3,2,1,0:T(8,128)(2,1)S(1)}, u32[]{:S(2)}, u32[]{:S(2)}) %collective-permute-start.4) | collective-permute-done | bytes 1048608 | tf_op jit(solution)/shard_map/ppermute | solution.py:62
  93.9 1.5 collective-permute-start.6
  95.6 0.6 add.68.refs_0_
  96.2 0.6 slice_bitcast_fusion.15.refs_1_
  96.7 1.2 broadcast_select_fusion.5
  97.9 0.8 pad_maximum_fusion.2.refs_2_
  98.8 10.0 %collective-permute-done.6.refs_6_ = bf16[4,1,128,1024]{3,2,1,0:T(8,128)(2,1)} collective-permute-done((bf16[4,1,128,1024]{3,2,1,0:T(8,128)(2,1)S(1)}, bf16[4,1,128,1024]{3,2,1,0:T(8,128)(2,1)}, u32[]{:S(2)}, u32[]{:S(2)}) %collective-permute-start.6) | collective-permute-done | bytes 1048608 | tf_op jit(solution)/shard_map/ppermute | solution.py:62
  108.8 5.4 %shard_map.55.own_ref.refs_0_ = bf16[1,128,1024]{2,1,0:T(8,128)(2,1)} custom-call(s32[1,16]{1,0:T(1,128)} %add.68.refs_0_, s32[1,4]{1,0:T(1,128)} %slice_bitcast_fusion.15.refs_1_, bf16[128,2048]{1,0:T(8,128)(2,1)} %pad_maximum_fusion.2.refs_2_, bf16[4,1,128,1024]{3,2,1,0:T(8,128)(2,1)} %copy-done, bf16[4,1,128,1024]{3,2,1,0:T(8,128)(2,1)} %copy-done.1, ...), custom_call_target="tpu_custom_call" | custom-call | flops 1 | bytes 1 | tf_op jit(solution)/shard_map/pallas_call | solution.py:209
  114.2 1.7 collective-permute-done.7.other_ref
  115.9 0.7 copy-done.11
  116.6 2.0 shard_map.56
  118.7 6.6 %all-to-all-start = ((bf16[16,1,64,128]{3,2,1,0:T(8,128)(2,1)}), bf16[16,1,64,128]{3,2,1,0:T(8,128)(2,1)S(1)}, u32[]{:S(2)}, u32[]{:S(2)}) async-start(bf16[16,1,64,128]{3,2,1,0:T(8,128)(2,1)} %get-tuple-element.16), calls=%async_computation | async-start | bytes 524288 | tf_op jit(solution)/shard_map/all_to_all | solution.py:415
  125.4 14.5 %all-to-all-done.own_ref = bf16[16,1,64,128]{3,2,1,0:T(8,128)(2,1)S(1)} async-done(((bf16[16,1,64,128]{3,2,1,0:T(8,128)(2,1)}), bf16[16,1,64,128]{3,2,1,0:T(8,128)(2,1)S(1)}, u32[]{:S(2)}, u32[]{:S(2)}) %all-to-all-start) | async-done | bytes 262176 | tf_op jit(solution)/shard_map/all_to_all | solution.py:415
  140.0 0.6 fusion.28
  140.6 0.9 collective-permute-done.8.other_ref
  141.5 0.7 copy-done.12
  142.2 2.1 shard_map.57.refs_3_
  144.3 5.2 %shard_map.58 = (f32[128,1024]{1,0:T(8,128)}, bf16[128,1024]{1,0:T(8,128)(2,1)}) custom-call(s32[1,16]{1,0:T(1,128)} %add.68.refs_0_, s32[1,4]{1,0:T(1,128)} %get-tuple-element.52.refs_1_, bf16[128,2048]{1,0:T(8,128)(2,1)} %bitcast.126, bf16[4,1,128,1024]{3,2,1,0:T(8,128)(2,1)} %copy-done, bf16[4,1,128,1024]{3,2,1,0:T(8,128)(2,1)} %copy-done.1, ...), custom_call_target="tpu_custom_call" | custom-call | flops 1 | bytes 1 | tf_op jit(solution)/shard_map/pallas_call | solution.py:209
  150.2 1.0 collective-permute-done.9
  151.3 1.0 broadcast_select_fusion.3
  152.3 0.8 pad_maximum_fusion.3.refs_5_.refs_6_
  153.1 10.4 %all-gather.5.cloned.1.call-done = bf16[32,128,1024]{2,1,0:T(8,128)(2,1)} async-done(((bf16[2,128,1024]{2,1,0:T(8,128)(2,1)}), bf16[32,128,1024]{2,1,0:T(8,128)(2,1)}) %all-gather.5.cloned.1.call-update) | async-done | bytes 8388624 | tf_op jit(solution)/shard_map/all_gather | solution.py:395
  163.5 0.6 iota.39.refs_0_
  164.1 7.4 %shard_map.59.own_ref.refs_1_ = bf16[2,128,1024]{2,1,0:T(8,128)(2,1)} custom-call(s32[1,16]{1,0:T(1,128)} %iota.39.refs_0_, s32[2,4]{1,0:T(2,128)} %slice_bitcast_fusion.8.refs_1_, bf16[128,2048]{1,0:T(8,128)(2,1)} %pad_maximum_fusion.2.refs_2_, bf16[128,2048]{1,0:T(8,128)(2,1)} %bitcast.129, bf16[128,2048]{1,0:T(8,128)(2,1)} %bitcast.127, ...), custom_call_target="tpu_custom_call" | custom-call | flops 1 | bytes 1 | tf_op jit(solution)/shard_map/pallas_call | solution.py:209
  171.5 2.1 collective-permute-done.10.other_ref
  173.6 0.8 copy-done.10
  174.5 2.6 shard_map.60
  177.0 27.4 %all_to_all.15.own_ref = bf16[16,2,64,128]{3,2,1,0:T(8,128)(2,1)S(1)} all-to-all(bf16[16,2,64,128]{3,2,1,0:T(8,128)(2,1)} %get-tuple-element.19), channel_id=1, replica_groups=mesh['wide'=16,'narrow'=2] {'wide'}, dimensions={0} | all-to-all | bytes 1048576 | tf_op jit(solution)/shard_map/all_to_all | solution.py:415
  204.4 0.6 slice_bitcast_fusion.7.refs_1_
  205.0 1.3 collective-permute-done.11.other_ref
  206.4 0.8 copy-done.9
  207.2 2.7 shard_map.61.refs_4_
  209.9 2.6 slice_bitcast_fusion.3
  212.4 0.6 iota.40.refs_0_
  213.0 6.5 %shard_map.62 = (f32[128,1024]{1,0:T(8,128)}, bf16[128,1024]{1,0:T(8,128)(2,1)}) custom-call(s32[1,16]{1,0:T(1,128)} %iota.40.refs_0_, s32[1,4]{1,0:T(1,128)} %get-tuple-element.51.refs_1_, bf16[128,2048]{1,0:T(8,128)(2,1)} %get-tuple-element.35.refs_2_.refs_8_, bf16[128,2048]{1,0:T(8,128)(2,1)} %get-tuple-element.34.refs_3_.refs_9_, ...), custom_call_target="tpu_custom_call" | custom-call | flops 1 | bytes 1 | tf_op jit(solution)/shard_map/pallas_call | solution.py:209
  219.6 1.1 slice_bitcast_fusion.5
  220.7 0.6 collective-permute-done.12
  221.3 1.0 broadcast_select_fusion.1
  222.3 0.8 pad_maximum_fusion.5.refs_10_
  223.1 104.7 %all-gather.7.cloned.1.call-done = bf16[48,128,1024]{2,1,0:T(8,128)(2,1)} async-done(((bf16[3,128,1024]{2,1,0:T(8,128)(2,1)}), bf16[48,128,1024]{2,1,0:T(8,128)(2,1)}) %all-gather.7.cloned.1.call-update) | async-done | bytes 12582928 | tf_op jit(solution)/shard_map/all_gather | solution.py:393
  327.7 0.6 iota.35.refs_0_
  328.3 11.7 %shard_map.63.own_ref.refs_2_ = bf16[3,128,1024]{2,1,0:T(8,128)(2,1)} custom-call(s32[1,16]{1,0:T(1,128)} %iota.35.refs_0_, s32[3,4]{1,0:T(4,128)} %slice_bitcast_fusion.7.refs_1_, bf16[128,2048]{1,0:T(8,128)(2,1)} %pad_maximum_fusion.2.refs_2_, bf16[128,2048]{1,0:T(8,128)(2,1)} %bitcast.130, bf16[128,2048]{1,0:T(8,128)(2,1)} %get-tuple-element.37.refs_4_, ...), custom_call_target="tpu_custom_call" | custom-call | flops 1 | bytes 1 | tf_op jit(solution)/shard_map/pallas_call | solution.py:209
  340.0 2.5 collective-permute-done.13.other_ref
  342.5 0.9 copy-done.7
  343.4 3.0 shard_map.64
  346.4 25.4 %all_to_all.16.own_ref = bf16[16,3,64,128]{3,2,1,0:T(8,128)(2,1)S(1)} all-to-all(bf16[16,3,64,128]{3,2,1,0:T(8,128)(2,1)} %get-tuple-element.21), channel_id=1, replica_groups=mesh['wide'=16,'narrow'=2] {'wide'}, dimensions={0} | all-to-all | bytes 1572864 | tf_op jit(solution)/shard_map/all_to_all | solution.py:415
  371.8 6.1 %shard_map.67.held_ref = f32[4,128,4,1024]{3,2,1,0:T(4,128)} custom-call(s32[1]{0:T(128)} %bitcast.id_ref, f32[4,128,1024]{2,1,0:T(8,128)} %first_ref.1, bf16[1,128,1024]{2,1,0:T(8,128)(2,1)} %shard_map.55.own_ref.refs_0_, bf16[2,128,1024]{2,1,0:T(8,128)(2,1)} %shard_map.59.own_ref.refs_1_, bf16[3,128,1024]{2,1,0:T(8,128)(2,1)} %shard_map.63.own_ref.refs_2_, ...), custom_call_target="tpu_custom_call" | custom-call | bytes 1 | tf_op jit(solution)/shard_map/pallas_call | solution.py:321
  377.9 0.9 copy-done.8
  378.8 3.0 shard_map.65.turn_ref
  381.8 2.6 slice_bitcast_fusion
  384.9 7.9 %shard_map.66 = (f32[128,1024]{1,0:T(8,128)}, bf16[128,1024]{1,0:T(8,128)(2,1)}) custom-call(s32[1,16]{1,0:T(1,128)} %iota.41.refs_0_, s32[1,4]{1,0:T(1,128)} %get-tuple-element.50.refs_1_, bf16[128,2048]{1,0:T(8,128)(2,1)} %get-tuple-element.33.refs_2_, bf16[128,2048]{1,0:T(8,128)(2,1)} %get-tuple-element.32.refs_3_, ...), custom_call_target="tpu_custom_call" | custom-call | flops 1 | bytes 1 | tf_op jit(solution)/shard_map/pallas_call | solution.py:209
  392.7 3.9 shard_map.68
  (73 shorter events, 4.4 us)
Async XLA Ops:
  6.5 157.0 %all-gather.5.cloned.1.call-start = ((), (), s32[]{:S(2)}) async-start(), calls=%async_computation.3 | async-start | bytes 8912896 | tf_op jit(solution)/shard_map/all_gather | solution.py:395
  15.8 311.9 %all-gather.7.cloned.1.call-start = ((), (), s32[]{:S(2)}) async-start(), calls=%async_computation.4 | async-start | bytes 13369344 | tf_op jit(solution)/shard_map/all_gather | solution.py:393
  16.0 42.9 %copy-start.13 = (s32[4,8]{1,0:T(4,128)S(1)}, s32[4,8]{1,0:T(4,128)}, u32[]{:S(2)}) copy-start(s32[4,8]{1,0:T(4,128)} %param.8) | copy-start | bytes 388
  16.1 43.1 %copy-start.14 = (s32[15]{0:T(128)S(1)}, s32[15]{0:T(128)}, u32[]{:S(2)}) copy-start(s32[15]{0:T(128)} %param.7) | copy-start | bytes 184
  17.4 12.9 %collective-permute-start.3 = (bf16[1,128,1024]{2,1,0:T(8,128)(2,1)S(1)}, bf16[1,128,1024]{2,1,0:T(8,128)(2,1)S(1)}, u32[]{:S(2)}, u32[]{:S(2)}) collective-permute-start(bf16[1,128,1024]{2,1,0:T(8,128)(2,1)S(1)} %bitcast_multiply_fusion), channel_id=1, source_target_pairs={{0,24},{2,26},{4,28},{6,30},{8,0},{10,2},{12,4},{14,6},{16,8},{18,... | collective-permute-start | bytes 786440 | tf_op jit(solution)/shard_map/ppermute | solution.py:68
  22.5 33.5 %collective-permute-start.2 = (bf16[1,128,1024]{2,1,0:T(8,128)(2,1)S(1)}, bf16[1,128,1024]{2,1,0:T(8,128)(2,1)S(1)}, u32[]{:S(2)}, u32[]{:S(2)}) collective-permute-start(bf16[1,128,1024]{2,1,0:T(8,128)(2,1)S(1)} %bitcast_multiply_fusion), channel_id=1, source_target_pairs={{0,16},{2,18},{4,20},{6,22},{8,24},{10,26},{12,28},{14,30},{16,0},... | collective-permute-start | bytes 786440 | tf_op jit(solution)/shard_map/ppermute | solution.py:68
  22.5 33.5 %collective-permute-start.1 = (bf16[1,128,1024]{2,1,0:T(8,128)(2,1)S(1)}, bf16[1,128,1024]{2,1,0:T(8,128)(2,1)S(1)}, u32[]{:S(2)}, u32[]{:S(2)}) collective-permute-start(bf16[1,128,1024]{2,1,0:T(8,128)(2,1)S(1)} %bitcast_multiply_fusion), channel_id=1, source_target_pairs={{0,8},{2,10},{4,12},{6,14},{8,16},{10,18},{12,20},{14,22},{16,24},... | collective-permute-start | bytes 786440 | tf_op jit(solution)/shard_map/ppermute | solution.py:68
  56.2 52.6 %copy-start = (bf16[4,1,128,1024]{3,2,1,0:T(8,128)(2,1)}, bf16[4,1,128,1024]{3,2,1,0:T(8,128)(2,1)S(1)}, u32[]{:S(2)}) copy-start(bf16[4,1,128,1024]{3,2,1,0:T(8,128)(2,1)S(1)} %pad_maximum_fusion.refs_3_) | copy-start | bytes 3145732
  56.2 37.7 %collective-permute-start.4 = (bf16[4,1,128,1024]{3,2,1,0:T(8,128)(2,1)S(1)}, bf16[4,1,128,1024]{3,2,1,0:T(8,128)(2,1)S(1)}, u32[]{:S(2)}, u32[]{:S(2)}) collective-permute-start(bf16[4,1,128,1024]{3,2,1,0:T(8,128)(2,1)S(1)} %pad_maximum_fusion.refs_3_), channel_id=1, source_target_pairs={{0,2},{1,5},{2,0},{3,7},{4,6},{5,1},{6,4},{7,3},{8,10},{9,13},{10,... | collective-permute-start | bytes 3145736 | tf_op jit(solution)/shard_map/ppermute | solution.py:62
  58.8 37.9 %collective-permute-start = (bf16[128,1024]{1,0:T(8,128)(2,1)S(1)}, bf16[128,1024]{1,0:T(8,128)(2,1)}, u32[]{:S(2)}, u32[]{:S(2)}) collective-permute-start(bf16[128,1024]{1,0:T(8,128)(2,1)S(1)} %fusion.1), channel_id=1, source_target_pairs={{0,1},{1,0},{2,3},{3,2},{4,5},{5,4},{6,7},{7,6},{8,9},{9,8},{10,11... | collective-permute-start | bytes 786440 | tf_op jit(solution)/shard_map/ppermute | solution.py:42
  60.0 38.8 %collective-permute-start.5 = (bf16[4,1,128,1024]{3,2,1,0:T(8,128)(2,1)S(1)}, bf16[4,1,128,1024]{3,2,1,0:T(8,128)(2,1)S(1)}, u32[]{:S(2)}, u32[]{:S(2)}) collective-permute-start(bf16[4,1,128,1024]{3,2,1,0:T(8,128)(2,1)S(1)} %pad_maximum_fusion.refs_3_), channel_id=1, source_target_pairs={{0,4},{1,3},{2,6},{3,1},{4,0},{5,7},{6,2},{7,5},{8,12},{9,11},{10,... | collective-permute-start | bytes 3145736 | tf_op jit(solution)/shard_map/ppermute | solution.py:62
  93.9 14.9 %copy-start.1 = (bf16[4,1,128,1024]{3,2,1,0:T(8,128)(2,1)}, bf16[4,1,128,1024]{3,2,1,0:T(8,128)(2,1)S(1)}, u32[]{:S(2)}) copy-start(bf16[4,1,128,1024]{3,2,1,0:T(8,128)(2,1)S(1)} %collective-permute-done.4.refs_4_) | copy-start | bytes 3145732
  93.9 14.9 %collective-permute-start.6 = (bf16[4,1,128,1024]{3,2,1,0:T(8,128)(2,1)S(1)}, bf16[4,1,128,1024]{3,2,1,0:T(8,128)(2,1)}, u32[]{:S(2)}, u32[]{:S(2)}) collective-permute-start(bf16[4,1,128,1024]{3,2,1,0:T(8,128)(2,1)S(1)} %collective-permute-done.4.refs_4_), channel_id=1, source_target_pairs={{0,4},{1,3},{2,6},{3,1},{4,0},{5,7},{6,2},{7,5},{8,12},{9,11},{10,... | collective-permute-start | bytes 3145736 | tf_op jit(solution)/shard_map/ppermute | solution.py:62
  98.8 10.0 %copy-start.2 = (bf16[4,1,128,1024]{3,2,1,0:T(8,128)(2,1)}, bf16[4,1,128,1024]{3,2,1,0:T(8,128)(2,1)S(1)}, u32[]{:S(2)}) copy-start(bf16[4,1,128,1024]{3,2,1,0:T(8,128)(2,1)S(1)} %collective-permute-done.5.refs_5_) | copy-start | bytes 3145732
  114.2 1.7 collective-permute-start.7
  115.9 0.7 copy-start.11
  118.7 21.3 %all-to-all-start = ((bf16[16,1,64,128]{3,2,1,0:T(8,128)(2,1)}), bf16[16,1,64,128]{3,2,1,0:T(8,128)(2,1)S(1)}, u32[]{:S(2)}, u32[]{:S(2)}) async-start(bf16[16,1,64,128]{3,2,1,0:T(8,128)(2,1)} %get-tuple-element.16), calls=%async_computation | async-start | bytes 524288 | tf_op jit(solution)/shard_map/all_to_all | solution.py:415
  139.9 1.5 copy-start.6
  139.9 1.5 collective-permute-start.8
  141.5 0.7 copy-start.12
  149.5 1.7 collective-permute-start.9
  171.5 2.1 collective-permute-start.10
  173.6 0.8 copy-start.10
  204.4 1.9 copy-start.4
  204.4 1.9 collective-permute-start.11
  206.4 0.8 copy-start.9
  213.0 6.6 %copy-start.5 = (bf16[2,128,2048]{2,1,0:T(8,128)(2,1)S(1)}, bf16[2,128,2048]{2,1,0:T(8,128)(2,1)}, u32[]{:S(2)}) copy-start(bf16[2,128,2048]{2,1,0:T(8,128)(2,1)} %get-tuple-element.18) | copy-start | bytes 3145732
  219.5 1.7 collective-permute-start.12
  340.0 2.5 collective-permute-start.13
  342.5 0.9 copy-start.7
  371.8 6.1 %copy-start.3 = (bf16[16,3,64,128]{3,2,1,0:T(8,128)(2,1)}, bf16[16,3,64,128]{3,2,1,0:T(8,128)(2,1)S(1)}, u32[]{:S(2)}) copy-start(bf16[16,3,64,128]{3,2,1,0:T(8,128)(2,1)S(1)} %all_to_all.16.own_ref) | copy-start | bytes 2359300
  371.8 6.1 %collective-permute-start.14 = (bf16[16,3,64,128]{3,2,1,0:T(8,128)(2,1)S(1)}, bf16[16,3,64,128]{3,2,1,0:T(8,128)(2,1)S(1)}, u32[]{:S(2)}, u32[]{:S(2)}) collective-permute-start(bf16[16,3,64,128]{3,2,1,0:T(8,128)(2,1)S(1)} %all_to_all.16.own_ref), channel_id=1, source_target_pairs={{0,1},{1,0},{2,3},{3,2},{4,5},{5,4},{6,7},{7,6},{8,9},{9,8},{10,11... | collective-permute-start | bytes 2359304 | tf_op jit(solution)/shard_map/ppermute | solution.py:282
  377.9 0.9 copy-start.8
Sparse Core Ops, SparseCore 0:
  15.9 147.5 all-gather.4
  166.3 161.4 all-gather.6

commit v3 on v2

--- a/solution.py
+++ b/solution.py
@@ -291,6 +291,279 @@
     )(lax.axis_index("narrow").astype(jnp.int32).reshape(1), got, other)
 
 
+SRC, POS, HELD, OWN, KEEP = 0, 16, 24, 40, 48
+WIDTHS = {2: (4, 2), 3: (4, 2, 1)}
+
+
+def table_body(id_ref, parent_ref, node_ref, structure_ref, out_ref):
+    core, row = id_ref[0], id_ref[1]
+    for i in range(out_ref.shape[0]):
+        out_ref[i] = jnp.int32(0)
+    one, none = jnp.int32(1), jnp.int32(0)
+    nodes = [[node_ref[k, t] for t in range(LT)] for k in range(LEV)]
+    above = [[parent_ref[nodes[k][t]] for t in range(LT)] for k in range(LEV)]
+    left = nodes[1][0]
+    key1 = [jnp.where(nodes[1][t] == left, none, one) for t in range(LT)]
+
+    def second(k, t):
+        found = none
+        for u in range(LT):
+            less = (above[k][u] == above[k][t]) & (nodes[k][u] < nodes[k][t])
+            found = jnp.where(less, one, found)
+        return found
+
+    key2 = [jnp.where(above[2][t] == left, none, 2 * one) + second(2, t) for t in range(LT)]
+    for t in range(LT):
+        again = none
+        for u in range(t):
+            again = jnp.where(nodes[2][u] == nodes[2][t], one, again)
+        place = again * 4 + key2[t]
+        out_ref[SRC + t] = place
+        out_ref[HELD + place] = jnp.int32(t)
+        upper = none
+        for u in range(LT):
+            upper = jnp.where(nodes[2][u] == above[3][t], key2[u], upper)
+        place = second(3, t) * 4 + upper
+        out_ref[SRC + LT + t] = place
+        out_ref[HELD + LT + place] = jnp.int32(t)
+        rank = none
+        for u in range(t):
+            rank = rank + jnp.where(key1[u] == key1[t], one, none)
+        out_ref[POS + key1[t] * 4 + rank] = jnp.int32(t)
+
+        @pl.when(row == t)
+        def _():
+            out_ref[OWN] = key1[t]
+            out_ref[OWN + 1] = key2[t]
+            out_ref[OWN + 2] = out_ref[SRC + LT + t] % 4
+
+    for m in (2, 3):
+        for k in range(m):
+            for i in range(WIDTHS[m][k]):
+                q = i
+                if k == 1:
+                    q = out_ref[OWN] * 2 + i
+                if k == 2:
+                    q = out_ref[OWN + 1]
+                tile = out_ref[HELD + (m - 2) * LT + core * 4 + q]
+                at = KEEP + (m - 2) * 16 + k * 4 + i
+                out_ref[at] = structure_ref[node_ref[m, tile], k, row]
+                out_ref[at + 32] = tile
+
+
+def make_table(parent, tile_node, structure, row_tile):
+    ids = jnp.stack([lax.axis_index("narrow"), row_tile]).astype(jnp.int32)
+    return pl.pallas_call(
+        table_body,
+        in_specs=[pl.BlockSpec(memory_space=pltpu.SMEM)] * 4,
+        out_specs=pl.BlockSpec(memory_space=pltpu.SMEM),
+        out_shape=jax.ShapeDtypeStruct((128,), jnp.int32),
+    )(ids, parent, tile_node, structure)
+
+
+PAIRS = ((0, 2), (1, 2), (0, 3), (1, 3), (2, 3))
+
+
+def pack_body(id_ref, table_ref, own_ref, other_ref, two_ref, three_ref):
+    half = LT // 2
+    for b, (k, m) in enumerate(PAIRS):
+        out = two_ref if m == 2 else three_ref
+        base = sum(WIDTHS[m][:k])
+        for i in range(WIDTHS[m][k]):
+            at = KEEP + (m - 2) * 16 + k * 4 + i
+            tile = table_ref[at + 32]
+            keep = table_ref[at] > 0
+            mine = tile // half == id_ref[0]
+            start = pl.multiple_of(tile % half * TILE, TILE)
+            cols = slice((base + i) * TILE, (base + i + 1) * TILE)
+
+            @pl.when(keep & mine)
+            def _():
+                out[:, cols] = own_ref[b, :, pl.ds(start, TILE)]
+
+            @pl.when(keep & jnp.logical_not(mine))
+            def _():
+                out[:, cols] = other_ref[b, :, pl.ds(start, TILE)]
+
+            @pl.when(jnp.logical_not(keep))
+            def _():
+                out[:, cols] = jnp.zeros((out.shape[0], TILE), BF)
+
+
+def packed(factor, table):
+    r = factor.shape[1]
+    own = jnp.stack([factor[k, :, m, :] for k, m in PAIRS])
+    other = lax.ppermute(own, "narrow", [(0, 1), (1, 0)])
+    whole = pl.BlockSpec(memory_space=pltpu.VMEM)
+    scalar = pl.BlockSpec(memory_space=pltpu.SMEM)
+    return pl.pallas_call(
+        pack_body,
+        in_specs=[scalar, scalar, whole, whole],
+        out_specs=(whole, whole),
+        out_shape=tuple(jax.ShapeDtypeStruct((r, sum(WIDTHS[m]) * TILE), BF) for m in (2, 3)),
+        compiler_params=pltpu.CompilerParams(vmem_limit_bytes=VMEM),
+        cost_estimate=pl.CostEstimate(flops=1, bytes_accessed=1, transcendentals=0),
+    )(lax.axis_index("narrow").astype(jnp.int32).reshape(1), table, own, other)
+
+
+def sparse_body(level, rows_n, mirror, table_ref, *refs):
+    row_refs = [refs[q * level : (q + 1) * level] for q in range(rows_n)]
+    refs = refs[rows_n * level :]
+    piece_refs, out_ref, lhs = refs[:level], refs[level], refs[level + 1]
+    r = row_refs[0][0].shape[0]
+    span = LT * TILE
+    per = TILE // r
+    q = pl.program_id(0)
+
+    @pl.when(q == 0)
+    def _():
+        for p in range(rows_n):
+            for j in range(level):
+                lhs[p * r : (p + 1) * r, j * span : (j + 1) * span] = row_refs[p][j][...]
+
+    if mirror:
+        q = table_ref[OWN + level - 1]
+    total = jnp.dot(lhs[:, :span], piece_refs[0][...].reshape(span, TILE), preferred_element_type=F32)
+    for j in range(1, level):
+        for i in range(4 // j):
+            if j == 1:
+                tile = table_ref[POS + q // 2 * 4 + i]
+            else:
+                tile = table_ref[HELD + i * 4 + q]
+            start = pl.multiple_of(j * span + tile * TILE, TILE)
+            block = piece_refs[j][pl.ds(tile * per, per)].reshape(TILE, TILE)
+            total += jnp.dot(lhs[:, pl.ds(start, TILE)], block, preferred_element_type=F32)
+    if mirror:
+        out_ref[...] = total
+    else:
+        for p in range(rows_n):
+            value = -total[p * r : (p + 1) * r]
+            if p == 1:
+                value = jnp.where(table_ref[OWN] == q // 2, value, 0.0)
+            if p == 2:
+                value = jnp.where(table_ref[OWN + 1] == q, value, 0.0)
+            out_ref[p] = value.astype(BF)
+
+
+def sparse_product(level, table, rows, panel, mirror):
+    wide, r, _ = panel.shape
+    rows_n = len(rows)
+
+    def column(j):
+        def index(i, t):
+            q = t[OWN + level - 1] if mirror else i
+            if j == 0:
+                return (0, 0, q)
+            if j == 1:
+                return (0, 0, 4 + q % 2)
+            return (0, 0, 6)
+
+        return index
+
+    whole = pl.BlockSpec(memory_space=pltpu.VMEM)
+    flat = [x for row in rows for x in row]
+    specs = [whole] * len(flat) + [pl.BlockSpec((wide, r, TILE), column(j)) for j in range(level)]
+    if mirror:
+        shape = jax.ShapeDtypeStruct((r, TILE), F32)
+        out_spec = pl.BlockSpec((r, TILE), lambda i, t: (0, 0))
+    else:
+        shape = jax.ShapeDtypeStruct((rows_n, r, 4 * TILE), BF)
+        out_spec = pl.BlockSpec((rows_n, r, TILE), lambda i, t: (0, 0, i))
+    return pl.pallas_call(
+        functools.partial(sparse_body, level, rows_n, mirror),
+        grid_spec=pltpu.PrefetchScalarGridSpec(
+            num_scalar_prefetch=1,
+            grid=(1 if mirror else 4,),
+            in_specs=specs,
+            out_specs=out_spec,
+            scratch_shapes=[pltpu.VMEM((rows_n * r, level * LT * TILE), BF)],
+        ),
+        out_shape=shape,
+        compiler_params=pltpu.CompilerParams(vmem_limit_bytes=VMEM),
+        cost_estimate=pl.CostEstimate(flops=1, bytes_accessed=1, transcendentals=0),
+    )(table, *flat, *[panel] * level)
+
+
+def place_body(level, levels, id_ref, table_ref, own_ref, other_ref, slots_ref, full_ref):
+    r = own_ref.shape[1]
+    part = r // 2
+    per = TILE // r
+    me = id_ref[0]
+    first = pl.multiple_of(me * part, part)
+    for c in range(LT):
+        source = table_ref[SRC + (level - 2) * LT + c]
+        start = pl.multiple_of(source % 4 * TILE, TILE)
+
+        def put(ref):
+            for k in range(levels):
+                full_ref[k, :, c * TILE : (c + 1) * TILE] = ref[k, :, pl.ds(start, TILE)]
+                for i in range(per):
+                    at = pl.multiple_of(start + i * r, r)
+                    slots_ref[c * per + i, k] = ref[k, pl.ds(first, part), pl.ds(at, r)]
+
+        @pl.when(source // 4 == me)
+        def _():
+            put(own_ref)
+
+        @pl.when(source // 4 != me)
+        def _():
+            put(other_ref)
+
+
+def place_slots(level, table, value):
+    wide = lax.axis_size("wide")
+    l, r, c = value.shape
+    other = lax.ppermute(value, "narrow", [(0, 1), (1, 0)])
+    whole = pl.BlockSpec(memory_space=pltpu.VMEM)
+    scalar = pl.BlockSpec(memory_space=pltpu.SMEM)
+    return pl.pallas_call(
+        functools.partial(place_body, level, l),
+        in_specs=[scalar, scalar, whole, whole],
+        out_specs=(whole, whole),
+        out_shape=(
+            jax.ShapeDtypeStruct((wide, l, r // 2, r), BF),
+            jax.ShapeDtypeStruct((l, r, 2 * c), BF),
+        ),
+        compiler_params=pltpu.CompilerParams(vmem_limit_bytes=VMEM),
+        cost_estimate=pl.CostEstimate(flops=1, bytes_accessed=1, transcendentals=0),
+    )(lax.axis_index("narrow").astype(jnp.int32).reshape(1), table, value, other)
+
+
+def diag_body(level, id_ref, table_ref, own_ref, other_ref, diag_ref, out_ref, low_ref):
+    me, row = id_ref[0], id_ref[1]
+    half = LT // 2
+    base = SRC + (level - 2) * LT
+    for c in range(LT):
+        source = table_ref[base + c]
+        same = source % 4 == table_ref[base + row] % 4
+        if level == 3:
+            same = row == c
+        cols = slice(c * TILE, (c + 1) * TILE)
+        inner = jnp.where(source // 4 == me, own_ref[...], other_ref[...])
+        value = jnp.where(same, diag_ref[:, cols] - inner, 0.0)
+        low_ref[:, cols] = value.astype(BF)
+
+        @pl.when(me == c // half)
+        def _():
+            out_ref[:, (c % half) * TILE : (c % half + 1) * TILE] = value
+
+
+def diag_block(level, table, inner, diag, row_tile):
+    r, span = diag.shape
+    other = lax.ppermute(inner, "narrow", [(0, 1), (1, 0)])
+    ids = jnp.stack([lax.axis_index("narrow"), row_tile]).astype(jnp.int32)
+    whole = pl.BlockSpec(memory_space=pltpu.VMEM)
+    scalar = pl.BlockSpec(memory_space=pltpu.SMEM)
+    return pl.pallas_call(
+        functools.partial(diag_body, level),
+        in_specs=[scalar, scalar, whole, whole, whole],
+        out_specs=(whole, whole),
+        out_shape=(jax.ShapeDtypeStruct((r, span // 2), F32), jax.ShapeDtypeStruct((r, span), BF)),
+        compiler_params=pltpu.CompilerParams(vmem_limit_bytes=VMEM),
+        cost_estimate=pl.CostEstimate(flops=1, bytes_accessed=1, transcendentals=0),
+    )(ids, table, inner, other, diag)
+
+
 def upper_body(id_ref, first_ref, *refs):
     news, turns, diags, out_ref = refs[0:3], refs[3:5], refs[5:7], refs[7]
     for k in range(LEV - 1):
@@ -315,7 +588,7 @@
     step = min(r, 32)
     shape = jax.ShapeDtypeStruct((LEV, r, LEV, c), F32)
     specs = [pl.BlockSpec((1, step, c), lambda i, n: (0, i, 0))]
-    specs += [pl.BlockSpec((m, step, c), lambda i, n: (0, i, 0)) for m in range(1, LEV)]
+    specs += [pl.BlockSpec((m, step, c), lambda i, n: (0, i, n[0])) for m in range(1, LEV)]
     specs += [pl.BlockSpec((k, step, c), lambda i, n: (0, i, n[0])) for k in range(1, LEV - 1)]
     specs += [pl.BlockSpec((step, c), lambda i, n: (i, 0)) for k in range(1, LEV - 1)]
     return pl.pallas_call(
@@ -390,24 +663,33 @@
 
     wide = lax.axis_size("wide")
     whole_place = jnp.arange(wide, dtype=jnp.int32)
-    last = lax.all_gather(panel_of(3), "wide", axis=0)
+    compact = lax.axis_size("narrow") == 2 and row_count % 128 == 0 and TILE % row_count == 0
     first = along_z(panel_of(1), None)
-    gathered_two = lax.all_gather(panel_of(2), "wide", axis=0)
-    gathered = {1: along_both(along_xy(first, None), None)}
-    gathered[3] = [last]
-    gathered[2] = [gathered_two]
+    if compact:
+        table = make_table(parent, tile_node, structure, row_pos)
+        shards = packed(factor, table)
+        panels = {m: lax.all_gather(shards[m - 2], "wide", axis=0) for m in (2, 3)}
+        wide_diag = {m: narrow_all(diag_inverse[m], 1) for m in (2, 3)}
+    else:
+        panels = {m: lax.all_gather(panel_of(m), "wide", axis=0) for m in (2, 3)}
+    one = along_both(along_xy(first, None), None)
 
     rows = {0: [narrow_all(diag_inverse[0].astype(BF), 1)]}
     news, turns, diags = [], [], []
     for level in range(1, LEV):
-        arrays = gathered[level]
         known = [rows[k] for k in range(level)]
-        groups = [(tuple(range(level)), place if level == 1 else whole_place, arrays)]
-        value = product(known, groups, above[:level, level])
-        news.append(value)
-        if level == 1:
-            pass
-        slots, full = make_slots(value)
+        packed_here = compact and level > 1
+        if packed_here:
+            value = sparse_product(level, table, known, panels[level], False)
+            slots, full = place_slots(level, table, value)
+        else:
+            if level == 1:
+                groups = [((0,), place, one)]
+            else:
+                groups = [(tuple(range(level)), whole_place, [panels[level]])]
+            value = product(known, groups, above[:level, level])
+            slots, full = make_slots(value)
+        news.append(full)
         for k in range(level):
             rows[k].append(full[k])
         if level == LEV - 1:
@@ -416,10 +698,15 @@
         turn = mirrored(got, full)
         turns.append(turn)
         rows[level] = [turn[k] for k in range(level)]
-        done, low = product([rows[level]], groups, same[level : level + 1], (diag_inverse, level))
+        if packed_here:
+            inner = sparse_product(level, table, [rows[level]], panels[level], True)
+            done, whole_low = diag_block(level, table, inner, wide_diag[level], row_pos)
+        else:
+            done, low = product([rows[level]], groups, same[level : level + 1], (diag_inverse, level))
+            whole_low = narrow_all(low, 1) if level < LEV - 1 else None
         diags.append(done)
         if level < LEV - 1:
-            rows[level].append(narrow_all(low, 1))
+            rows[level].append(whole_low)
     return lower_rows(turns[-1], diags[-1], out)
 
 

time: 405 us -> 344 us (0.85)
  waiting for transfers between devices: 215 us -> 166 us
  blocking collectives: 52.8 us -> 25.4 us
  starting transfers between devices: 17.8 us -> 29.7 us
    all_gather x2, waiting for transfers between devices: 115 us -> 43.9 us  [local(): panels = {m: lax.all_gather(shards[m - 2], 'wide', axis=0) for m in (2, 3)}]
    pallas_call x0 -> x10, Pallas kernels: none -> 42.2 us  [the longest x4 25.1 us: sparse_product(): pl.pallas_call(functools.partial(sparse_body, level, rows_n, mirror), gri...]
    pallas_call x6 -> x2, Pallas kernels: 44 us -> 9.97 us  [product(): pl.pallas_call(functools.partial(product_body, plan, rows_n, steps_n, dia...]
    all_to_all x2 -> x1, blocking collectives: 52.8 us -> 25.4 us  [local(): got = lax.all_to_all(slots, 'wide', split_axis=0, concat_axis=0, tiled=True)]
    all_to_all x1 -> x2, waiting for transfers between devices: 14.5 us -> 34.2 us  [local(): got = lax.all_to_all(slots, 'wide', split_axis=0, concat_axis=0, tiled=True)]
    all_to_all x1 -> x2, starting transfers between devices: 6.61 us -> 17 us  [local(): got = lax.all_to_all(slots, 'wide', split_axis=0, concat_axis=0, tiled=True)]
    pallas_call x3 -> x1, Pallas kernels: 7.61 us -> 2.05 us  [make_slots(): pl.pallas_call(functools.partial(slots_body, l, wide), in_specs=[pl.Block...]
    ppermute x3 -> x1, waiting for transfers between devices: 6.35 us -> 1.74 us  [make_slots(): other = lax.ppermute(value, 'narrow', [(0, 1), (1, 0)])]
  transfers between devices with their start and end apart: 18 -> 23, of which waited for: 14 -> 14; matrix products, arithmetic and copies ran while one was open for 4% -> 6% of each run, Pallas kernels for 10% -> 12%
where the time goes in v3:
time: 344 us; the launch traced here: 343 us
  waiting for transfers between devices  166 us (48%)
  Pallas kernels  71.4 us (21%)
  starting transfers between devices  29.7 us (9%)
  blocking collectives  25.4 us (7%)
  local copies, waits for them, and re-layouts  24 us (7%)
  between operations  13.7 us (4%)
  other arithmetic  10.4 us (3%)
    ppermute x3, waiting for transfers between devices, swap(): return lax.ppermute(value, ('wide', 'narrow'), pairs)  46.4 us
    all_gather x2, waiting for transfers between devices, local(): panels = {m: lax.all_gather(shards[m - 2], 'wide', axis=0) for m in (2, 3)}  43.9 us
    all_to_all x2, waiting for transfers between devices, local(): got = lax.all_to_all(slots, 'wide', split_axis=0, concat_axis=0, tiled=True)  34.2 us
    ppermute x3, waiting for transfers between devices, shifts(): lax.ppermute(value, 'wide', [(i, (i + 4 * hop) % wide) for i in range(wid...  30 us
    all_to_all x1, blocking collectives, local(): got = lax.all_to_all(slots, 'wide', split_axis=0, concat_axis=0, tiled=True)  25.4 us
    pallas_call x4, Pallas kernels, sparse_product(): pl.pallas_call(functools.partial(sparse_body, level, rows_n, mirror), gri...  25.1 us
    all_to_all x2, starting transfers between devices, local(): got = lax.all_to_all(slots, 'wide', split_axis=0, concat_axis=0, tiled=True)  17 us
    pallas_call x2, Pallas kernels, product(): pl.pallas_call(functools.partial(product_body, plan, rows_n, steps_n, dia...  9.97 us
  transfers between devices with their start and end apart: 23, of which 14 were waited for; matrix products, arithmetic and copies ran while one was open for 6% of the time, Pallas kernels for 12%

profile of v3, /device:TPU:0, one launch (start us, length us, event | category | flops | bytes accessed | tf_op | source)
XLA Modules:
  0.0 342.7 jit_solution(149741326733068186)
XLA Ops:
  6.5 6.1 %fusion.30 = (bf16[1,128,1,1024]{3,2,1,0:T(2,128)(2,1)S(1)}, bf16[1,128,1,1024]{3,2,1,0:T(2,128)(2,1)S(1)}, bf16[1,128,1,1024]{3,2,1,0:T(2,128)(2,1)S(1)}, bf16[...) fusion(bf16[4,128,4,1024]{3,2,1,0:T(4,128)(2,1)} %param.5), kind=kLoop, calls=%fused_computation.77 | loop fusion | bytes 3145728 | tf_op jit(solution)/shard_map/slice | solution.py:395
  13.7 0.7 copy.7.structure_ref
  14.4 0.7 pad_add_fusion.id_ref
  15.0 2.4 shard_map.55.table_ref
  17.4 1.1 copy-done.9
  18.5 3.0 shard_map.60
  21.6 0.7 all-gather.7.cloned.1.call-update
  23.2 5.0 %collective-permute-start.3 = (bf16[1,128,1024]{2,1,0:T(8,128)(2,1)S(1)}, bf16[1,128,1024]{2,1,0:T(8,128)(2,1)S(1)}, u32[]{:S(2)}, u32[]{:S(2)}) collective-permute-start(bf16[1,128,1024]{2,1,0:T(8,128)(2,1)S(1)} %bitcast_multiply_fusion), channel_id=1, source_target_pairs={{0,24},{2,26},{4,28},{6,30},{8,0},{10,2},{12,4},{14,6},{16,8},{18,... | collective-permute-start | bytes 786440 | tf_op jit(solution)/shard_map/ppermute | solution.py:68
  28.2 1.0 collective-permute-start.1
  29.3 6.8 %collective-permute-done.3 = bf16[1,128,1024]{2,1,0:T(8,128)(2,1)S(1)} collective-permute-done((bf16[1,128,1024]{2,1,0:T(8,128)(2,1)S(1)}, bf16[1,128,1024]{2,1,0:T(8,128)(2,1)S(1)}, u32[]{:S(2)}, u32[]{:S(2)}) %collective-permute-start.3) | collective-permute-done | bytes 262176 | tf_op jit(solution)/shard_map/ppermute | solution.py:68
  36.1 23.2 %collective-permute-done.2 = bf16[1,128,1024]{2,1,0:T(8,128)(2,1)S(1)} collective-permute-done((bf16[1,128,1024]{2,1,0:T(8,128)(2,1)S(1)}, bf16[1,128,1024]{2,1,0:T(8,128)(2,1)S(1)}, u32[]{:S(2)}, u32[]{:S(2)}) %collective-permute-start.2) | collective-permute-done | bytes 262176 | tf_op jit(solution)/shard_map/ppermute | solution.py:68
  59.5 1.6 collective-permute-start.4
  61.0 1.1 fusion
  63.2 1.5 collective-permute-start.5
  64.8 28.7 %collective-permute-done.4.refs_4_ = bf16[4,1,128,1024]{3,2,1,0:T(8,128)(2,1)S(1)} collective-permute-done((bf16[4,1,128,1024]{3,2,1,0:T(8,128)(2,1)S(1)}, bf16[4,1,128,1024]{3,2,1,0:T(8,128)(2,1)S(1)}, u32[]{:S(2)}, u32[]{:S(2)}) %collective-permute-start.4) | collective-permute-done | bytes 1048608 | tf_op jit(solution)/shard_map/ppermute | solution.py:62
  93.5 1.5 collective-permute-start.6
  96.3 1.2 broadcast_select_fusion.7
  97.5 0.8 pad_maximum_fusion.3.refs_2_.refs_0_
  98.3 17.7 %collective-permute-done.6.refs_6_ = bf16[4,1,128,1024]{3,2,1,0:T(8,128)(2,1)} collective-permute-done((bf16[4,1,128,1024]{3,2,1,0:T(8,128)(2,1)S(1)}, bf16[4,1,128,1024]{3,2,1,0:T(8,128)(2,1)}, u32[]{:S(2)}, u32[]{:S(2)}) %collective-permute-start.6) | collective-permute-done | bytes 1048608 | tf_op jit(solution)/shard_map/ppermute | solution.py:62
  116.0 4.8 %shard_map.56.own_ref = bf16[1,128,1024]{2,1,0:T(8,128)(2,1)} custom-call(s32[1,16]{1,0:T(1,128)} %add.64.refs_0_, s32[1,4]{1,0:T(1,128)} %fusion.25.refs_1_, bf16[128,2048]{1,0:T(8,128)(2,1)} %pad_maximum_fusion.3.refs_2_.refs_0_, bf16[4,1,128,1024]{3,2,1,0:T(8,128)(2,1)} %copy-done.1, bf16[4,1,128,1024]{3,2,1,0:T(8,128)(2,1)} %copy-done.3, ...), custom_call_target="tpu_custom_call" | custom-call | flops 1 | bytes 1 | tf_op jit(solution)/shard_map/pallas_call | solution.py:209
  120.9 1.7 collective-permute-done.7.other_ref
  122.6 0.7 copy-done.16
  123.3 2.0 shard_map.57
  125.4 10.2 %all-to-all-start = ((bf16[16,1,64,128]{3,2,1,0:T(8,128)(2,1)}), bf16[16,1,64,128]{3,2,1,0:T(8,128)(2,1)S(1)}, u32[]{:S(2)}, u32[]{:S(2)}) async-start(bf16[16,1,64,128]{3,2,1,0:T(8,128)(2,1)} %get-tuple-element.19), calls=%async_computation | async-start | bytes 524288 | tf_op jit(solution)/shard_map/all_to_all | solution.py:697
  135.7 13.3 %all-to-all-done.own_ref = bf16[16,1,64,128]{3,2,1,0:T(8,128)(2,1)S(1)} async-done(((bf16[16,1,64,128]{3,2,1,0:T(8,128)(2,1)}), bf16[16,1,64,128]{3,2,1,0:T(8,128)(2,1)S(1)}, u32[]{:S(2)}, u32[]{:S(2)}) %all-to-all-start) | async-done | bytes 262176 | tf_op jit(solution)/shard_map/all_to_all | solution.py:697
  149.6 0.9 collective-permute-done.8.other_ref
  150.6 0.7 copy-done.17
  151.3 2.0 shard_map.58.refs_3_
  153.3 5.1 %shard_map.59 = (f32[128,1024]{1,0:T(8,128)}, bf16[128,1024]{1,0:T(8,128)(2,1)}) custom-call(s32[1,16]{1,0:T(1,128)} %add.64.refs_0_, s32[1,4]{1,0:T(1,128)} %slice_convert_fusion.1.refs_1_, bf16[128,2048]{1,0:T(8,128)(2,1)} %bitcast.116, bf16[4,1,128,1024]{3,2,1,0:T(8,128)(2,1)} %copy-done.1, bf16[4,1,128,1024]{3,2,1,0:T(8,128)(2,1)} %copy-done.3, ...), custom_call_target="tpu_custom_call" | custom-call | flops 1 | bytes 1 | tf_op jit(solution)/shard_map/pallas_call | solution.py:209
  158.5 1.6 collective-permute-done.9
  160.2 1.0 broadcast_select_fusion.5
  161.2 0.8 pad_maximum_fusion.4.refs_3_.refs_4_
  162.0 7.5 %shard_map.61.own_ref = bf16[2,128,1024]{2,1,0:T(8,128)(2,1)} custom-call(s32[128]{0:T(128)} %shard_map.55.table_ref, bf16[128,2048]{1,0:T(8,128)(2,1)} %pad_maximum_fusion.3.refs_2_.refs_0_, bf16[128,2048]{1,0:T(8,128)(2,1)} %bitcast.119, bf16[128,2048]{1,0:T(8,128)(2,1)} %bitcast.117, bf16[128,2048]{1,0:T(8,128)(2,1)} %pad_maximum_fusion.4.refs_3_.refs_4_, ...), custom_call_target="tpu_custom_call" | custom-call | flops 1 | bytes 1 | tf_op jit(solution)/shard_map/pallas_call | solution.py:472
  169.6 2.0 collective-permute-done.11.other_ref
  171.6 0.8 copy-done.15
  172.4 2.8 shard_map.62
  175.2 6.8 %all-to-all-start.1 = ((bf16[16,2,64,128]{3,2,1,0:T(8,128)(2,1)}), bf16[16,2,64,128]{3,2,1,0:T(8,128)(2,1)S(1)}, u32[]{:S(2)}, u32[]{:S(2)}) async-start(bf16[16,2,64,128]{3,2,1,0:T(8,128)(2,1)} %get-tuple-element.23), calls=%async_computation.1 | async-start | bytes 1048576 | tf_op jit(solution)/shard_map/all_to_all | solution.py:697
  182.0 1.1 slice_bitcast_fusion.5
  183.5 20.9 %all-to-all-done.1.own_ref = bf16[16,2,64,128]{3,2,1,0:T(8,128)(2,1)S(1)} async-done(((bf16[16,2,64,128]{3,2,1,0:T(8,128)(2,1)}), bf16[16,2,64,128]{3,2,1,0:T(8,128)(2,1)S(1)}, u32[]{:S(2)}, u32[]{:S(2)}) %all-to-all-start.1) | async-done | bytes 524320 | tf_op jit(solution)/shard_map/all_to_all | solution.py:697
  204.4 0.8 copy-done.13
  205.3 2.2 broadcast_select_fusion.1
  207.5 1.0 pad_maximum_fusion.1.diag_ref
  208.5 0.8 copy-done.14
  209.3 2.5 shard_map.63.refs_4_
  211.8 2.3 slice_bitcast_fusion.3
  214.1 3.8 %shard_map.64.own_ref = f32[128,256]{1,0:T(8,128)} custom-call(s32[128]{0:T(128)} %shard_map.55.table_ref, bf16[128,2048]{1,0:T(8,128)(2,1)} %get-tuple-element.49.refs_0_.refs_6_, bf16[128,2048]{1,0:T(8,128)(2,1)} %get-tuple-element.48.refs_1_.refs_7_, bf16[16,128,1536]{2,1,0:T(8,128)(2,1)} %bitcast.114, bf16[16,128,1536]{2,1,0:T(8,128)(2,1)} %bitcast.115), custom_call_target="tpu_custom_call" | custom-call | flops 1 | bytes 1 | tf_op jit(solution)/shard_map/pallas_call | solution.py:472
  218.3 1.1 slice_bitcast_fusion.7
  219.5 0.7 copy-done.19
  220.1 2.9 shard_map.65
  223.0 43.9 %all-gather.7.cloned.1.call-done = bf16[2048,1792]{1,0:T(8,128)(2,1)} async-done(((bf16[128,1792]{1,0:T(8,128)(2,1)}), bf16[2048,1792]{1,0:T(8,128)(2,1)}) %all-gather.7.cloned.1.call-update) | async-done | bytes 7340048 | tf_op jit(solution)/shard_map/all_gather | solution.py:671
  266.9 9.5 %shard_map.66.own_ref = bf16[3,128,1024]{2,1,0:T(8,128)(2,1)} custom-call(s32[128]{0:T(128)} %shard_map.55.table_ref, bf16[128,2048]{1,0:T(8,128)(2,1)} %pad_maximum_fusion.3.refs_2_.refs_0_, bf16[128,2048]{1,0:T(8,128)(2,1)} %bitcast.120, bf16[128,2048]{1,0:T(8,128)(2,1)} %get-tuple-element.51.refs_2_, bf16[128,2048]{1,0:T(8,128)(2,1)} %bitcast.118, ...), custom_call_target="tpu_custom_call" | custom-call | flops 1 | bytes 1 | tf_op jit(solution)/shard_map/pallas_call | solution.py:472
  276.5 2.5 collective-permute-done.15.other_ref
  279.0 0.9 copy-done.11
  279.8 3.4 %shard_map.67 = (bf16[16,3,64,128]{3,2,1,0:T(8,128)(2,1)}, bf16[3,128,2048]{2,1,0:T(8,128)(2,1)}) custom-call(s32[1]{0:T(128)} %bitcast.id_ref, s32[128]{0:T(128)} %shard_map.55.table_ref, bf16[3,128,1024]{2,1,0:T(8,128)(2,1)} %shard_map.66.own_ref, bf16[3,128,1024]{2,1,0:T(8,128)(2,1)} %copy-done.11), custom_call_target="tpu_custom_call" | custom-call | flops 1 | bytes 1 | tf_op jit(solution)/shard_map/pallas_call | solution.py:519
  283.3 25.4 %all_to_all.15.own_ref = bf16[16,3,64,128]{3,2,1,0:T(8,128)(2,1)S(1)} all-to-all(bf16[16,3,64,128]{3,2,1,0:T(8,128)(2,1)} %get-tuple-element.26), channel_id=1, replica_groups=mesh['wide'=16,'narrow'=2] {'wide'}, dimensions={0} | all-to-all | bytes 1572864 | tf_op jit(solution)/shard_map/all_to_all | solution.py:697
  308.7 2.3 collective-permute-done.16.other_ref
  311.0 0.9 copy-done.12
  311.9 3.0 shard_map.68.turn_ref
  314.8 2.6 slice_bitcast_fusion
  317.4 4.3 %shard_map.69.own_ref = f32[128,256]{1,0:T(8,128)} custom-call(s32[128]{0:T(128)} %shard_map.55.table_ref, bf16[128,2048]{1,0:T(8,128)(2,1)} %get-tuple-element.47.refs_0_, bf16[128,2048]{1,0:T(8,128)(2,1)} %get-tuple-element.46.refs_1_, bf16[128,2048]{1,0:T(8,128)(2,1)} %get-tuple-element.45.refs_2_, bf16[16,128,1792]{2,1,0:T(8,128)(2,1)} %bitcast.109, ...), custom_call_target="tpu_custom_call" | custom-call | flops 1 | bytes 1 | tf_op jit(solution)/shard_map/pallas_call | solution.py:472
  321.9 1.1 pad_maximum_fusion.2.diag_ref
  322.9 5.8 %shard_map.71.held_ref = f32[4,128,4,1024]{3,2,1,0:T(4,128)} custom-call(s32[1]{0:T(128)} %bitcast.id_ref, f32[4,128,1024]{2,1,0:T(8,128)} %first_ref.1, bf16[1,128,2048]{2,1,0:T(8,128)(2,1)} %get-tuple-element.18.refs_0_, bf16[2,128,2048]{2,1,0:T(8,128)(2,1)} %get-tuple-element.22.refs_1_, bf16[3,128,2048]{2,1,0:T(8,128)(2,1)} %get-tuple-element.28.refs_2_, ...), custom_call_target="tpu_custom_call" | custom-call | bytes 1 | tf_op jit(solution)/shard_map/pallas_call | solution.py:594
  329.4 2.7 shard_map.70
  332.1 3.8 %shard_map.72 = f32[4,128,4,1024]{3,2,1,0:T(4,128)} custom-call(s32[1]{0:T(128)} %bitcast.id_ref, bf16[3,128,2048]{2,1,0:T(8,128)(2,1)} %shard_map.68.turn_ref, f32[128,1024]{1,0:T(8,128)} %get-tuple-element.27.diag_ref, f32[4,128,4,1024]{3,2,1,0:T(4,128)} %shard_map.71.held_ref), custom_call_target="tpu_custom_call", output_to_operand_aliasing={{}: (3, {})} | custom-call | bytes 1 | tf_op jit(solution)/shard_map/pallas_call | solution.py:611
  (91 shorter events, 7.4 us)
Async XLA Ops:
  6.5 155.5 %all-gather.5.cloned.1.call-start = ((), (), s32[]{:S(2)}) async-start(), calls=%async_computation.3 | async-start | bytes 6684672 | tf_op jit(solution)/shard_map/all_gather | solution.py:671
  12.8 0.8 copy-start.20
  13.1 4.3 %copy-start.8 = (bf16[5,128,1024]{2,1,0:T(8,128)(2,1)}, bf16[5,128,1024]{2,1,0:T(8,128)(2,1)S(1)}, u32[]{:S(2)}) copy-start(bf16[5,128,1024]{2,1,0:T(8,128)(2,1)S(1)} %fusion.1.own_ref) | copy-start | bytes 3932164
  13.1 4.3 %collective-permute-start.10 = (bf16[5,128,1024]{2,1,0:T(8,128)(2,1)S(1)}, bf16[5,128,1024]{2,1,0:T(8,128)(2,1)S(1)}, u32[]{:S(2)}, u32[]{:S(2)}) collective-permute-start(bf16[5,128,1024]{2,1,0:T(8,128)(2,1)S(1)} %fusion.1.own_ref), channel_id=1, source_target_pairs={{0,1},{1,0},{2,3},{3,2},{4,5},{5,4},{6,7},{7,6},{8,9},{9,8},{10,11... | collective-permute-start | bytes 3932168 | tf_op jit(solution)/shard_map/ppermute | solution.py:396
  17.4 4.9 %copy-start.21 = (s32[4,8]{1,0:T(4,128)S(1)}, s32[4,8]{1,0:T(4,128)}, u32[]{:S(2)}) copy-start(s32[4,8]{1,0:T(4,128)} %node_ref.1) | copy-start | bytes 388
  17.4 1.1 copy-start.9
  21.5 245.4 %all-gather.7.cloned.1.call-start = ((), (), s32[]{:S(2)}) async-start(), calls=%async_computation.4 | async-start | bytes 7798784 | tf_op jit(solution)/shard_map/all_gather | solution.py:671
  23.2 12.9 %collective-permute-start.3 = (bf16[1,128,1024]{2,1,0:T(8,128)(2,1)S(1)}, bf16[1,128,1024]{2,1,0:T(8,128)(2,1)S(1)}, u32[]{:S(2)}, u32[]{:S(2)}) collective-permute-start(bf16[1,128,1024]{2,1,0:T(8,128)(2,1)S(1)} %bitcast_multiply_fusion), channel_id=1, source_target_pairs={{0,24},{2,26},{4,28},{6,30},{8,0},{10,2},{12,4},{14,6},{16,8},{18,... | collective-permute-start | bytes 786440 | tf_op jit(solution)/shard_map/ppermute | solution.py:68
  28.2 31.1 %collective-permute-start.2 = (bf16[1,128,1024]{2,1,0:T(8,128)(2,1)S(1)}, bf16[1,128,1024]{2,1,0:T(8,128)(2,1)S(1)}, u32[]{:S(2)}, u32[]{:S(2)}) collective-permute-start(bf16[1,128,1024]{2,1,0:T(8,128)(2,1)S(1)} %bitcast_multiply_fusion), channel_id=1, source_target_pairs={{0,16},{2,18},{4,20},{6,22},{8,24},{10,26},{12,28},{14,30},{16,0},... | collective-permute-start | bytes 786440 | tf_op jit(solution)/shard_map/ppermute | solution.py:68
  28.2 31.1 %collective-permute-start.1 = (bf16[1,128,1024]{2,1,0:T(8,128)(2,1)S(1)}, bf16[1,128,1024]{2,1,0:T(8,128)(2,1)S(1)}, u32[]{:S(2)}, u32[]{:S(2)}) collective-permute-start(bf16[1,128,1024]{2,1,0:T(8,128)(2,1)S(1)} %bitcast_multiply_fusion), channel_id=1, source_target_pairs={{0,8},{2,10},{4,12},{6,14},{8,16},{10,18},{12,20},{14,22},{16,24},... | collective-permute-start | bytes 786440 | tf_op jit(solution)/shard_map/ppermute | solution.py:68
  59.3 3.1 copy-start.22
  59.4 38.9 %copy-start.1 = (bf16[4,1,128,1024]{3,2,1,0:T(8,128)(2,1)}, bf16[4,1,128,1024]{3,2,1,0:T(8,128)(2,1)S(1)}, u32[]{:S(2)}) copy-start(bf16[4,1,128,1024]{3,2,1,0:T(8,128)(2,1)S(1)} %pad_maximum_fusion.refs_3_) | copy-start | bytes 3145732
  59.5 34.0 %collective-permute-start.4 = (bf16[4,1,128,1024]{3,2,1,0:T(8,128)(2,1)S(1)}, bf16[4,1,128,1024]{3,2,1,0:T(8,128)(2,1)S(1)}, u32[]{:S(2)}, u32[]{:S(2)}) collective-permute-start(bf16[4,1,128,1024]{3,2,1,0:T(8,128)(2,1)S(1)} %pad_maximum_fusion.refs_3_), channel_id=1, source_target_pairs={{0,2},{1,5},{2,0},{3,7},{4,6},{5,1},{6,4},{7,3},{8,10},{9,13},{10,... | collective-permute-start | bytes 3145736 | tf_op jit(solution)/shard_map/ppermute | solution.py:62
  62.1 34.2 %collective-permute-start = (bf16[128,1024]{1,0:T(8,128)(2,1)S(1)}, bf16[128,1024]{1,0:T(8,128)(2,1)}, u32[]{:S(2)}, u32[]{:S(2)}) collective-permute-start(bf16[128,1024]{1,0:T(8,128)(2,1)S(1)} %fusion), channel_id=1, source_target_pairs={{0,1},{1,0},{2,3},{3,2},{4,5},{5,4},{6,7},{7,6},{8,9},{9,8},{10,11... | collective-permute-start | bytes 786440 | tf_op jit(solution)/shard_map/ppermute | solution.py:42
  63.2 35.1 %collective-permute-start.5 = (bf16[4,1,128,1024]{3,2,1,0:T(8,128)(2,1)S(1)}, bf16[4,1,128,1024]{3,2,1,0:T(8,128)(2,1)S(1)}, u32[]{:S(2)}, u32[]{:S(2)}) collective-permute-start(bf16[4,1,128,1024]{3,2,1,0:T(8,128)(2,1)S(1)} %pad_maximum_fusion.refs_3_), channel_id=1, source_target_pairs={{0,4},{1,3},{2,6},{3,1},{4,0},{5,7},{6,2},{7,5},{8,12},{9,11},{10,... | collective-permute-start | bytes 3145736 | tf_op jit(solution)/shard_map/ppermute | solution.py:62
  93.5 22.6 %copy-start.3 = (bf16[4,1,128,1024]{3,2,1,0:T(8,128)(2,1)}, bf16[4,1,128,1024]{3,2,1,0:T(8,128)(2,1)S(1)}, u32[]{:S(2)}) copy-start(bf16[4,1,128,1024]{3,2,1,0:T(8,128)(2,1)S(1)} %collective-permute-done.4.refs_4_) | copy-start | bytes 3145732
  93.5 22.5 %collective-permute-start.6 = (bf16[4,1,128,1024]{3,2,1,0:T(8,128)(2,1)S(1)}, bf16[4,1,128,1024]{3,2,1,0:T(8,128)(2,1)}, u32[]{:S(2)}, u32[]{:S(2)}) collective-permute-start(bf16[4,1,128,1024]{3,2,1,0:T(8,128)(2,1)S(1)} %collective-permute-done.4.refs_4_), channel_id=1, source_target_pairs={{0,4},{1,3},{2,6},{3,1},{4,0},{5,7},{6,2},{7,5},{8,12},{9,11},{10,... | collective-permute-start | bytes 3145736 | tf_op jit(solution)/shard_map/ppermute | solution.py:62
  98.3 17.7 %copy-start.4 = (bf16[4,1,128,1024]{3,2,1,0:T(8,128)(2,1)}, bf16[4,1,128,1024]{3,2,1,0:T(8,128)(2,1)S(1)}, u32[]{:S(2)}) copy-start(bf16[4,1,128,1024]{3,2,1,0:T(8,128)(2,1)S(1)} %collective-permute-done.5.refs_5_) | copy-start | bytes 3145732
  120.9 1.7 collective-permute-start.7
  122.6 0.7 copy-start.16
  125.4 23.7 %all-to-all-start = ((bf16[16,1,64,128]{3,2,1,0:T(8,128)(2,1)}), bf16[16,1,64,128]{3,2,1,0:T(8,128)(2,1)S(1)}, u32[]{:S(2)}, u32[]{:S(2)}) async-start(bf16[16,1,64,128]{3,2,1,0:T(8,128)(2,1)} %get-tuple-element.19), calls=%async_computation | async-start | bytes 524288 | tf_op jit(solution)/shard_map/all_to_all | solution.py:697
  149.0 1.5 copy-start.10
  149.0 1.5 collective-permute-start.8
  150.6 0.7 copy-start.17
  158.4 1.7 collective-permute-start.9
  169.5 12.5 %copy-start = (f32[4,128,1024]{2,1,0:T(8,128)S(1)}, f32[4,128,1024]{2,1,0:T(8,128)}, u32[]{:S(2)}) copy-start(f32[4,128,1024]{2,1,0:T(8,128)} %first_ref.1) | copy-start | bytes 6291460
  169.5 2.1 collective-permute-start.11
  171.6 0.8 copy-start.15
  175.2 29.2 %all-to-all-start.1 = ((bf16[16,2,64,128]{3,2,1,0:T(8,128)(2,1)}), bf16[16,2,64,128]{3,2,1,0:T(8,128)(2,1)S(1)}, u32[]{:S(2)}, u32[]{:S(2)}) async-start(bf16[16,2,64,128]{3,2,1,0:T(8,128)(2,1)} %get-tuple-element.23), calls=%async_computation.1 | async-start | bytes 1048576 | tf_op jit(solution)/shard_map/all_to_all | solution.py:697
  183.0 21.4 %collective-permute-start.18 = (f32[128,1024]{1,0:T(8,128)}, f32[128,1024]{1,0:T(8,128)S(1)}, u32[]{:S(2)}, u32[]{:S(2)}) collective-permute-start(f32[128,1024]{1,0:T(8,128)} %get-tuple-element.43), channel_id=1, source_target_pairs={{0,1},{1,0},{2,3},{3,2},{4,5},{5,4},{6,7},{7,6},{8,9},{9,8},{10,11... | collective-permute-start | bytes 1572872 | tf_op jit(solution)/shard_map/ppermute | solution.py:42
  183.0 22.2 %collective-permute-start.14 = (f32[128,1024]{1,0:T(8,128)}, f32[128,1024]{1,0:T(8,128)}, u32[]{:S(2)}, u32[]{:S(2)}) collective-permute-start(f32[128,1024]{1,0:T(8,128)} %get-tuple-element.44), channel_id=1, source_target_pairs={{0,1},{1,0},{2,3},{3,2},{4,5},{5,4},{6,7},{7,6},{8,9},{9,8},{10,11... | collective-permute-start | bytes 1572872 | tf_op jit(solution)/shard_map/ppermute | solution.py:42
  204.4 3.0 copy-start.6
  204.4 4.1 %collective-permute-start.12 = (bf16[16,2,64,128]{3,2,1,0:T(8,128)(2,1)S(1)}, bf16[16,2,64,128]{3,2,1,0:T(8,128)(2,1)S(1)}, u32[]{:S(2)}, u32[]{:S(2)}) collective-permute-start(bf16[16,2,64,128]{3,2,1,0:T(8,128)(2,1)S(1)} %all-to-all-done.1.own_ref), channel_id=1, source_target_pairs={{0,1},{1,0},{2,3},{3,2},{4,5},{5,4},{6,7},{7,6},{8,9},{9,8},{10,11... | collective-permute-start | bytes 1572872 | tf_op jit(solution)/shard_map/ppermute | solution.py:282
  204.4 0.8 copy-start.13
  208.5 0.8 copy-start.14
  214.1 4.2 %copy-start.2 = (bf16[2,128,2048]{2,1,0:T(8,128)(2,1)S(1)}, bf16[2,128,2048]{2,1,0:T(8,128)(2,1)}, u32[]{:S(2)}) copy-start(bf16[2,128,2048]{2,1,0:T(8,128)(2,1)} %get-tuple-element.22.refs_1_) | copy-start | bytes 3145732
  217.8 1.6 collective-permute-start.13
  219.5 0.7 copy-start.19
  276.5 2.5 collective-permute-start.15
  278.9 0.9 copy-start.11
  308.7 2.3 copy-start.5
  308.7 2.3 collective-permute-start.16
  311.0 0.9 copy-start.12
  317.4 4.5 %copy-start.7 = (f32[128,1024]{1,0:T(8,128)S(1)}, f32[128,1024]{1,0:T(8,128)}, u32[]{:S(2)}) copy-start(f32[128,1024]{1,0:T(8,128)} %get-tuple-element.38) | copy-start | bytes 1572868
  321.7 7.0 %collective-permute-start.17 = (f32[128,256]{1,0:T(8,128)}, f32[128,256]{1,0:T(8,128)S(1)}, u32[]{:S(2)}, u32[]{:S(2)}) collective-permute-start(f32[128,256]{1,0:T(8,128)} %shard_map.69.own_ref), channel_id=1, source_target_pairs={{0,1},{1,0},{2,3},{3,2},{4,5},{5,4},{6,7},{7,6},{8,9},{9,8},{10,11... | collective-permute-start | bytes 393224 | tf_op jit(solution)/shard_map/ppermute | solution.py:553
  328.7 0.7 copy-start.18
Sparse Core Ops, SparseCore 0:
  21.7 128.9 all-gather.4
  153.3 113.5 all-gather.6

commit v4 on v3

--- a/solution.py
+++ b/solution.py
@@ -97,7 +97,7 @@
 
 def along_both(arrays, gate):
     near = arrays[1]
-    return arrays + [swap(near if gate is None else after(near, gate), 1)]
+    return arrays + [swap(near if gate is None else after(near, *gate), 1)]
 
 
 def product_body(plan, rows_n, steps_n, finish, *refs):
@@ -399,31 +399,42 @@
     return pl.pallas_call(
         pack_body,
         in_specs=[scalar, scalar, whole, whole],
-        out_specs=(whole, whole),
+        out_specs=(whole,) * 2,
         out_shape=tuple(jax.ShapeDtypeStruct((r, sum(WIDTHS[m]) * TILE), BF) for m in (2, 3)),
         compiler_params=pltpu.CompilerParams(vmem_limit_bytes=VMEM),
         cost_estimate=pl.CostEstimate(flops=1, bytes_accessed=1, transcendentals=0),
     )(lax.axis_index("narrow").astype(jnp.int32).reshape(1), table, own, other)
 
 
-def sparse_body(level, rows_n, mirror, table_ref, *refs):
-    row_refs = [refs[q * level : (q + 1) * level] for q in range(rows_n)]
-    refs = refs[rows_n * level :]
-    piece_refs, out_ref, lhs = refs[:level], refs[level], refs[level + 1]
-    r = row_refs[0][0].shape[0]
+def sparse_body(level, shapes, mirror, table_ref, place_ref, *refs):
+    row_refs, refs = refs[: len(shapes)], refs[len(shapes) :]
+    out_ref, lhs, rest = refs[-3:]
+    piece_refs = refs[:-3]
+    r = row_refs[0].shape[-2]
     span = LT * TILE
     per = TILE // r
     q = pl.program_id(0)
 
     @pl.when(q == 0)
     def _():
-        for p in range(rows_n):
-            for j in range(level):
-                lhs[p * r : (p + 1) * r, j * span : (j + 1) * span] = row_refs[p][j][...]
+        for ref, (_, many, at) in zip(row_refs, shapes, strict=True):
+            for p in range(many):
+                row, j = at[p]
+                block = ref[p] if len(ref.shape) == 3 else ref[...]
+                lhs[row * r : (row + 1) * r, j * span : (j + 1) * span] = block
+        if level == 3:
+            each = piece_refs[0].shape[0]
+            for a in range(4):
+                for i in range(each):
+                    rest[place_ref[a * each + i]] = piece_refs[a][i]
 
     if mirror:
         q = table_ref[OWN + level - 1]
-    total = jnp.dot(lhs[:, :span], piece_refs[0][...].reshape(span, TILE), preferred_element_type=F32)
+    if level == 3:
+        block = rest[:, :, pl.ds(pl.multiple_of(q * TILE, TILE), TILE)]
+    else:
+        block = piece_refs[0][...]
+    total = jnp.dot(lhs[:, :span], block.reshape(span, TILE), preferred_element_type=F32)
     for j in range(1, level):
         for i in range(4 // j):
             if j == 1:
@@ -431,12 +442,19 @@
             else:
                 tile = table_ref[HELD + i * 4 + q]
             start = pl.multiple_of(j * span + tile * TILE, TILE)
-            block = piece_refs[j][pl.ds(tile * per, per)].reshape(TILE, TILE)
-            total += jnp.dot(lhs[:, pl.ds(start, TILE)], block, preferred_element_type=F32)
+            if level == 2:
+                block = piece_refs[1][pl.ds(tile * per, per)]
+            elif j == 1:
+                block = rest[pl.ds(tile * per, per), :, pl.ds(pl.multiple_of((4 + q % 2) * TILE, TILE), TILE)]
+            else:
+                block = rest[pl.ds(tile * per, per), :, 6 * TILE : 7 * TILE]
+            total += jnp.dot(
+                lhs[:, pl.ds(start, TILE)], block.reshape(TILE, TILE), preferred_element_type=F32
+            )
     if mirror:
         out_ref[...] = total
     else:
-        for p in range(rows_n):
+        for p in range(level):
             value = -total[p * r : (p + 1) * r]
             if p == 1:
                 value = jnp.where(table_ref[OWN] == q // 2, value, 0.0)
@@ -445,43 +463,51 @@
             out_ref[p] = value.astype(BF)
 
 
-def sparse_product(level, table, rows, panel, mirror):
-    wide, r, _ = panel.shape
-    rows_n = len(rows)
+def sparse_product(level, table, place, rows, panel, rest, mirror):
+    wide = lax.axis_size("wide")
+    r = rows[0][0].shape[-2]
+    rows_n = 1 if mirror else level
 
     def column(j):
         def index(i, t):
             q = t[OWN + level - 1] if mirror else i
-            if j == 0:
-                return (0, 0, q)
-            if j == 1:
-                return (0, 0, 4 + q % 2)
-            return (0, 0, 6)
+            return (0, 0, q if j == 0 else 4 + q % 2)
 
         return index
 
     whole = pl.BlockSpec(memory_space=pltpu.VMEM)
-    flat = [x for row in rows for x in row]
-    specs = [whole] * len(flat) + [pl.BlockSpec((wide, r, TILE), column(j)) for j in range(level)]
+    flat = [array for array, _ in rows]
+    shapes = tuple((0, len(at), at) for _, at in rows)
+    specs = [pl.BlockSpec(memory_space=pltpu.SMEM)] + [whole] * len(flat)
+    operands = [table, place] + flat
+    for j in range(0 if level == 3 else 2):
+        specs.append(pl.BlockSpec((wide, r, TILE), column(j)))
+        operands.append(panel)
+    specs += [whole] * len(rest)
+    operands += rest
     if mirror:
         shape = jax.ShapeDtypeStruct((r, TILE), F32)
         out_spec = pl.BlockSpec((r, TILE), lambda i, t: (0, 0))
     else:
         shape = jax.ShapeDtypeStruct((rows_n, r, 4 * TILE), BF)
         out_spec = pl.BlockSpec((rows_n, r, TILE), lambda i, t: (0, 0, i))
-    return pl.pallas_call(
-        functools.partial(sparse_body, level, rows_n, mirror),
+    spare = (wide, r, 7 * TILE) if level == 3 else (1, 16, 128)
+    return pl.pallas_call(
+        functools.partial(sparse_body, level, shapes, mirror),
         grid_spec=pltpu.PrefetchScalarGridSpec(
             num_scalar_prefetch=1,
             grid=(1 if mirror else 4,),
             in_specs=specs,
             out_specs=out_spec,
-            scratch_shapes=[pltpu.VMEM((rows_n * r, level * LT * TILE), BF)],
+            scratch_shapes=[
+                pltpu.VMEM((rows_n * r, level * LT * TILE), BF),
+                pltpu.VMEM(spare, BF),
+            ],
         ),
         out_shape=shape,
         compiler_params=pltpu.CompilerParams(vmem_limit_bytes=VMEM),
         cost_estimate=pl.CostEstimate(flops=1, bytes_accessed=1, transcendentals=0),
-    )(table, *flat, *[panel] * level)
+    )(*operands)
 
 
 def place_body(level, levels, id_ref, table_ref, own_ref, other_ref, slots_ref, full_ref):
@@ -601,7 +627,7 @@
         ),
         out_shape=shape,
         compiler_params=pltpu.CompilerParams(vmem_limit_bytes=VMEM),
-        cost_estimate=pl.CostEstimate(flops=0, bytes_accessed=1, transcendentals=0),
+        cost_estimate=pl.CostEstimate(flops=0, bytes_accessed=40 * 2**20, transcendentals=0),
     )(lax.axis_index("narrow").astype(jnp.int32).reshape(1), diag_inverse, *news, *turns, *diags)
 
 
@@ -668,45 +694,65 @@
     if compact:
         table = make_table(parent, tile_node, structure, row_pos)
         shards = packed(factor, table)
-        panels = {m: lax.all_gather(shards[m - 2], "wide", axis=0) for m in (2, 3)}
+        panels = {2: lax.all_gather(shards[0], "wide", axis=0), 3: None}
         wide_diag = {m: narrow_all(diag_inverse[m], 1) for m in (2, 3)}
     else:
         panels = {m: lax.all_gather(panel_of(m), "wide", axis=0) for m in (2, 3)}
-    one = along_both(along_xy(first, None), None)
-
-    rows = {0: [narrow_all(diag_inverse[0].astype(BF), 1)]}
+    one = along_xy(first, None)
+    if compact:
+        third = along_z(after(shards[1], one[0]), None)
+    one = along_both(one, (one[2],) + tuple(third) if compact else None)
+
+    held = {}
+    rows = {0: [(narrow_all(diag_inverse[0].astype(BF), 1), ((0, 0),))]}
     news, turns, diags = [], [], []
+    rest = []
     for level in range(1, LEV):
-        known = [rows[k] for k in range(level)]
         packed_here = compact and level > 1
         if packed_here:
-            value = sparse_product(level, table, known, panels[level], False)
+            known = [part for k in range(level) for part in rows[k]] + [held[m] for m in range(1, level)]
+            if level == 2:
+                rest = along_xy(third, panels[2])
+            value = sparse_product(level, table, place, known, panels[level], rest if level == 3 else [], False)
             slots, full = place_slots(level, table, value)
         else:
             if level == 1:
                 groups = [((0,), place, one)]
+                known = [[rows[0][0][0]]]
             else:
                 groups = [(tuple(range(level)), whole_place, [panels[level]])]
+                known = []
+                for k in range(level):
+                    by_level = {}
+                    for array, at in rows[k] + [held[m] for m in range(1, level)]:
+                        for p, (row, j) in enumerate(at):
+                            if row == k:
+                                by_level[j] = array[p] if array.ndim == 3 else array
+                    known.append([by_level[j] for j in range(level)])
             value = product(known, groups, above[:level, level])
             slots, full = make_slots(value)
         news.append(full)
-        for k in range(level):
-            rows[k].append(full[k])
+        held[level] = (full, tuple((k, level) for k in range(level)))
         if level == LEV - 1:
             out = upper_rows(diag_inverse, news, turns, diags)
         got = lax.all_to_all(slots, "wide", split_axis=0, concat_axis=0, tiled=True)
+        if packed_here and level == 2:
+            rest = along_both(rest, (slots,))
+            got = after(got, rest[1], rest[2])
         turn = mirrored(got, full)
         turns.append(turn)
-        rows[level] = [turn[k] for k in range(level)]
+        rows[level] = [(turn, tuple((level, j) for j in range(level)))]
         if packed_here:
-            inner = sparse_product(level, table, [rows[level]], panels[level], True)
+            here = [(turn, tuple((0, j) for j in range(level)))]
+            inner = sparse_product(level, table, place, here, panels[level], rest if level == 3 else [], True)
             done, whole_low = diag_block(level, table, inner, wide_diag[level], row_pos)
         else:
-            done, low = product([rows[level]], groups, same[level : level + 1], (diag_inverse, level))
+            known = [[turn[k] for k in range(level)]]
+            done, low = product(known, groups, same[level : level + 1], (diag_inverse, level))
             whole_low = narrow_all(low, 1) if level < LEV - 1 else None
         diags.append(done)
         if level < LEV - 1:
-            rows[level].append(whole_low)
+            rows[level].append((whole_low, ((level, level),)))
     return lower_rows(turns[-1], diags[-1], out)
 
 

time: 344 us -> 327 us (0.951)
  waiting for transfers between devices: 166 us -> 140 us
  starting transfers between devices: 29.7 us -> 40.2 us
  local copies, waits for them, and re-layouts: 24 us -> 18.9 us
    all_gather x2 -> x1, waiting for transfers between devices: 43.9 us -> 0.01 us  [local(): panels = {2: lax.all_gather(shards[0], 'wide', axis=0), 3: None}]
    ppermute x3 -> x6, waiting for transfers between devices: 30 us -> 46.9 us  [shifts(): lax.ppermute(value, 'wide', [(i, (i + 4 * hop) % wide) for i in range(wid...]
    ppermute x3 -> x6, waiting for transfers between devices: 46.4 us -> 61.7 us  [swap(): return lax.ppermute(value, ('wide', 'narrow'), pairs)]
    all_to_all x2, waiting for transfers between devices: 34.2 us -> 22.2 us  [local(): got = lax.all_to_all(slots, 'wide', split_axis=0, concat_axis=0, tiled=True)]
    squeeze x3 -> x0, local copies, waits for them, and re-layouts: 5.94 us -> none  [the longest x2 4.86 us: local(): rows[level] = [turn[k] for k in range(level)]]
    ppermute x3 -> x6, starting transfers between devices: 6.02 us -> 11.6 us  [shifts(): lax.ppermute(value, 'wide', [(i, (i + 4 * hop) % wide) for i in range(wid...]
  transfers between devices with their start and end apart: 23 -> 28, of which waited for: 14 -> 15; matrix products, arithmetic and copies ran while one was open for 6% -> 5% of each run, Pallas kernels for 12% -> 13%
where the time goes in v4:
time: 327 us; the launch traced here: 325 us
  waiting for transfers between devices  140 us (43%)
  Pallas kernels  73.4 us (22%)
  starting transfers between devices  40.2 us (12%)
  blocking collectives  25.6 us (8%)
  local copies, waits for them, and re-layouts  18.9 us (6%)
  between operations  13.7 us (4%)
  other arithmetic  11.4 us (3%)
    ppermute x6, waiting for transfers between devices, swap(): return lax.ppermute(value, ('wide', 'narrow'), pairs)  61.7 us
    ppermute x6, waiting for transfers between devices, shifts(): lax.ppermute(value, 'wide', [(i, (i + 4 * hop) % wide) for i in range(wid...  46.9 us
    pallas_call x4, Pallas kernels, sparse_product(): pl.pallas_call(functools.partial(sparse_body, level, shapes, mirror), gri...  27.3 us
    all_to_all x1, blocking collectives, local(): got = lax.all_to_all(slots, 'wide', split_axis=0, concat_axis=0, tiled=True)  25.6 us
    all_to_all x2, waiting for transfers between devices, local(): got = lax.all_to_all(slots, 'wide', split_axis=0, concat_axis=0, tiled=True)  22.2 us
    all_to_all x2, starting transfers between devices, local(): got = lax.all_to_all(slots, 'wide', split_axis=0, concat_axis=0, tiled=True)  18.8 us
    ppermute x6, starting transfers between devices, shifts(): lax.ppermute(value, 'wide', [(i, (i + 4 * hop) % wide) for i in range(wid...  11.6 us
    pallas_call x2, Pallas kernels, product(): pl.pallas_call(functools.partial(product_body, plan, rows_n, steps_n, dia...  9.98 us
  transfers between devices with their start and end apart: 28, of which 15 were waited for; matrix products, arithmetic and copies ran while one was open for 5% of the time, Pallas kernels for 13%

profile of v4, /device:TPU:0, one launch (start us, length us, event | category | flops | bytes accessed | tf_op | source)
XLA Modules:
  0.0 325.3 jit_solution(11859659457433908515)
XLA Ops:
  6.5 6.1 %fusion.30 = (bf16[1,128,1,1024]{3,2,1,0:T(2,128)(2,1)S(1)}, bf16[1,128,1,1024]{3,2,1,0:T(2,128)(2,1)S(1)}, bf16[1,128,1,1024]{3,2,1,0:T(2,128)(2,1)S(1)}, bf16[...) fusion(bf16[4,128,4,1024]{3,2,1,0:T(4,128)(2,1)} %param.5), kind=kLoop, calls=%fused_computation.71 | loop fusion | bytes 3145728 | tf_op jit(solution)/shard_map/slice | solution.py:395
  13.7 0.7 copy.7.structure_ref
  15.0 2.4 shard_map.55.table_ref
  17.4 1.1 copy-done.7
  18.5 3.0 shard_map.56
  22.4 4.9 %collective-permute-start.3 = (bf16[1,128,1024]{2,1,0:T(8,128)(2,1)S(1)}, bf16[1,128,1024]{2,1,0:T(8,128)(2,1)S(1)}, u32[]{:S(2)}, u32[]{:S(2)}) collective-permute-start(bf16[1,128,1024]{2,1,0:T(8,128)(2,1)S(1)} %bitcast_multiply_fusion), channel_id=1, source_target_pairs={{0,24},{2,26},{4,28},{6,30},{8,0},{10,2},{12,4},{14,6},{16,8},{18,... | collective-permute-start | bytes 786440 | tf_op jit(solution)/shard_map/ppermute | solution.py:68
  27.3 1.0 collective-permute-start.1
  28.4 6.0 %collective-permute-done.3 = bf16[1,128,1024]{2,1,0:T(8,128)(2,1)S(1)} collective-permute-done((bf16[1,128,1024]{2,1,0:T(8,128)(2,1)S(1)}, bf16[1,128,1024]{2,1,0:T(8,128)(2,1)S(1)}, u32[]{:S(2)}, u32[]{:S(2)}) %collective-permute-start.3) | collective-permute-done | bytes 262176 | tf_op jit(solution)/shard_map/ppermute | solution.py:68
  34.4 24.1 %collective-permute-done.2 = bf16[1,128,1024]{2,1,0:T(8,128)(2,1)S(1)} collective-permute-done((bf16[1,128,1024]{2,1,0:T(8,128)(2,1)S(1)}, bf16[1,128,1024]{2,1,0:T(8,128)(2,1)S(1)}, u32[]{:S(2)}, u32[]{:S(2)}) %collective-permute-start.2) | collective-permute-done | bytes 262176 | tf_op jit(solution)/shard_map/ppermute | solution.py:68
  58.7 1.6 collective-permute-start.4
  60.2 1.5 collective-permute-start.5
  62.5 0.8 collective-permute-start.7
  63.3 1.9 collective-permute-start.8
  65.3 2.9 collective-permute-start.9
  68.5 1.1 fusion
  69.6 25.7 %collective-permute-done.4.refs_4_ = bf16[4,1,128,1024]{3,2,1,0:T(8,128)(2,1)S(1)} collective-permute-done((bf16[4,1,128,1024]{3,2,1,0:T(8,128)(2,1)S(1)}, bf16[4,1,128,1024]{3,2,1,0:T(8,128)(2,1)S(1)}, u32[]{:S(2)}, u32[]{:S(2)}) %collective-permute-start.4) | collective-permute-done | bytes 1048608 | tf_op jit(solution)/shard_map/ppermute | solution.py:62
  95.3 16.7 %collective-permute-done.8 = bf16[128,1792]{1,0:T(8,128)(2,1)S(1)} collective-permute-done((bf16[128,1792]{1,0:T(8,128)(2,1)}, bf16[128,1792]{1,0:T(8,128)(2,1)S(1)}, u32[]{:S(2)}, u32[]{:S(2)}) %collective-permute-start.8) | collective-permute-done | bytes 458784 | tf_op jit(solution)/shard_map/ppermute | solution.py:68
  112.1 0.8 copy-done.14
  115.0 1.2 broadcast_select_fusion.7
  116.1 0.8 pad_maximum_fusion.4.refs_2_.refs_0_
  117.0 27.1 %collective-permute-done.10.refs_6_ = bf16[4,1,128,1024]{3,2,1,0:T(8,128)(2,1)} collective-permute-done((bf16[4,1,128,1024]{3,2,1,0:T(8,128)(2,1)S(1)}, bf16[4,1,128,1024]{3,2,1,0:T(8,128)(2,1)}, u32[]{:S(2)}, u32[]{:S(2)}) %collective-permute-start.10) | collective-permute-done | bytes 1048608 | tf_op jit(solution)/shard_map/ppermute | solution.py:62
  144.1 4.8 %shard_map.57.own_ref = bf16[1,128,1024]{2,1,0:T(8,128)(2,1)} custom-call(s32[1,16]{1,0:T(1,128)} %add.69.refs_0_, s32[1,4]{1,0:T(1,128)} %fusion.25.refs_1_, bf16[128,2048]{1,0:T(8,128)(2,1)} %pad_maximum_fusion.4.refs_2_.refs_0_, bf16[4,1,128,1024]{3,2,1,0:T(8,128)(2,1)} %copy-done.1, bf16[4,1,128,1024]{3,2,1,0:T(8,128)(2,1)} %copy-done.2, ...), custom_call_target="tpu_custom_call" | custom-call | flops 1 | bytes 1 | tf_op jit(solution)/shard_map/pallas_call | solution.py:209
  148.9 1.7 collective-permute-done.11.other_ref
  150.7 0.7 copy-done.16
  151.4 2.0 shard_map.58
  153.4 14.9 %all-to-all-start = ((bf16[16,1,64,128]{3,2,1,0:T(8,128)(2,1)}), bf16[16,1,64,128]{3,2,1,0:T(8,128)(2,1)S(1)}, u32[]{:S(2)}, u32[]{:S(2)}) async-start(bf16[16,1,64,128]{3,2,1,0:T(8,128)(2,1)} %get-tuple-element.29), calls=%async_computation | async-start | bytes 524288 | tf_op jit(solution)/shard_map/all_to_all | solution.py:738
  168.4 10.0 %all-to-all-done.own_ref = bf16[16,1,64,128]{3,2,1,0:T(8,128)(2,1)S(1)} async-done(((bf16[16,1,64,128]{3,2,1,0:T(8,128)(2,1)}), bf16[16,1,64,128]{3,2,1,0:T(8,128)(2,1)S(1)}, u32[]{:S(2)}, u32[]{:S(2)}) %all-to-all-start) | async-done | bytes 262176 | tf_op jit(solution)/shard_map/all_to_all | solution.py:738
  178.4 3.0 pad_maximum_fusion.refs_7_.refs_1_
  181.4 0.8 collective-permute-start.15
  183.4 2.0 shard_map.59.refs_1_.refs_3_
  185.4 5.2 %shard_map.60 = (f32[128,1024]{1,0:T(8,128)}, bf16[128,1024]{1,0:T(8,128)(2,1)}) custom-call(s32[1,16]{1,0:T(1,128)} %add.69.refs_0_, s32[1,4]{1,0:T(1,128)} %slice_convert_fusion.1.refs_1_, bf16[128,2048]{1,0:T(8,128)(2,1)} %bitcast.98, bf16[4,1,128,1024]{3,2,1,0:T(8,128)(2,1)} %copy-done.1, bf16[4,1,128,1024]{3,2,1,0:T(8,128)(2,1)} %copy-done.2, ...), custom_call_target="tpu_custom_call" | custom-call | flops 1 | bytes 1 | tf_op jit(solution)/shard_map/pallas_call | solution.py:209
  191.5 1.1 collective-permute-start.16
  192.6 1.0 broadcast_select_fusion.5
  193.6 0.8 pad_maximum_fusion.5.refs_2_
  194.4 7.4 %shard_map.61.own_ref = bf16[2,128,1024]{2,1,0:T(8,128)(2,1)} custom-call(s32[128]{0:T(128)} %shard_map.55.table_ref, s32[16]{0:T(128)} %add.68.place_ref, bf16[128,2048]{1,0:T(8,128)(2,1)} %pad_maximum_fusion.4.refs_2_.refs_0_, bf16[1,128,2048]{2,1,0:T(8,128)(2,1)} %shard_map.59.refs_1_.refs_3_, bf16[128,2048]{1,0:T(8,128)(2,1)} %pad_maximum_fusion.5.refs_2_, ...), custom_call_target="tpu_custom_call" | custom-call | flops 1 | bytes 1 | tf_op jit(solution)/shard_map/pallas_call | solution.py:495
  201.9 2.0 collective-permute-done.14.other_ref
  203.9 0.8 copy-done.12
  204.7 2.8 shard_map.62
  207.6 4.0 %all-to-all-start.1 = ((bf16[16,2,64,128]{3,2,1,0:T(8,128)(2,1)}), bf16[16,2,64,128]{3,2,1,0:T(8,128)(2,1)S(1)}, u32[]{:S(2)}, u32[]{:S(2)}) async-start(bf16[16,2,64,128]{3,2,1,0:T(8,128)(2,1)} %get-tuple-element.33), calls=%async_computation.1 | async-start | bytes 1048576 | tf_op jit(solution)/shard_map/all_to_all | solution.py:738
  211.5 3.7 %collective-permute-done.15.refs_8_.refs_2_ = bf16[4,128,1792]{2,1,0:T(8,128)(2,1)} collective-permute-done((bf16[4,128,1792]{2,1,0:T(8,128)(2,1)}, bf16[4,128,1792]{2,1,0:T(8,128)(2,1)}, u32[]{:S(2)}, u32[]{:S(2)}) %collective-permute-start.15) | collective-permute-done | bytes 1835040 | tf_op jit(solution)/shard_map/ppermute | solution.py:62
  215.2 0.9 collective-permute-start.20
  216.2 0.9 slice_bitcast_fusion
  217.1 12.2 %all-to-all-done.1.own_ref = bf16[16,2,64,128]{3,2,1,0:T(8,128)(2,1)S(1)} async-done(((bf16[16,2,64,128]{3,2,1,0:T(8,128)(2,1)}), bf16[16,2,64,128]{3,2,1,0:T(8,128)(2,1)S(1)}, u32[]{:S(2)}, u32[]{:S(2)}) %all-to-all-start.1) | async-done | bytes 524320 | tf_op jit(solution)/shard_map/all_to_all | solution.py:738
  229.3 1.1 collective-permute-start.17
  230.9 1.1 collective-permute-done.17.other_ref
  232.0 0.8 copy-done.11
  232.8 2.5 shard_map.63.refs_0_.refs_3_.refs_4_
  235.5 3.6 %shard_map.64.own_ref = f32[128,256]{1,0:T(8,128)} custom-call(s32[128]{0:T(128)} %shard_map.55.table_ref, s32[16]{0:T(128)} %add.68.place_ref, bf16[2,128,2048]{2,1,0:T(8,128)(2,1)} %shard_map.63.refs_0_.refs_3_.refs_4_, bf16[16,128,1536]{2,1,0:T(8,128)(2,1)} %bitcast.96, bf16[16,128,1536]{2,1,0:T(8,128)(2,1)} %bitcast.97), custom_call_target="tpu_custom_call" | custom-call | flops 1 | bytes 1 | tf_op jit(solution)/shard_map/pallas_call | solution.py:495
  239.5 1.1 pad_maximum_fusion.2.diag_ref
  241.4 2.8 shard_map.65
  244.2 5.2 %collective-permute-done.20.refs_10_.refs_4_ = bf16[4,128,1792]{2,1,0:T(8,128)(2,1)} collective-permute-done((bf16[4,128,1792]{2,1,0:T(8,128)(2,1)}, bf16[4,128,1792]{2,1,0:T(8,128)(2,1)}, u32[]{:S(2)}, u32[]{:S(2)}) %collective-permute-start.20) | collective-permute-done | bytes 1835040 | tf_op jit(solution)/shard_map/ppermute | solution.py:62
  249.4 10.5 %shard_map.66.own_ref = bf16[3,128,1024]{2,1,0:T(8,128)(2,1)} custom-call(s32[128]{0:T(128)} %shard_map.55.table_ref, s32[16]{0:T(128)} %add.68.place_ref, bf16[128,2048]{1,0:T(8,128)(2,1)} %pad_maximum_fusion.4.refs_2_.refs_0_, bf16[1,128,2048]{2,1,0:T(8,128)(2,1)} %shard_map.59.refs_1_.refs_3_, bf16[128,2048]{1,0:T(8,128)(2,1)} %pad_maximum_fusion.5.refs_2_, ...), custom_call_target="tpu_custom_call" | custom-call | flops 1 | bytes 1 | tf_op jit(solution)/shard_map/pallas_call | solution.py:495
  260.2 2.1 collective-permute-done.21.other_ref
  262.4 0.9 copy-done.9
  263.2 3.3 %shard_map.67 = (bf16[16,3,64,128]{3,2,1,0:T(8,128)(2,1)}, bf16[3,128,2048]{2,1,0:T(8,128)(2,1)}) custom-call(s32[1]{0:T(128)} %bitcast.id_ref, s32[128]{0:T(128)} %shard_map.55.table_ref, bf16[3,128,1024]{2,1,0:T(8,128)(2,1)} %shard_map.66.own_ref, bf16[3,128,1024]{2,1,0:T(8,128)(2,1)} %copy-done.9), custom_call_target="tpu_custom_call" | custom-call | flops 1 | bytes 1 | tf_op jit(solution)/shard_map/pallas_call | solution.py:545
  266.5 25.6 %all_to_all.15.own_ref = bf16[16,3,64,128]{3,2,1,0:T(8,128)(2,1)S(1)} all-to-all(bf16[16,3,64,128]{3,2,1,0:T(8,128)(2,1)} %get-tuple-element.42), channel_id=1, replica_groups=mesh['wide'=16,'narrow'=2] {'wide'}, dimensions={0} | all-to-all | bytes 1572864 | tf_op jit(solution)/shard_map/all_to_all | solution.py:738
  292.2 2.3 collective-permute-done.22.other_ref
  294.5 0.9 copy-done.10
  295.4 3.0 shard_map.68.refs_0_.turn_ref
  298.4 5.9 %shard_map.69.own_ref = f32[128,256]{1,0:T(8,128)} custom-call(s32[128]{0:T(128)} %shard_map.55.table_ref, s32[16]{0:T(128)} %add.68.place_ref, bf16[3,128,2048]{2,1,0:T(8,128)(2,1)} %shard_map.68.refs_0_.turn_ref, bf16[4,128,1792]{2,1,0:T(8,128)(2,1)} %pad_maximum_fusion.refs_7_.refs_1_, bf16[4,128,1792]{2,1,0:T(8,128)(2,1)} %collective-permute-done.15.refs_8_.refs_2_, ...), custom_call_target="tpu_custom_call" | custom-call | flops 1 | bytes 1 | tf_op jit(solution)/shard_map/pallas_call | solution.py:495
  304.4 1.1 pad_maximum_fusion.3.diag_ref
  305.5 5.8 %shard_map.71.held_ref = f32[4,128,4,1024]{3,2,1,0:T(4,128)} custom-call(s32[1]{0:T(128)} %bitcast.id_ref, f32[4,128,1024]{2,1,0:T(8,128)} %first_ref.1, bf16[1,128,2048]{2,1,0:T(8,128)(2,1)} %get-tuple-element.31.refs_3_.refs_5_.refs_0_, bf16[2,128,2048]{2,1,0:T(8,128)(2,1)} %get-tuple-element.40.refs_6_.refs_1_, ...), custom_call_target="tpu_custom_call" | custom-call | bytes 41943040 | tf_op jit(solution)/shard_map/pallas_call | solution.py:620
  312.0 2.6 shard_map.70
  314.6 3.8 %shard_map.72 = f32[4,128,4,1024]{3,2,1,0:T(4,128)} custom-call(s32[1]{0:T(128)} %bitcast.id_ref, bf16[3,128,2048]{2,1,0:T(8,128)(2,1)} %shard_map.68.refs_0_.turn_ref, f32[128,1024]{1,0:T(8,128)} %get-tuple-element.43.diag_ref, f32[4,128,4,1024]{3,2,1,0:T(4,128)} %shard_map.71.held_ref), custom_call_target="tpu_custom_call", output_to_operand_aliasing={{}: (3, {})} | custom-call | bytes 1 | tf_op jit(solution)/shard_map/pallas_call | solution.py:637
  (99 shorter events, 11.2 us)
Async XLA Ops:
  6.5 171.9 %all-gather.3.cloned.1.call-start = ((), (), s32[]{:S(2)}) async-start(), calls=%async_computation.3 | async-start | bytes 6684672 | tf_op jit(solution)/shard_map/all_gather | solution.py:697
  12.7 1.0 copy-start.20
  13.0 8.5 %copy-start.21 = (s32[4,8]{1,0:T(4,128)S(1)}, s32[4,8]{1,0:T(4,128)}, u32[]{:S(2)}) copy-start(s32[4,8]{1,0:T(4,128)} %node_ref.1) | copy-start | bytes 388
  13.1 4.3 %copy-start.6 = (bf16[5,128,1024]{2,1,0:T(8,128)(2,1)}, bf16[5,128,1024]{2,1,0:T(8,128)(2,1)S(1)}, u32[]{:S(2)}) copy-start(bf16[5,128,1024]{2,1,0:T(8,128)(2,1)S(1)} %fusion.1.own_ref) | copy-start | bytes 3932164
  13.1 4.2 %collective-permute-start.6 = (bf16[5,128,1024]{2,1,0:T(8,128)(2,1)S(1)}, bf16[5,128,1024]{2,1,0:T(8,128)(2,1)S(1)}, u32[]{:S(2)}, u32[]{:S(2)}) collective-permute-start(bf16[5,128,1024]{2,1,0:T(8,128)(2,1)S(1)} %fusion.1.own_ref), channel_id=1, source_target_pairs={{0,1},{1,0},{2,3},{3,2},{4,5},{5,4},{6,7},{7,6},{8,9},{9,8},{10,11... | collective-permute-start | bytes 3932168 | tf_op jit(solution)/shard_map/ppermute | solution.py:396
  17.4 1.1 copy-start.7
  22.3 39.7 %copy-start.22 = (s32[15]{0:T(128)S(1)}, s32[15]{0:T(128)}, u32[]{:S(2)}) copy-start(s32[15]{0:T(128)} %parent_ref.1) | copy-start | bytes 184
  22.4 12.0 %collective-permute-start.3 = (bf16[1,128,1024]{2,1,0:T(8,128)(2,1)S(1)}, bf16[1,128,1024]{2,1,0:T(8,128)(2,1)S(1)}, u32[]{:S(2)}, u32[]{:S(2)}) collective-permute-start(bf16[1,128,1024]{2,1,0:T(8,128)(2,1)S(1)} %bitcast_multiply_fusion), channel_id=1, source_target_pairs={{0,24},{2,26},{4,28},{6,30},{8,0},{10,2},{12,4},{14,6},{16,8},{18,... | collective-permute-start | bytes 786440 | tf_op jit(solution)/shard_map/ppermute | solution.py:68
  27.3 31.2 %collective-permute-start.2 = (bf16[1,128,1024]{2,1,0:T(8,128)(2,1)S(1)}, bf16[1,128,1024]{2,1,0:T(8,128)(2,1)S(1)}, u32[]{:S(2)}, u32[]{:S(2)}) collective-permute-start(bf16[1,128,1024]{2,1,0:T(8,128)(2,1)S(1)} %bitcast_multiply_fusion), channel_id=1, source_target_pairs={{0,16},{2,18},{4,20},{6,22},{8,24},{10,26},{12,28},{14,30},{16,0},... | collective-permute-start | bytes 786440 | tf_op jit(solution)/shard_map/ppermute | solution.py:68
  27.3 31.2 %collective-permute-start.1 = (bf16[1,128,1024]{2,1,0:T(8,128)(2,1)S(1)}, bf16[1,128,1024]{2,1,0:T(8,128)(2,1)S(1)}, u32[]{:S(2)}, u32[]{:S(2)}) collective-permute-start(bf16[1,128,1024]{2,1,0:T(8,128)(2,1)S(1)} %bitcast_multiply_fusion), channel_id=1, source_target_pairs={{0,8},{2,10},{4,12},{6,14},{8,16},{10,18},{12,20},{14,22},{16,24},... | collective-permute-start | bytes 786440 | tf_op jit(solution)/shard_map/ppermute | solution.py:68
  58.7 85.4 %copy-start.1 = (bf16[4,1,128,1024]{3,2,1,0:T(8,128)(2,1)}, bf16[4,1,128,1024]{3,2,1,0:T(8,128)(2,1)S(1)}, u32[]{:S(2)}) copy-start(bf16[4,1,128,1024]{3,2,1,0:T(8,128)(2,1)S(1)} %pad_maximum_fusion.1.refs_3_) | copy-start | bytes 3145732
  58.7 36.6 %collective-permute-start.4 = (bf16[4,1,128,1024]{3,2,1,0:T(8,128)(2,1)S(1)}, bf16[4,1,128,1024]{3,2,1,0:T(8,128)(2,1)S(1)}, u32[]{:S(2)}, u32[]{:S(2)}) collective-permute-start(bf16[4,1,128,1024]{3,2,1,0:T(8,128)(2,1)S(1)} %pad_maximum_fusion.1.refs_3_), channel_id=1, source_target_pairs={{0,2},{1,5},{2,0},{3,7},{4,6},{5,1},{6,4},{7,3},{8,10},{9,13},{10,... | collective-permute-start | bytes 3145736 | tf_op jit(solution)/shard_map/ppermute | solution.py:62
  60.2 35.1 %collective-permute-start.5 = (bf16[4,1,128,1024]{3,2,1,0:T(8,128)(2,1)S(1)}, bf16[4,1,128,1024]{3,2,1,0:T(8,128)(2,1)S(1)}, u32[]{:S(2)}, u32[]{:S(2)}) collective-permute-start(bf16[4,1,128,1024]{3,2,1,0:T(8,128)(2,1)S(1)} %pad_maximum_fusion.1.refs_3_), channel_id=1, source_target_pairs={{0,4},{1,3},{2,6},{3,1},{4,0},{5,7},{6,2},{7,5},{8,12},{9,11},{10,... | collective-permute-start | bytes 3145736 | tf_op jit(solution)/shard_map/ppermute | solution.py:62
  62.5 32.8 %collective-permute-start.7 = (bf16[128,1792]{1,0:T(8,128)(2,1)}, bf16[128,1792]{1,0:T(8,128)(2,1)S(1)}, u32[]{:S(2)}, u32[]{:S(2)}) collective-permute-start(bf16[128,1792]{1,0:T(8,128)(2,1)} %get-tuple-element.34), channel_id=1, source_target_pairs={{0,8},{2,10},{4,12},{6,14},{8,16},{10,18},{12,20},{14,22},{16,24},... | collective-permute-start | bytes 1376264 | tf_op jit(solution)/shard_map/ppermute | solution.py:68
  63.3 48.8 %collective-permute-start.8 = (bf16[128,1792]{1,0:T(8,128)(2,1)}, bf16[128,1792]{1,0:T(8,128)(2,1)S(1)}, u32[]{:S(2)}, u32[]{:S(2)}) collective-permute-start(bf16[128,1792]{1,0:T(8,128)(2,1)} %get-tuple-element.34), channel_id=1, source_target_pairs={{0,16},{2,18},{4,20},{6,22},{8,24},{10,26},{12,28},{14,30},{16,0},... | collective-permute-start | bytes 1376264 | tf_op jit(solution)/shard_map/ppermute | solution.py:68
  65.3 46.8 %collective-permute-start.9 = (bf16[128,1792]{1,0:T(8,128)(2,1)}, bf16[128,1792]{1,0:T(8,128)(2,1)S(1)}, u32[]{:S(2)}, u32[]{:S(2)}) collective-permute-start(bf16[128,1792]{1,0:T(8,128)(2,1)} %get-tuple-element.34), channel_id=1, source_target_pairs={{0,24},{2,26},{4,28},{6,30},{8,0},{10,2},{12,4},{14,6},{16,8},{18,... | collective-permute-start | bytes 1376264 | tf_op jit(solution)/shard_map/ppermute | solution.py:68
  95.3 48.8 %copy-start.2 = (bf16[4,1,128,1024]{3,2,1,0:T(8,128)(2,1)}, bf16[4,1,128,1024]{3,2,1,0:T(8,128)(2,1)S(1)}, u32[]{:S(2)}) copy-start(bf16[4,1,128,1024]{3,2,1,0:T(8,128)(2,1)S(1)} %collective-permute-done.4.refs_4_) | copy-start | bytes 3145732
  95.3 19.7 %collective-permute-start = (bf16[128,1024]{1,0:T(8,128)(2,1)S(1)}, bf16[128,1024]{1,0:T(8,128)(2,1)}, u32[]{:S(2)}, u32[]{:S(2)}) collective-permute-start(bf16[128,1024]{1,0:T(8,128)(2,1)S(1)} %fusion), channel_id=1, source_target_pairs={{0,1},{1,0},{2,3},{3,2},{4,5},{5,4},{6,7},{7,6},{8,9},{9,8},{10,11... | collective-permute-start | bytes 786440 | tf_op jit(solution)/shard_map/ppermute | solution.py:42
  95.3 48.8 %copy-start.3 = (bf16[4,1,128,1024]{3,2,1,0:T(8,128)(2,1)}, bf16[4,1,128,1024]{3,2,1,0:T(8,128)(2,1)S(1)}, u32[]{:S(2)}) copy-start(bf16[4,1,128,1024]{3,2,1,0:T(8,128)(2,1)S(1)} %collective-permute-done.5.refs_5_) | copy-start | bytes 3145732
  95.3 16.8 %copy-start.13 = (bf16[128,1792]{1,0:T(8,128)(2,1)}, bf16[128,1792]{1,0:T(8,128)(2,1)S(1)}, u32[]{:S(2)}) copy-start(bf16[128,1792]{1,0:T(8,128)(2,1)S(1)} %collective-permute-done.7) | copy-start | bytes 1376260
  112.1 0.8 copy-start.14
  112.9 0.8 copy-start.15
  112.9 31.2 %collective-permute-start.10 = (bf16[4,1,128,1024]{3,2,1,0:T(8,128)(2,1)S(1)}, bf16[4,1,128,1024]{3,2,1,0:T(8,128)(2,1)}, u32[]{:S(2)}, u32[]{:S(2)}) collective-permute-start(bf16[4,1,128,1024]{3,2,1,0:T(8,128)(2,1)S(1)} %collective-permute-done.4.refs_4_), channel_id=1, source_target_pairs={{0,4},{1,3},{2,6},{3,1},{4,0},{5,7},{6,2},{7,5},{8,12},{9,11},{10,... | collective-permute-start | bytes 3145736 | tf_op jit(solution)/shard_map/ppermute | solution.py:62
  148.9 1.7 collective-permute-start.11
  150.7 0.7 copy-start.16
  153.4 25.0 %all-to-all-start = ((bf16[16,1,64,128]{3,2,1,0:T(8,128)(2,1)}), bf16[16,1,64,128]{3,2,1,0:T(8,128)(2,1)S(1)}, u32[]{:S(2)}, u32[]{:S(2)}) async-start(bf16[16,1,64,128]{3,2,1,0:T(8,128)(2,1)} %get-tuple-element.29), calls=%async_computation | async-start | bytes 524288 | tf_op jit(solution)/shard_map/all_to_all | solution.py:738
  178.4 3.0 copy-start.8
  178.4 4.3 %collective-permute-start.12 = (bf16[16,1,64,128]{3,2,1,0:T(8,128)(2,1)S(1)}, bf16[16,1,64,128]{3,2,1,0:T(8,128)(2,1)S(1)}, u32[]{:S(2)}, u32[]{:S(2)}) collective-permute-start(bf16[16,1,64,128]{3,2,1,0:T(8,128)(2,1)S(1)} %all-to-all-done.own_ref), channel_id=1, source_target_pairs={{0,1},{1,0},{2,3},{3,2},{4,5},{5,4},{6,7},{7,6},{8,9},{9,8},{10,11... | collective-permute-start | bytes 786440 | tf_op jit(solution)/shard_map/ppermute | solution.py:282
  181.4 33.8 %collective-permute-start.15 = (bf16[4,128,1792]{2,1,0:T(8,128)(2,1)}, bf16[4,128,1792]{2,1,0:T(8,128)(2,1)}, u32[]{:S(2)}, u32[]{:S(2)}) collective-permute-start(bf16[4,128,1792]{2,1,0:T(8,128)(2,1)} %pad_maximum_fusion.refs_7_.refs_1_), channel_id=1, source_target_pairs={{0,2},{1,5},{2,0},{3,7},{4,6},{5,1},{6,4},{7,3},{8,10},{9,13},{10,... | collective-permute-start | bytes 5505032 | tf_op jit(solution)/shard_map/ppermute | solution.py:62
  182.7 0.7 copy-start.17
  190.6 2.0 collective-permute-start.13
  191.5 37.8 %collective-permute-start.16 = (bf16[4,128,1792]{2,1,0:T(8,128)(2,1)}, bf16[4,128,1792]{2,1,0:T(8,128)(2,1)}, u32[]{:S(2)}, u32[]{:S(2)}) collective-permute-start(bf16[4,128,1792]{2,1,0:T(8,128)(2,1)} %pad_maximum_fusion.refs_7_.refs_1_), channel_id=1, source_target_pairs={{0,4},{1,3},{2,6},{3,1},{4,0},{5,7},{6,2},{7,5},{8,12},{9,11},{10,... | collective-permute-start | bytes 5505032 | tf_op jit(solution)/shard_map/ppermute | solution.py:62
  201.8 14.4 %copy-start = (f32[4,128,1024]{2,1,0:T(8,128)S(1)}, f32[4,128,1024]{2,1,0:T(8,128)}, u32[]{:S(2)}) copy-start(f32[4,128,1024]{2,1,0:T(8,128)} %first_ref.1) | copy-start | bytes 6291460
  201.8 2.1 collective-permute-start.14
  203.9 0.8 copy-start.12
  207.6 21.7 %all-to-all-start.1 = ((bf16[16,2,64,128]{3,2,1,0:T(8,128)(2,1)}), bf16[16,2,64,128]{3,2,1,0:T(8,128)(2,1)S(1)}, u32[]{:S(2)}, u32[]{:S(2)}) async-start(bf16[16,2,64,128]{3,2,1,0:T(8,128)(2,1)} %get-tuple-element.33), calls=%async_computation.1 | async-start | bytes 1048576 | tf_op jit(solution)/shard_map/all_to_all | solution.py:738
  215.2 34.1 %collective-permute-start.20 = (bf16[4,128,1792]{2,1,0:T(8,128)(2,1)}, bf16[4,128,1792]{2,1,0:T(8,128)(2,1)}, u32[]{:S(2)}, u32[]{:S(2)}) collective-permute-start(bf16[4,128,1792]{2,1,0:T(8,128)(2,1)} %collective-permute-done.15.refs_8_.refs_2_), channel_id=1, source_target_pairs={{0,4},{1,3},{2,6},{3,1},{4,0},{5,7},{6,2},{7,5},{8,12},{9,11},{10,... | collective-permute-start | bytes 5505032 | tf_op jit(solution)/shard_map/ppermute | solution.py:62
  229.2 2.7 copy-start.5
  229.3 2.7 collective-permute-start.17
  230.4 4.9 %collective-permute-start.24 = (f32[128,1024]{1,0:T(8,128)}, f32[128,1024]{1,0:T(8,128)S(1)}, u32[]{:S(2)}, u32[]{:S(2)}) collective-permute-start(f32[128,1024]{1,0:T(8,128)} %get-tuple-element.59), channel_id=1, source_target_pairs={{0,1},{1,0},{2,3},{3,2},{4,5},{5,4},{6,7},{7,6},{8,9},{9,8},{10,11... | collective-permute-start | bytes 1572872 | tf_op jit(solution)/shard_map/ppermute | solution.py:42
  230.5 4.8 %collective-permute-start.19 = (f32[128,1024]{1,0:T(8,128)S(1)}, f32[128,1024]{1,0:T(8,128)S(1)}, u32[]{:S(2)}, u32[]{:S(2)}) collective-permute-start(f32[128,1024]{1,0:T(8,128)S(1)} %get-tuple-element.60), channel_id=1, source_target_pairs={{0,1},{1,0},{2,3},{3,2},{4,5},{5,4},{6,7},{7,6},{8,9},{9,8},{10,11... | collective-permute-start | bytes 1572872 | tf_op jit(solution)/shard_map/ppermute | solution.py:42
  232.0 0.8 copy-start.11
  239.1 1.6 collective-permute-start.18
  240.7 0.7 copy-start.19
  259.9 2.5 collective-permute-start.21
  262.4 0.9 copy-start.9
  292.2 2.3 copy-start.4
  292.2 2.3 collective-permute-start.22
  294.5 0.9 copy-start.10
  304.3 7.0 %collective-permute-start.23 = (f32[128,256]{1,0:T(8,128)}, f32[128,256]{1,0:T(8,128)S(1)}, u32[]{:S(2)}, u32[]{:S(2)}) collective-permute-start(f32[128,256]{1,0:T(8,128)} %shard_map.69.own_ref), channel_id=1, source_target_pairs={{0,1},{1,0},{2,3},{3,2},{4,5},{5,4},{6,7},{7,6},{8,9},{9,8},{10,11... | collective-permute-start | bytes 393224 | tf_op jit(solution)/shard_map/ppermute | solution.py:579
  311.3 0.7 copy-start.18
Sparse Core Ops, SparseCore 0:
  21.7 144.5 all-gather.2

commit v5 on v4

--- a/solution.py
+++ b/solution.py
@@ -85,6 +85,25 @@
 
 def along_z(x, gate):
     return shifts(x if gate is None else after(x, gate))
+
+
+def along_line(x, gate):
+    wide = lax.axis_size("wide")
+    depth = wide // 4
+    z = lax.axis_index("wide") // 4
+    up = down = x if gate is None else after(x, gate)
+    ups, downs = [up], [down]
+    for hop in range(1, depth):
+        up = lax.ppermute(up, "wide", [(i, i + 4) for i in range(4 * (hop - 1), wide - 4)])
+        down = lax.ppermute(down, "wide", [(i, i - 4) for i in range(4, wide - 4 * (hop - 1))])
+        ups.append(up)
+        downs.append(down)
+    return ups, downs, [z >= hop for hop in range(depth)]
+
+
+def line_pieces(ups, downs, below):
+    depth = len(ups)
+    return [ups[0]] + [jnp.where(below[k], ups[k], downs[depth - k]) for k in range(1, depth)]
 
 
 def along_xy(pieces, gate):
@@ -422,18 +441,14 @@
                 row, j = at[p]
                 block = ref[p] if len(ref.shape) == 3 else ref[...]
                 lhs[row * r : (row + 1) * r, j * span : (j + 1) * span] = block
-        if level == 3:
-            each = piece_refs[0].shape[0]
-            for a in range(4):
-                for i in range(each):
-                    rest[place_ref[a * each + i]] = piece_refs[a][i]
+        each = piece_refs[0].shape[0]
+        for a in range(4):
+            for i in range(each):
+                rest[place_ref[a * each + i]] = piece_refs[a][i]
 
     if mirror:
         q = table_ref[OWN + level - 1]
-    if level == 3:
-        block = rest[:, :, pl.ds(pl.multiple_of(q * TILE, TILE), TILE)]
-    else:
-        block = piece_refs[0][...]
+    block = rest[:, :, pl.ds(pl.multiple_of(q * TILE, TILE), TILE)]
     total = jnp.dot(lhs[:, :span], block.reshape(span, TILE), preferred_element_type=F32)
     for j in range(1, level):
         for i in range(4 // j):
@@ -442,9 +457,7 @@
             else:
                 tile = table_ref[HELD + i * 4 + q]
             start = pl.multiple_of(j * span + tile * TILE, TILE)
-            if level == 2:
-                block = piece_refs[1][pl.ds(tile * per, per)]
-            elif j == 1:
+            if j == 1:
                 block = rest[pl.ds(tile * per, per), :, pl.ds(pl.multiple_of((4 + q % 2) * TILE, TILE), TILE)]
             else:
                 block = rest[pl.ds(tile * per, per), :, 6 * TILE : 7 * TILE]
@@ -463,26 +476,16 @@
             out_ref[p] = value.astype(BF)
 
 
-def sparse_product(level, table, place, rows, panel, rest, mirror):
+def sparse_product(level, table, place, rows, rest, mirror):
     wide = lax.axis_size("wide")
     r = rows[0][0].shape[-2]
     rows_n = 1 if mirror else level
-
-    def column(j):
-        def index(i, t):
-            q = t[OWN + level - 1] if mirror else i
-            return (0, 0, q if j == 0 else 4 + q % 2)
-
-        return index
 
     whole = pl.BlockSpec(memory_space=pltpu.VMEM)
     flat = [array for array, _ in rows]
     shapes = tuple((0, len(at), at) for _, at in rows)
     specs = [pl.BlockSpec(memory_space=pltpu.SMEM)] + [whole] * len(flat)
     operands = [table, place] + flat
-    for j in range(0 if level == 3 else 2):
-        specs.append(pl.BlockSpec((wide, r, TILE), column(j)))
-        operands.append(panel)
     specs += [whole] * len(rest)
     operands += rest
     if mirror:
@@ -491,7 +494,6 @@
     else:
         shape = jax.ShapeDtypeStruct((rows_n, r, 4 * TILE), BF)
         out_spec = pl.BlockSpec((rows_n, r, TILE), lambda i, t: (0, 0, i))
-    spare = (wide, r, 7 * TILE) if level == 3 else (1, 16, 128)
     return pl.pallas_call(
         functools.partial(sparse_body, level, shapes, mirror),
         grid_spec=pltpu.PrefetchScalarGridSpec(
@@ -501,7 +503,7 @@
             out_specs=out_spec,
             scratch_shapes=[
                 pltpu.VMEM((rows_n * r, level * LT * TILE), BF),
-                pltpu.VMEM(spare, BF),
+                pltpu.VMEM((wide, r, rest[0].shape[-1]), BF),
             ],
         ),
         out_shape=shape,
@@ -694,14 +696,13 @@
     if compact:
         table = make_table(parent, tile_node, structure, row_pos)
         shards = packed(factor, table)
-        panels = {2: lax.all_gather(shards[0], "wide", axis=0), 3: None}
         wide_diag = {m: narrow_all(diag_inverse[m], 1) for m in (2, 3)}
     else:
         panels = {m: lax.all_gather(panel_of(m), "wide", axis=0) for m in (2, 3)}
     one = along_xy(first, None)
     if compact:
-        third = along_z(after(shards[1], one[0]), None)
-    one = along_both(one, (one[2],) + tuple(third) if compact else None)
+        second = along_z(after(shards[0], one[0]), None)
+    one = along_both(one, (one[2],) + tuple(second) if compact else None)
 
     held = {}
     rows = {0: [(narrow_all(diag_inverse[0].astype(BF), 1), ((0, 0),))]}
@@ -712,8 +713,10 @@
         if packed_here:
             known = [part for k in range(level) for part in rows[k]] + [held[m] for m in range(1, level)]
             if level == 2:
-                rest = along_xy(third, panels[2])
-            value = sparse_product(level, table, place, known, panels[level], rest if level == 3 else [], False)
+                held_line = lax.optimization_barrier(tuple(third[0] + third[1]) + (diags[0],))
+                depth = len(third[0])
+                ahead = along_xy(line_pieces(held_line[:depth], held_line[depth:-1], third[2]), None)
+            value = sparse_product(level, table, place, known, rest, False)
             slots, full = place_slots(level, table, value)
         else:
             if level == 1:
@@ -730,21 +733,31 @@
                                 by_level[j] = array[p] if array.ndim == 3 else array
                     known.append([by_level[j] for j in range(level)])
             value = product(known, groups, above[:level, level])
+            if compact:
+                ahead = along_xy(second, value)
+                third = along_line(after(shards[1], ahead[0]), None)
             slots, full = make_slots(value)
         news.append(full)
         held[level] = (full, tuple((k, level) for k in range(level)))
         if level == LEV - 1:
             out = upper_rows(diag_inverse, news, turns, diags)
         got = lax.all_to_all(slots, "wide", split_axis=0, concat_axis=0, tiled=True)
-        if packed_here and level == 2:
-            rest = along_both(rest, (slots,))
-            got = after(got, rest[1], rest[2])
+        if level == LEV - 1:
+            got = after(got, out)
+        now = rest
+        if compact and level < LEV - 1:
+            if level == 1:
+                rest = along_both(ahead, (got, ahead[2]) + tuple(third[0][1:] + third[1][1:]))
+                got = after(got, ahead[1], ahead[2])
+            else:
+                rest = along_both(ahead, (slots, ahead[2]))
+                got = after(got, ahead[1], ahead[2])
         turn = mirrored(got, full)
         turns.append(turn)
         rows[level] = [(turn, tuple((level, j) for j in range(level)))]
         if packed_here:
             here = [(turn, tuple((0, j) for j in range(level)))]
-            inner = sparse_product(level, table, place, here, panels[level], rest if level == 3 else [], True)
+            inner = sparse_product(level, table, place, here, now, True)
             done, whole_low = diag_block(level, table, inner, wide_diag[level], row_pos)
         else:
             known = [[turn[k] for k in range(level)]]

time: 327 us -> 300 us (0.917)
  blocking collectives: 25.6 us -> 0 us
  starting transfers between devices: 40.2 us -> 56.9 us
  between operations: 13.7 us -> 0.45 us
  waiting for transfers between devices: 140 us -> 133 us
    all_to_all x1 -> x0, blocking collectives: 25.6 us -> none  [local(): got = lax.all_to_all(slots, 'wide', split_axis=0, concat_axis=0, tiled=True)]
    ppermute x0 -> x6, starting transfers between devices: none -> 12.1 us  [the longest x3 8.2 us: along_line(): lax.ppermute(up, 'wide', [(i, i + 4) for i in range(4 * (hop - 1), wide -...]
    ppermute x6 -> x9, waiting for transfers between devices: 61.7 us -> 51.5 us  [swap(): return lax.ppermute(value, ('wide', 'narrow'), pairs)]
    ppermute x0 -> x6, waiting for transfers between devices: none -> 7.56 us  [the longest x3 7.55 us: along_line(): lax.ppermute(down, 'wide', [(i, i - 4) for i in range(4, wide - 4 * (hop...]
    ppermute x6, waiting for transfers between devices: 46.9 us -> 42.2 us  [shifts(): lax.ppermute(value, 'wide', [(i, (i + 4 * hop) % wide) for i in range(wid...]
    all_to_all x2 -> x3, starting transfers between devices: 18.8 us -> 22.9 us  [local(): got = lax.all_to_all(slots, 'wide', split_axis=0, concat_axis=0, tiled=True)]
    ppermute x6 -> x9, starting transfers between devices: 6.39 us -> 9.74 us  [swap(): return lax.ppermute(value, ('wide', 'narrow'), pairs)]
    unnamed x53 -> x69, local copies, waits for them, and re-layouts: 9.48 us -> 8.63 us
  transfers between devices with their start and end apart: 28 -> 37, of which waited for: 15 -> 19; matrix products, arithmetic and copies ran while one was open for 5% -> 6% of each run, Pallas kernels for 13% -> 14%
where the time goes in v5:
time: 300 us; the launch traced here: 298 us
  waiting for transfers between devices  133 us (44%)
  Pallas kernels  75.6 us (25%)
  starting transfers between devices  56.9 us (19%)
  local copies, waits for them, and re-layouts  18.2 us (6%)
  other arithmetic  12.5 us (4%)
    ppermute x9, waiting for transfers between devices, swap(): return lax.ppermute(value, ('wide', 'narrow'), pairs)  51.5 us
    ppermute x6, waiting for transfers between devices, shifts(): lax.ppermute(value, 'wide', [(i, (i + 4 * hop) % wide) for i in range(wid...  42.2 us
    pallas_call x4, Pallas kernels, sparse_product(): pl.pallas_call(functools.partial(sparse_body, level, shapes, mirror), gri...  29.6 us
    all_to_all x3, starting transfers between devices, local(): got = lax.all_to_all(slots, 'wide', split_axis=0, concat_axis=0, tiled=True)  22.9 us
    all_to_all x3, waiting for transfers between devices, local(): got = lax.all_to_all(slots, 'wide', split_axis=0, concat_axis=0, tiled=True)  21.9 us
    ppermute x6, starting transfers between devices, shifts(): lax.ppermute(value, 'wide', [(i, (i + 4 * hop) % wide) for i in range(wid...  10.7 us
    pallas_call x2, Pallas kernels, product(): pl.pallas_call(functools.partial(product_body, plan, rows_n, steps_n, dia...  9.95 us
    ppermute x9, starting transfers between devices, swap(): return lax.ppermute(value, ('wide', 'narrow'), pairs)  9.74 us
  transfers between devices with their start and end apart: 37, of which 19 were waited for; matrix products, arithmetic and copies ran while one was open for 6% of the time, Pallas kernels for 14%

profile of v5, /device:TPU:0, one launch (start us, length us, event | category | flops | bytes accessed | tf_op | source)
XLA Modules:
  0.0 298.5 jit_solution(14091842035555352509)
XLA Ops:
  0.0 6.1 %fusion.30 = (bf16[1,128,1,1024]{3,2,1,0:T(2,128)(2,1)S(1)}, bf16[1,128,1,1024]{3,2,1,0:T(2,128)(2,1)S(1)}, bf16[1,128,1,1024]{3,2,1,0:T(2,128)(2,1)S(1)}, bf16[...) fusion(bf16[4,128,4,1024]{3,2,1,0:T(4,128)(2,1)} %param.5), kind=kLoop, calls=%fused_computation.75 | loop fusion | bytes 3145728 | tf_op jit(solution)/shard_map/slice | solution.py:414
  8.0 4.9 %collective-permute-start.3 = (bf16[1,128,1024]{2,1,0:T(8,128)(2,1)S(1)}, bf16[1,128,1024]{2,1,0:T(8,128)(2,1)S(1)}, u32[]{:S(2)}, u32[]{:S(2)}) collective-permute-start(bf16[1,128,1024]{2,1,0:T(8,128)(2,1)S(1)} %bitcast_multiply_fusion), channel_id=1, source_target_pairs={{0,24},{2,26},{4,28},{6,30},{8,0},{10,2},{12,4},{14,6},{16,8},{18,... | collective-permute-start | bytes 786440 | tf_op jit(solution)/shard_map/ppermute | solution.py:68
  12.9 1.0 collective-permute-start.1
  14.2 5.4 %collective-permute-done.3 = bf16[1,128,1024]{2,1,0:T(8,128)(2,1)S(1)} collective-permute-done((bf16[1,128,1024]{2,1,0:T(8,128)(2,1)S(1)}, bf16[1,128,1024]{2,1,0:T(8,128)(2,1)S(1)}, u32[]{:S(2)}, u32[]{:S(2)}) %collective-permute-start.3) | collective-permute-done | bytes 262176 | tf_op jit(solution)/shard_map/ppermute | solution.py:68
  19.6 16.0 %collective-permute-done.2 = bf16[1,128,1024]{2,1,0:T(8,128)(2,1)S(1)} collective-permute-done((bf16[1,128,1024]{2,1,0:T(8,128)(2,1)S(1)}, bf16[1,128,1024]{2,1,0:T(8,128)(2,1)S(1)}, u32[]{:S(2)}, u32[]{:S(2)}) %collective-permute-start.2) | collective-permute-done | bytes 262176 | tf_op jit(solution)/shard_map/ppermute | solution.py:68
  35.8 1.6 collective-permute-start.5
  37.4 1.5 collective-permute-start.4
  40.1 2.4 shard_map.55.table_ref
  43.0 3.0 %shard_map.56 = (bf16[128,1536]{1,0:T(8,128)(2,1)}, bf16[128,1792]{1,0:T(8,128)(2,1)}) custom-call(s32[1]{0:T(128)} %bitcast.id_ref, s32[128]{0:T(128)} %shard_map.55.table_ref, bf16[5,128,1024]{2,1,0:T(8,128)(2,1)} %copy-done.8, bf16[5,128,1024]{2,1,0:T(8,128)(2,1)} %collective-permute-done.6.other_ref), custom_call_target="tpu_custom_call" | custom-call | flops 1 | bytes 1 | tf_op jit(solution)/shard_map/pallas_call | solution.py:418
  46.1 2.8 collective-permute-start.8
  48.9 2.0 collective-permute-start.7
  51.2 1.1 fusion
  52.3 9.3 %collective-permute-done.5.refs_5_ = bf16[4,1,128,1024]{3,2,1,0:T(8,128)(2,1)S(1)} collective-permute-done((bf16[4,1,128,1024]{3,2,1,0:T(8,128)(2,1)S(1)}, bf16[4,1,128,1024]{3,2,1,0:T(8,128)(2,1)S(1)}, u32[]{:S(2)}, u32[]{:S(2)}) %collective-permute-start.5) | collective-permute-done | bytes 1048608 | tf_op jit(solution)/shard_map/ppermute | solution.py:62
  61.6 20.8 %collective-permute-done.8 = bf16[128,1536]{1,0:T(8,128)(2,1)S(1)} collective-permute-done((bf16[128,1536]{1,0:T(8,128)(2,1)}, bf16[128,1536]{1,0:T(8,128)(2,1)S(1)}, u32[]{:S(2)}, u32[]{:S(2)}) %collective-permute-start.8) | collective-permute-done | bytes 393248 | tf_op jit(solution)/shard_map/ppermute | solution.py:68
  85.2 1.2 broadcast_select_fusion.7
  87.2 10.9 %collective-permute-done.10.refs_6_ = bf16[4,1,128,1024]{3,2,1,0:T(8,128)(2,1)S(1)} collective-permute-done((bf16[4,1,128,1024]{3,2,1,0:T(8,128)(2,1)}, bf16[4,1,128,1024]{3,2,1,0:T(8,128)(2,1)S(1)}, u32[]{:S(2)}, u32[]{:S(2)}) %collective-permute-start.10) | collective-permute-done | bytes 1048608 | tf_op jit(solution)/shard_map/ppermute | solution.py:62
  98.2 1.0 copy-done.5
  99.2 4.8 %shard_map.57.own_ref = bf16[1,128,1024]{2,1,0:T(8,128)(2,1)} custom-call(s32[1,16]{1,0:T(1,128)} %add.73.refs_0_, s32[1,4]{1,0:T(1,128)} %fusion.25.refs_1_, bf16[128,2048]{1,0:T(8,128)(2,1)} %pad_maximum_fusion.5.refs_2_.refs_0_, bf16[4,1,128,1024]{3,2,1,0:T(8,128)(2,1)} %copy-done.2, bf16[4,1,128,1024]{3,2,1,0:T(8,128)(2,1)} %collective-permute-done.4.refs_4_, ...), custom_call_target="tpu_custom_call" | custom-call | flops 1 | bytes 1 | tf_op jit(solution)/shard_map/pallas_call | solution.py:228
  105.4 1.3 collective-permute-start.19
  106.7 5.3 %collective-permute-start.16 = (bf16[128,1792]{1,0:T(8,128)(2,1)S(1)}, bf16[128,1792]{1,0:T(8,128)(2,1)}, u32[]{:S(2)}, u32[]{:S(2)}) collective-permute-start(bf16[128,1792]{1,0:T(8,128)(2,1)S(1)} %copy-done.15), channel_id=1, source_target_pairs={{0,8},{2,10},{4,12},{6,14},{8,16},{10,18},{12,20},{14,22},{16,24},... | collective-permute-start | bytes 1376264 | tf_op jit(solution)/shard_map/ppermute | solution.py:97
  112.0 4.7 %collective-permute-done.19 = bf16[128,1792]{1,0:T(8,128)(2,1)} collective-permute-done((bf16[128,1792]{1,0:T(8,128)(2,1)S(1)}, bf16[128,1792]{1,0:T(8,128)(2,1)}, u32[]{:S(2)}, u32[]{:S(2)}) %collective-permute-start.19) | collective-permute-done | bytes 458784 | tf_op jit(solution)/shard_map/ppermute | solution.py:98
  116.7 1.3 collective-permute-start.20
  118.0 1.4 collective-permute-start.17
  120.1 2.0 shard_map.58
  122.2 8.1 %all-to-all-start = ((bf16[16,1,64,128]{3,2,1,0:T(8,128)(2,1)}), bf16[16,1,64,128]{3,2,1,0:T(8,128)(2,1)S(1)}, u32[]{:S(2)}, u32[]{:S(2)}) async-start(bf16[16,1,64,128]{3,2,1,0:T(8,128)(2,1)} %get-tuple-element.40), calls=%async_computation | async-start | bytes 524288 | tf_op jit(solution)/shard_map/all_to_all | solution.py:744
  130.3 1.3 collective-permute-start.21
  131.6 1.4 collective-permute-start.18
  133.2 7.7 %all-to-all-done.own_ref = bf16[16,1,64,128]{3,2,1,0:T(8,128)(2,1)S(1)} async-done(((bf16[16,1,64,128]{3,2,1,0:T(8,128)(2,1)}), bf16[16,1,64,128]{3,2,1,0:T(8,128)(2,1)S(1)}, u32[]{:S(2)}, u32[]{:S(2)}) %all-to-all-start) | async-done | bytes 262176 | tf_op jit(solution)/shard_map/all_to_all | solution.py:744
  141.7 2.8 collective-permute-done.21
  144.6 1.6 collective-permute-start.22
  146.2 2.0 shard_map.59.refs_1_.refs_3_
  148.2 5.1 %shard_map.60 = (f32[128,1024]{1,0:T(8,128)}, bf16[128,1024]{1,0:T(8,128)(2,1)}) custom-call(s32[1,16]{1,0:T(1,128)} %add.73.refs_0_, s32[1,4]{1,0:T(1,128)} %slice_convert_fusion.1.refs_1_, bf16[128,2048]{1,0:T(8,128)(2,1)} %bitcast.100, bf16[4,1,128,1024]{3,2,1,0:T(8,128)(2,1)} %copy-done.2, bf16[4,1,128,1024]{3,2,1,0:T(8,128)(2,1)} %collective-permute-done.4.refs_4_, ...), custom_call_target="tpu_custom_call" | custom-call | flops 1 | bytes 1 | tf_op jit(solution)/shard_map/pallas_call | solution.py:228
  153.3 1.1 select_bitcast_fusion.2
  154.4 1.1 select_bitcast_fusion.1
  155.6 1.1 select_bitcast_fusion
  156.7 1.5 pad_maximum_fusion.refs_7_.refs_1_
  158.6 1.5 collective-permute-start.24
  160.7 0.9 collective-permute-done.15
  162.5 9.1 %collective-permute-done.22.refs_7_.refs_4_ = bf16[4,128,1536]{2,1,0:T(8,128)(2,1)} collective-permute-done((bf16[4,128,1536]{2,1,0:T(8,128)(2,1)}, bf16[4,128,1536]{2,1,0:T(8,128)(2,1)}, u32[]{:S(2)}, u32[]{:S(2)}) %collective-permute-start.22) | collective-permute-done | bytes 1572896 | tf_op jit(solution)/shard_map/ppermute | solution.py:62
  171.6 7.9 %shard_map.61.own_ref = bf16[2,128,1024]{2,1,0:T(8,128)(2,1)} custom-call(s32[128]{0:T(128)} %shard_map.55.table_ref, s32[16]{0:T(128)} %add.72.place_ref, bf16[128,2048]{1,0:T(8,128)(2,1)} %pad_maximum_fusion.5.refs_2_.refs_0_, bf16[1,128,2048]{2,1,0:T(8,128)(2,1)} %shard_map.59.refs_1_.refs_3_, bf16[128,2048]{1,0:T(8,128)(2,1)} %pad_maximum_fusion.6.refs_2_, ...), custom_call_target="tpu_custom_call" | custom-call | flops 1 | bytes 1 | tf_op jit(solution)/shard_map/pallas_call | solution.py:497
  179.5 2.1 collective-permute-done.23.other_ref
  182.4 2.8 shard_map.62
  185.2 7.8 %all-to-all-start.1 = ((bf16[16,2,64,128]{3,2,1,0:T(8,128)(2,1)}), bf16[16,2,64,128]{3,2,1,0:T(8,128)(2,1)S(1)}, u32[]{:S(2)}, u32[]{:S(2)}) async-start(bf16[16,2,64,128]{3,2,1,0:T(8,128)(2,1)} %get-tuple-element.51), calls=%async_computation.1 | async-start | bytes 1048576 | tf_op jit(solution)/shard_map/all_to_all | solution.py:744
  193.0 16.9 %collective-permute-done.25.refs_9_.refs_3_ = bf16[4,128,1792]{2,1,0:T(8,128)(2,1)} collective-permute-done((bf16[4,128,1792]{2,1,0:T(8,128)(2,1)}, bf16[4,128,1792]{2,1,0:T(8,128)(2,1)}, u32[]{:S(2)}, u32[]{:S(2)}) %collective-permute-start.25) | collective-permute-done | bytes 1835040 | tf_op jit(solution)/shard_map/ppermute | solution.py:62
  209.9 1.6 collective-permute-start.29
  211.5 1.1 slice_bitcast_fusion
  213.1 1.4 collective-permute-done.26.other_ref
  215.3 2.5 shard_map.63.refs_0_.refs_3_.refs_4_
  218.0 5.3 %shard_map.64.own_ref = f32[128,256]{1,0:T(8,128)} custom-call(s32[128]{0:T(128)} %shard_map.55.table_ref, s32[16]{0:T(128)} %add.72.place_ref, bf16[2,128,2048]{2,1,0:T(8,128)(2,1)} %shard_map.63.refs_0_.refs_3_.refs_4_, bf16[4,128,1536]{2,1,0:T(8,128)(2,1)} %copy-done.1, bf16[4,128,1536]{2,1,0:T(8,128)(2,1)} %collective-permute-done.12.refs_5_.refs_2_, ...), custom_call_target="tpu_custom_call" | custom-call | flops 1 | bytes 1 | tf_op jit(solution)/shard_map/pallas_call | solution.py:497
  223.4 1.1 pad_maximum_fusion.3.diag_ref
  225.5 2.7 shard_map.65
  228.2 5.3 %collective-permute-done.29.refs_10_.refs_4_ = bf16[4,128,1792]{2,1,0:T(8,128)(2,1)} collective-permute-done((bf16[4,128,1792]{2,1,0:T(8,128)(2,1)}, bf16[4,128,1792]{2,1,0:T(8,128)(2,1)}, u32[]{:S(2)}, u32[]{:S(2)}) %collective-permute-start.29) | collective-permute-done | bytes 1835040 | tf_op jit(solution)/shard_map/ppermute | solution.py:62
  233.4 10.5 %shard_map.66.own_ref = bf16[3,128,1024]{2,1,0:T(8,128)(2,1)} custom-call(s32[128]{0:T(128)} %shard_map.55.table_ref, s32[16]{0:T(128)} %add.72.place_ref, bf16[128,2048]{1,0:T(8,128)(2,1)} %pad_maximum_fusion.5.refs_2_.refs_0_, bf16[1,128,2048]{2,1,0:T(8,128)(2,1)} %shard_map.59.refs_1_.refs_3_, bf16[128,2048]{1,0:T(8,128)(2,1)} %pad_maximum_fusion.6.refs_2_, ...), custom_call_target="tpu_custom_call" | custom-call | flops 1 | bytes 1 | tf_op jit(solution)/shard_map/pallas_call | solution.py:497
  243.9 2.5 collective-permute-done.30.other_ref
  247.3 3.4 %shard_map.67 = (bf16[16,3,64,128]{3,2,1,0:T(8,128)(2,1)}, bf16[3,128,2048]{2,1,0:T(8,128)(2,1)}) custom-call(s32[1]{0:T(128)} %bitcast.id_ref, s32[128]{0:T(128)} %shard_map.55.table_ref, bf16[3,128,1024]{2,1,0:T(8,128)(2,1)} %shard_map.66.own_ref, bf16[3,128,1024]{2,1,0:T(8,128)(2,1)} %copy-done.11), custom_call_target="tpu_custom_call" | custom-call | flops 1 | bytes 1 | tf_op jit(solution)/shard_map/pallas_call | solution.py:547
  250.7 7.0 %all-to-all-start.2 = ((bf16[16,3,64,128]{3,2,1,0:T(8,128)(2,1)}), bf16[16,3,64,128]{3,2,1,0:T(8,128)(2,1)S(1)}, u32[]{:S(2)}, u32[]{:S(2)}) async-start(bf16[16,3,64,128]{3,2,1,0:T(8,128)(2,1)} %get-tuple-element.64), calls=%async_computation.2 | async-start | bytes 1572864 | tf_op jit(solution)/shard_map/all_to_all | solution.py:744
  257.7 5.9 %shard_map.68.held_ref = f32[4,128,4,1024]{3,2,1,0:T(4,128)} custom-call(s32[1]{0:T(128)} %bitcast.id_ref, f32[4,128,1024]{2,1,0:T(8,128)} %first_ref.1, bf16[1,128,2048]{2,1,0:T(8,128)(2,1)} %get-tuple-element.47.refs_3_.refs_5_.refs_0_, bf16[2,128,2048]{2,1,0:T(8,128)(2,1)} %get-tuple-element.62.refs_6_.refs_1_, ...), custom_call_target="tpu_custom_call" | custom-call | bytes 41943040 | tf_op jit(solution)/shard_map/pallas_call | solution.py:622
  263.6 14.1 %all-to-all-done.2.own_ref = bf16[16,3,64,128]{3,2,1,0:T(8,128)(2,1)S(1)} async-done(((bf16[16,3,64,128]{3,2,1,0:T(8,128)(2,1)}), bf16[16,3,64,128]{3,2,1,0:T(8,128)(2,1)S(1)}, u32[]{:S(2)}, u32[]{:S(2)}) %all-to-all-start.2) | async-done | bytes 786464 | tf_op jit(solution)/shard_map/all_to_all | solution.py:744
  277.7 2.3 collective-permute-done.31.other_ref
  280.9 3.1 %shard_map.69.refs_0_.turn_ref = bf16[3,128,2048]{2,1,0:T(8,128)(2,1)} custom-call(s32[1]{0:T(128)} %bitcast.id_ref, bf16[16,3,64,128]{3,2,1,0:T(8,128)(2,1)} %copy-done.6, bf16[16,3,64,128]{3,2,1,0:T(8,128)(2,1)} %copy-done.12), custom_call_target="tpu_custom_call" | custom-call | flops 1 | bytes 1 | tf_op jit(solution)/shard_map/pallas_call | solution.py:303
  283.9 5.9 %shard_map.70.own_ref = f32[128,256]{1,0:T(8,128)} custom-call(s32[128]{0:T(128)} %shard_map.55.table_ref, s32[16]{0:T(128)} %add.72.place_ref, bf16[3,128,2048]{2,1,0:T(8,128)(2,1)} %shard_map.69.refs_0_.turn_ref, bf16[4,128,1792]{2,1,0:T(8,128)(2,1)} %pad_maximum_fusion.refs_7_.refs_1_, bf16[4,128,1792]{2,1,0:T(8,128)(2,1)} %collective-permute-done.24.refs_8_.refs_2_, ...), custom_call_target="tpu_custom_call" | custom-call | flops 1 | bytes 1 | tf_op jit(solution)/shard_map/pallas_call | solution.py:497
  290.0 1.1 pad_maximum_fusion.4.diag_ref
  292.0 2.6 shard_map.71
  294.6 3.8 %shard_map.72 = f32[4,128,4,1024]{3,2,1,0:T(4,128)} custom-call(s32[1]{0:T(128)} %bitcast.id_ref, bf16[3,128,2048]{2,1,0:T(8,128)(2,1)} %shard_map.69.refs_0_.turn_ref, f32[128,1024]{1,0:T(8,128)} %get-tuple-element.68.diag_ref, f32[4,128,4,1024]{3,2,1,0:T(4,128)} %shard_map.68.held_ref), custom_call_target="tpu_custom_call", output_to_operand_aliasing={{}: (3, {})} | custom-call | bytes 1 | tf_op jit(solution)/shard_map/pallas_call | solution.py:639
  (135 shorter events, 19.4 us)
Async XLA Ops:
  6.2 0.9 copy-start.28
  6.2 1.0 copy-start.29
  6.6 29.2 %copy-start.8 = (bf16[5,128,1024]{2,1,0:T(8,128)(2,1)}, bf16[5,128,1024]{2,1,0:T(8,128)(2,1)S(1)}, u32[]{:S(2)}) copy-start(bf16[5,128,1024]{2,1,0:T(8,128)(2,1)S(1)} %fusion.1.own_ref) | copy-start | bytes 3932164
  6.6 36.4 %collective-permute-start.6 = (bf16[5,128,1024]{2,1,0:T(8,128)(2,1)S(1)}, bf16[5,128,1024]{2,1,0:T(8,128)(2,1)}, u32[]{:S(2)}, u32[]{:S(2)}) collective-permute-start(bf16[5,128,1024]{2,1,0:T(8,128)(2,1)S(1)} %fusion.1.own_ref), channel_id=1, source_target_pairs={{0,1},{1,0},{2,3},{3,2},{4,5},{5,4},{6,7},{7,6},{8,9},{9,8},{10,11... | collective-permute-start | bytes 3932168 | tf_op jit(solution)/shard_map/ppermute | solution.py:415
  8.0 34.5 %copy-start.30 = (s32[15]{0:T(128)S(1)}, s32[15]{0:T(128)}, u32[]{:S(2)}) copy-start(s32[15]{0:T(128)} %parent_ref.1) | copy-start | bytes 184
  8.0 11.6 %collective-permute-start.3 = (bf16[1,128,1024]{2,1,0:T(8,128)(2,1)S(1)}, bf16[1,128,1024]{2,1,0:T(8,128)(2,1)S(1)}, u32[]{:S(2)}, u32[]{:S(2)}) collective-permute-start(bf16[1,128,1024]{2,1,0:T(8,128)(2,1)S(1)} %bitcast_multiply_fusion), channel_id=1, source_target_pairs={{0,24},{2,26},{4,28},{6,30},{8,0},{10,2},{12,4},{14,6},{16,8},{18,... | collective-permute-start | bytes 786440 | tf_op jit(solution)/shard_map/ppermute | solution.py:68
  12.9 22.7 %collective-permute-start.2 = (bf16[1,128,1024]{2,1,0:T(8,128)(2,1)S(1)}, bf16[1,128,1024]{2,1,0:T(8,128)(2,1)S(1)}, u32[]{:S(2)}, u32[]{:S(2)}) collective-permute-start(bf16[1,128,1024]{2,1,0:T(8,128)(2,1)S(1)} %bitcast_multiply_fusion), channel_id=1, source_target_pairs={{0,16},{2,18},{4,20},{6,22},{8,24},{10,26},{12,28},{14,30},{16,0},... | collective-permute-start | bytes 786440 | tf_op jit(solution)/shard_map/ppermute | solution.py:68
  12.9 22.7 %collective-permute-start.1 = (bf16[1,128,1024]{2,1,0:T(8,128)(2,1)S(1)}, bf16[1,128,1024]{2,1,0:T(8,128)(2,1)S(1)}, u32[]{:S(2)}, u32[]{:S(2)}) collective-permute-start(bf16[1,128,1024]{2,1,0:T(8,128)(2,1)S(1)} %bitcast_multiply_fusion), channel_id=1, source_target_pairs={{0,8},{2,10},{4,12},{6,14},{8,16},{10,18},{12,20},{14,22},{16,24},... | collective-permute-start | bytes 786440 | tf_op jit(solution)/shard_map/ppermute | solution.py:68
  35.8 16.5 %copy-start.2 = (bf16[4,1,128,1024]{3,2,1,0:T(8,128)(2,1)}, bf16[4,1,128,1024]{3,2,1,0:T(8,128)(2,1)S(1)}, u32[]{:S(2)}) copy-start(bf16[4,1,128,1024]{3,2,1,0:T(8,128)(2,1)S(1)} %pad_maximum_fusion.2.refs_3_) | copy-start | bytes 3145732
  35.8 25.8 %collective-permute-start.5 = (bf16[4,1,128,1024]{3,2,1,0:T(8,128)(2,1)S(1)}, bf16[4,1,128,1024]{3,2,1,0:T(8,128)(2,1)S(1)}, u32[]{:S(2)}, u32[]{:S(2)}) collective-permute-start(bf16[4,1,128,1024]{3,2,1,0:T(8,128)(2,1)S(1)} %pad_maximum_fusion.2.refs_3_), channel_id=1, source_target_pairs={{0,4},{1,3},{2,6},{3,1},{4,0},{5,7},{6,2},{7,5},{8,12},{9,11},{10,... | collective-permute-start | bytes 3145736 | tf_op jit(solution)/shard_map/ppermute | solution.py:62
  37.4 24.2 %collective-permute-start.4 = (bf16[4,1,128,1024]{3,2,1,0:T(8,128)(2,1)S(1)}, bf16[4,1,128,1024]{3,2,1,0:T(8,128)(2,1)}, u32[]{:S(2)}, u32[]{:S(2)}) collective-permute-start(bf16[4,1,128,1024]{3,2,1,0:T(8,128)(2,1)S(1)} %pad_maximum_fusion.2.refs_3_), channel_id=1, source_target_pairs={{0,2},{1,5},{2,0},{3,7},{4,6},{5,1},{6,4},{7,3},{8,10},{9,13},{10,... | collective-permute-start | bytes 3145736 | tf_op jit(solution)/shard_map/ppermute | solution.py:62
  46.1 15.5 %collective-permute-start.9 = (bf16[128,1536]{1,0:T(8,128)(2,1)}, bf16[128,1536]{1,0:T(8,128)(2,1)S(1)}, u32[]{:S(2)}, u32[]{:S(2)}) collective-permute-start(bf16[128,1536]{1,0:T(8,128)(2,1)} %get-tuple-element.41), channel_id=1, source_target_pairs={{0,24},{2,26},{4,28},{6,30},{8,0},{10,2},{12,4},{14,6},{16,8},{18,... | collective-permute-start | bytes 1179656 | tf_op jit(solution)/shard_map/ppermute | solution.py:68
  46.1 36.3 %collective-permute-start.8 = (bf16[128,1536]{1,0:T(8,128)(2,1)}, bf16[128,1536]{1,0:T(8,128)(2,1)S(1)}, u32[]{:S(2)}, u32[]{:S(2)}) collective-permute-start(bf16[128,1536]{1,0:T(8,128)(2,1)} %get-tuple-element.41), channel_id=1, source_target_pairs={{0,16},{2,18},{4,20},{6,22},{8,24},{10,26},{12,28},{14,30},{16,0},... | collective-permute-start | bytes 1179656 | tf_op jit(solution)/shard_map/ppermute | solution.py:68
  48.9 33.5 %collective-permute-start.7 = (bf16[128,1536]{1,0:T(8,128)(2,1)}, bf16[128,1536]{1,0:T(8,128)(2,1)S(1)}, u32[]{:S(2)}, u32[]{:S(2)}) collective-permute-start(bf16[128,1536]{1,0:T(8,128)(2,1)} %get-tuple-element.41), channel_id=1, source_target_pairs={{0,8},{2,10},{4,12},{6,14},{8,16},{10,18},{12,20},{14,22},{16,24},... | collective-permute-start | bytes 1179656 | tf_op jit(solution)/shard_map/ppermute | solution.py:68
  61.6 36.6 %copy-start.4 = (bf16[4,1,128,1024]{3,2,1,0:T(8,128)(2,1)}, bf16[4,1,128,1024]{3,2,1,0:T(8,128)(2,1)S(1)}, u32[]{:S(2)}) copy-start(bf16[4,1,128,1024]{3,2,1,0:T(8,128)(2,1)S(1)} %collective-permute-done.5.refs_5_) | copy-start | bytes 3145732
  61.6 23.6 %collective-permute-start = (bf16[128,1024]{1,0:T(8,128)(2,1)S(1)}, bf16[128,1024]{1,0:T(8,128)(2,1)}, u32[]{:S(2)}, u32[]{:S(2)}) collective-permute-start(bf16[128,1024]{1,0:T(8,128)(2,1)S(1)} %fusion), channel_id=1, source_target_pairs={{0,1},{1,0},{2,3},{3,2},{4,5},{5,4},{6,7},{7,6},{8,9},{9,8},{10,11... | collective-permute-start | bytes 786440 | tf_op jit(solution)/shard_map/ppermute | solution.py:42
  61.6 20.8 %copy-start.18 = (bf16[128,1536]{1,0:T(8,128)(2,1)}, bf16[128,1536]{1,0:T(8,128)(2,1)S(1)}, u32[]{:S(2)}) copy-start(bf16[128,1536]{1,0:T(8,128)(2,1)S(1)} %collective-permute-done.9) | copy-start | bytes 1179652
  83.1 0.8 copy-start.22
  83.1 15.0 %collective-permute-start.10 = (bf16[4,1,128,1024]{3,2,1,0:T(8,128)(2,1)}, bf16[4,1,128,1024]{3,2,1,0:T(8,128)(2,1)S(1)}, u32[]{:S(2)}, u32[]{:S(2)}) collective-permute-start(bf16[4,1,128,1024]{3,2,1,0:T(8,128)(2,1)} %collective-permute-done.4.refs_4_), channel_id=1, source_target_pairs={{0,4},{1,3},{2,6},{3,1},{4,0},{5,7},{6,2},{7,5},{8,12},{9,11},{10,... | collective-permute-start | bytes 3145736 | tf_op jit(solution)/shard_map/ppermute | solution.py:62
  87.2 16.8 %copy-start.17 = (bf16[128,1536]{1,0:T(8,128)(2,1)S(1)}, bf16[128,1536]{1,0:T(8,128)(2,1)}, u32[]{:S(2)}) copy-start(bf16[128,1536]{1,0:T(8,128)(2,1)} %get-tuple-element.41) | copy-start | bytes 1179652
  87.2 16.8 %copy-start.19 = (bf16[128,1536]{1,0:T(8,128)(2,1)S(1)}, bf16[128,1536]{1,0:T(8,128)(2,1)}, u32[]{:S(2)}) copy-start(bf16[128,1536]{1,0:T(8,128)(2,1)} %copy-done.18) | copy-start | bytes 1179652
  87.2 16.8 %copy-start.21 = (bf16[128,1536]{1,0:T(8,128)(2,1)S(1)}, bf16[128,1536]{1,0:T(8,128)(2,1)}, u32[]{:S(2)}) copy-start(bf16[128,1536]{1,0:T(8,128)(2,1)} %copy-done.20) | copy-start | bytes 1179652
  87.2 16.8 %copy-start.23 = (bf16[128,1536]{1,0:T(8,128)(2,1)S(1)}, bf16[128,1536]{1,0:T(8,128)(2,1)}, u32[]{:S(2)}) copy-start(bf16[128,1536]{1,0:T(8,128)(2,1)} %copy-done.22) | copy-start | bytes 1179652
  98.2 1.0 copy-start.5
  104.0 1.3 copy-start.15
  104.0 8.0 %copy-start.10 = (bf16[1,128,1024]{2,1,0:T(8,128)(2,1)S(1)}, bf16[1,128,1024]{2,1,0:T(8,128)(2,1)}, u32[]{:S(2)}) copy-start(bf16[1,128,1024]{2,1,0:T(8,128)(2,1)} %shard_map.57.own_ref) | copy-start | bytes 786436
  104.2 49.1 %copy-start.1 = (bf16[4,128,1536]{2,1,0:T(8,128)(2,1)}, bf16[4,128,1536]{2,1,0:T(8,128)(2,1)S(1)}, u32[]{:S(2)}) copy-start(bf16[4,128,1536]{2,1,0:T(8,128)(2,1)S(1)} %pad_maximum_fusion.1.refs_4_.refs_1_) | copy-start | bytes 4718596
  104.3 36.7 %collective-permute-start.13 = (bf16[4,128,1536]{2,1,0:T(8,128)(2,1)S(1)}, bf16[4,128,1536]{2,1,0:T(8,128)(2,1)S(1)}, u32[]{:S(2)}, u32[]{:S(2)}) collective-permute-start(bf16[4,128,1536]{2,1,0:T(8,128)(2,1)S(1)} %pad_maximum_fusion.1.refs_4_.refs_1_), channel_id=1, source_target_pairs={{0,4},{1,3},{2,6},{3,1},{4,0},{5,7},{6,2},{7,5},{8,12},{9,11},{10,... | collective-permute-start | bytes 4718600 | tf_op jit(solution)/shard_map/ppermute | solution.py:62
  104.8 36.1 %collective-permute-start.12 = (bf16[4,128,1536]{2,1,0:T(8,128)(2,1)S(1)}, bf16[4,128,1536]{2,1,0:T(8,128)(2,1)}, u32[]{:S(2)}, u32[]{:S(2)}) collective-permute-start(bf16[4,128,1536]{2,1,0:T(8,128)(2,1)S(1)} %pad_maximum_fusion.1.refs_4_.refs_1_), channel_id=1, source_target_pairs={{0,2},{1,5},{2,0},{3,7},{4,6},{5,1},{6,4},{7,3},{8,10},{9,13},{10,... | collective-permute-start | bytes 4718600 | tf_op jit(solution)/shard_map/ppermute | solution.py:62
  105.4 11.3 %collective-permute-start.19 = (bf16[128,1792]{1,0:T(8,128)(2,1)S(1)}, bf16[128,1792]{1,0:T(8,128)(2,1)}, u32[]{:S(2)}, u32[]{:S(2)}) collective-permute-start(bf16[128,1792]{1,0:T(8,128)(2,1)S(1)} %copy-done.15), channel_id=1, source_target_pairs={{8,0},{10,2},{12,4},{14,6},{16,8},{18,10},{20,12},{22,14},{24,16},... | collective-permute-start | bytes 1376264 | tf_op jit(solution)/shard_map/ppermute | solution.py:98
  106.7 11.3 %collective-permute-start.16 = (bf16[128,1792]{1,0:T(8,128)(2,1)S(1)}, bf16[128,1792]{1,0:T(8,128)(2,1)}, u32[]{:S(2)}, u32[]{:S(2)}) collective-permute-start(bf16[128,1792]{1,0:T(8,128)(2,1)S(1)} %copy-done.15), channel_id=1, source_target_pairs={{0,8},{2,10},{4,12},{6,14},{8,16},{10,18},{12,20},{14,22},{16,24},... | collective-permute-start | bytes 1376264 | tf_op jit(solution)/shard_map/ppermute | solution.py:97
  112.0 7.4 %collective-permute-start.11 = (bf16[1,128,1024]{2,1,0:T(8,128)(2,1)S(1)}, bf16[1,128,1024]{2,1,0:T(8,128)(2,1)S(1)}, u32[]{:S(2)}, u32[]{:S(2)}) collective-permute-start(bf16[1,128,1024]{2,1,0:T(8,128)(2,1)S(1)} %copy-done.10), channel_id=1, source_target_pairs={{0,1},{1,0},{2,3},{3,2},{4,5},{5,4},{6,7},{7,6},{8,9},{9,8},{10,11... | collective-permute-start | bytes 786440 | tf_op jit(solution)/shard_map/ppermute | solution.py:267
  116.7 13.6 %collective-permute-start.20 = (bf16[128,1792]{1,0:T(8,128)(2,1)}, bf16[128,1792]{1,0:T(8,128)(2,1)}, u32[]{:S(2)}, u32[]{:S(2)}) collective-permute-start(bf16[128,1792]{1,0:T(8,128)(2,1)} %collective-permute-done.19), channel_id=1, source_target_pairs={{8,0},{10,2},{12,4},{14,6},{16,8},{18,10},{20,12},{22,14},{9,1},{1... | collective-permute-start | bytes 1376264 | tf_op jit(solution)/shard_map/ppermute | solution.py:98
  118.0 13.6 %collective-permute-start.17 = (bf16[128,1792]{1,0:T(8,128)(2,1)}, bf16[128,1792]{1,0:T(8,128)(2,1)}, u32[]{:S(2)}, u32[]{:S(2)}) collective-permute-start(bf16[128,1792]{1,0:T(8,128)(2,1)} %collective-permute-done.16), channel_id=1, source_target_pairs={{8,16},{10,18},{12,20},{14,22},{16,24},{18,26},{20,28},{22,30},{9,... | collective-permute-start | bytes 1376264 | tf_op jit(solution)/shard_map/ppermute | solution.py:97
  122.2 18.8 %all-to-all-start = ((bf16[16,1,64,128]{3,2,1,0:T(8,128)(2,1)}), bf16[16,1,64,128]{3,2,1,0:T(8,128)(2,1)S(1)}, u32[]{:S(2)}, u32[]{:S(2)}) async-start(bf16[16,1,64,128]{3,2,1,0:T(8,128)(2,1)} %get-tuple-element.40), calls=%async_computation | async-start | bytes 524288 | tf_op jit(solution)/shard_map/all_to_all | solution.py:744
  130.3 14.3 %collective-permute-start.21 = (bf16[128,1792]{1,0:T(8,128)(2,1)}, bf16[128,1792]{1,0:T(8,128)(2,1)}, u32[]{:S(2)}, u32[]{:S(2)}) collective-permute-start(bf16[128,1792]{1,0:T(8,128)(2,1)} %collective-permute-done.20), channel_id=1, source_target_pairs={{8,0},{10,2},{12,4},{14,6},{9,1},{11,3},{13,5},{15,7}} | collective-permute-start | bytes 1376264 | tf_op jit(solution)/shard_map/ppermute | solution.py:98
  131.6 13.0 %collective-permute-start.18 = (bf16[128,1792]{1,0:T(8,128)(2,1)}, bf16[128,1792]{1,0:T(8,128)(2,1)}, u32[]{:S(2)}, u32[]{:S(2)}) collective-permute-start(bf16[128,1792]{1,0:T(8,128)(2,1)} %collective-permute-done.17), channel_id=1, source_target_pairs={{16,24},{18,26},{20,28},{22,30},{17,25},{19,27},{21,29},{23,31}} | collective-permute-start | bytes 1376264 | tf_op jit(solution)/shard_map/ppermute | solution.py:97
  140.9 5.2 %copy-start.9 = (bf16[16,1,64,128]{3,2,1,0:T(8,128)(2,1)}, bf16[16,1,64,128]{3,2,1,0:T(8,128)(2,1)S(1)}, u32[]{:S(2)}) copy-start(bf16[16,1,64,128]{3,2,1,0:T(8,128)(2,1)S(1)} %all-to-all-done.own_ref) | copy-start | bytes 786436
  140.9 12.4 %copy-start.3 = (bf16[4,128,1536]{2,1,0:T(8,128)(2,1)}, bf16[4,128,1536]{2,1,0:T(8,128)(2,1)S(1)}, u32[]{:S(2)}) copy-start(bf16[4,128,1536]{2,1,0:T(8,128)(2,1)S(1)} %collective-permute-done.13.refs_6_.refs_3_) | copy-start | bytes 4718596
  140.9 5.2 %collective-permute-start.14 = (bf16[16,1,64,128]{3,2,1,0:T(8,128)(2,1)S(1)}, bf16[16,1,64,128]{3,2,1,0:T(8,128)(2,1)}, u32[]{:S(2)}, u32[]{:S(2)}) collective-permute-start(bf16[16,1,64,128]{3,2,1,0:T(8,128)(2,1)S(1)} %all-to-all-done.own_ref), channel_id=1, source_target_pairs={{0,1},{1,0},{2,3},{3,2},{4,5},{5,4},{6,7},{7,6},{8,9},{9,8},{10,11... | collective-permute-start | bytes 786440 | tf_op jit(solution)/shard_map/ppermute | solution.py:301
  144.6 27.0 %collective-permute-start.22 = (bf16[4,128,1536]{2,1,0:T(8,128)(2,1)}, bf16[4,128,1536]{2,1,0:T(8,128)(2,1)}, u32[]{:S(2)}, u32[]{:S(2)}) collective-permute-start(bf16[4,128,1536]{2,1,0:T(8,128)(2,1)} %collective-permute-done.12.refs_5_.refs_2_), channel_id=1, source_target_pairs={{0,4},{1,3},{2,6},{3,1},{4,0},{5,7},{6,2},{7,5},{8,12},{9,11},{10,... | collective-permute-start | bytes 4718600 | tf_op jit(solution)/shard_map/ppermute | solution.py:62
  154.4 2.2 copy-start.16
  156.7 3.4 %copy-start.25 = (bf16[128,1024]{1,0:T(8,128)(2,1)S(1)}, bf16[128,1024]{1,0:T(8,128)(2,1)}, u32[]{:S(2)}) copy-start(bf16[128,1024]{1,0:T(8,128)(2,1)} %get-tuple-element.46) | copy-start | bytes 786436
  158.2 51.7 %collective-permute-start.25 = (bf16[4,128,1792]{2,1,0:T(8,128)(2,1)}, bf16[4,128,1792]{2,1,0:T(8,128)(2,1)}, u32[]{:S(2)}, u32[]{:S(2)}) collective-permute-start(bf16[4,128,1792]{2,1,0:T(8,128)(2,1)} %pad_maximum_fusion.refs_7_.refs_1_), channel_id=1, source_target_pairs={{0,4},{1,3},{2,6},{3,1},{4,0},{5,7},{6,2},{7,5},{8,12},{9,11},{10,... | collective-permute-start | bytes 5505032 | tf_op jit(solution)/shard_map/ppermute | solution.py:62
  158.6 51.3 %collective-permute-start.24 = (bf16[4,128,1792]{2,1,0:T(8,128)(2,1)}, bf16[4,128,1792]{2,1,0:T(8,128)(2,1)}, u32[]{:S(2)}, u32[]{:S(2)}) collective-permute-start(bf16[4,128,1792]{2,1,0:T(8,128)(2,1)} %pad_maximum_fusion.refs_7_.refs_1_), channel_id=1, source_target_pairs={{0,2},{1,5},{2,0},{3,7},{4,6},{5,1},{6,4},{7,3},{8,10},{9,13},{10,... | collective-permute-start | bytes 5505032 | tf_op jit(solution)/shard_map/ppermute | solution.py:62
  160.1 1.5 collective-permute-start.15
  179.5 32.0 %copy-start = (f32[4,128,1024]{2,1,0:T(8,128)S(1)}, f32[4,128,1024]{2,1,0:T(8,128)}, u32[]{:S(2)}) copy-start(f32[4,128,1024]{2,1,0:T(8,128)} %first_ref.1) | copy-start | bytes 6291460
  179.5 2.1 collective-permute-start.23
  181.6 0.8 copy-start.14
  185.2 27.3 %all-to-all-start.1 = ((bf16[16,2,64,128]{3,2,1,0:T(8,128)(2,1)}), bf16[16,2,64,128]{3,2,1,0:T(8,128)(2,1)S(1)}, u32[]{:S(2)}, u32[]{:S(2)}) async-start(bf16[16,2,64,128]{3,2,1,0:T(8,128)(2,1)} %get-tuple-element.51), calls=%async_computation.1 | async-start | bytes 1048576 | tf_op jit(solution)/shard_map/all_to_all | solution.py:744
  209.9 23.5 %collective-permute-start.29 = (bf16[4,128,1792]{2,1,0:T(8,128)(2,1)}, bf16[4,128,1792]{2,1,0:T(8,128)(2,1)}, u32[]{:S(2)}, u32[]{:S(2)}) collective-permute-start(bf16[4,128,1792]{2,1,0:T(8,128)(2,1)} %collective-permute-done.24.refs_8_.refs_2_), channel_id=1, source_target_pairs={{0,4},{1,3},{2,6},{3,1},{4,0},{5,7},{6,2},{7,5},{8,12},{9,11},{10,... | collective-permute-start | bytes 5505032 | tf_op jit(solution)/shard_map/ppermute | solution.py:62
  212.5 2.0 copy-start.7
  212.5 2.0 collective-permute-start.26
  212.5 5.2 %collective-permute-start.33 = (f32[128,1024]{1,0:T(8,128)}, f32[128,1024]{1,0:T(8,128)S(1)}, u32[]{:S(2)}, u32[]{:S(2)}) collective-permute-start(f32[128,1024]{1,0:T(8,128)} %get-tuple-element.81), channel_id=1, source_target_pairs={{0,1},{1,0},{2,3},{3,2},{4,5},{5,4},{6,7},{7,6},{8,9},{9,8},{10,11... | collective-permute-start | bytes 1572872 | tf_op jit(solution)/shard_map/ppermute | solution.py:42
  213.0 4.7 %collective-permute-start.28 = (f32[128,1024]{1,0:T(8,128)}, f32[128,1024]{1,0:T(8,128)S(1)}, u32[]{:S(2)}, u32[]{:S(2)}) collective-permute-start(f32[128,1024]{1,0:T(8,128)} %get-tuple-element.82), channel_id=1, source_target_pairs={{0,1},{1,0},{2,3},{3,2},{4,5},{5,4},{6,7},{7,6},{8,9},{9,8},{10,11... | collective-permute-start | bytes 1572872 | tf_op jit(solution)/shard_map/ppermute | solution.py:42
  214.5 0.8 copy-start.13
  223.3 1.6 collective-permute-start.27
  243.9 2.5 collective-permute-start.30
  246.4 0.9 copy-start.11
  250.7 27.0 %all-to-all-start.2 = ((bf16[16,3,64,128]{3,2,1,0:T(8,128)(2,1)}), bf16[16,3,64,128]{3,2,1,0:T(8,128)(2,1)S(1)}, u32[]{:S(2)}, u32[]{:S(2)}) async-start(bf16[16,3,64,128]{3,2,1,0:T(8,128)(2,1)} %get-tuple-element.64), calls=%async_computation.2 | async-start | bytes 1572864 | tf_op jit(solution)/shard_map/all_to_all | solution.py:744
  277.7 2.3 copy-start.6
  277.7 2.3 collective-permute-start.31
  280.0 0.9 copy-start.12
  289.8 1.6 collective-permute-start.32
  (4 other events, 2.8 us)

commit v6 on v5

--- a/solution.py
+++ b/solution.py
@@ -701,8 +701,8 @@
         panels = {m: lax.all_gather(panel_of(m), "wide", axis=0) for m in (2, 3)}
     one = along_xy(first, None)
     if compact:
-        second = along_z(after(shards[0], one[0]), None)
-    one = along_both(one, (one[2],) + tuple(second) if compact else None)
+        second = along_line(after(shards[0], one[0]), None)
+    one = along_both(one, (one[2],) if compact else None)
 
     held = {}
     rows = {0: [(narrow_all(diag_inverse[0].astype(BF), 1), ((0, 0),))]}
@@ -722,6 +722,8 @@
             if level == 1:
                 groups = [((0,), place, one)]
                 known = [[rows[0][0][0]]]
+                if compact:
+                    known[0][0] = after(known[0][0], *second[0][1:], *second[1][1:])
             else:
                 groups = [(tuple(range(level)), whole_place, [panels[level]])]
                 known = []
@@ -734,7 +736,9 @@
                     known.append([by_level[j] for j in range(level)])
             value = product(known, groups, above[:level, level])
             if compact:
-                ahead = along_xy(second, value)
+                held_line = lax.optimization_barrier(tuple(second[0] + second[1]) + (value,))
+                depth = len(second[0])
+                ahead = along_xy(line_pieces(held_line[:depth], held_line[depth:-1], second[2]), None)
                 third = along_line(after(shards[1], ahead[0]), None)
             slots, full = make_slots(value)
         news.append(full)

time: 300 us -> 292 us (0.973)
  waiting for transfers between devices: 133 us -> 110 us
  starting transfers between devices: 56.9 us -> 69.2 us
    ppermute x6 -> x3, waiting for transfers between devices: 42.2 us -> 18.4 us  [shifts(): lax.ppermute(value, 'wide', [(i, (i + 4 * hop) % wide) for i in range(wid...]
    ppermute x3 -> x6, waiting for transfers between devices: 7.55 us -> 23.5 us  [along_line(): lax.ppermute(down, 'wide', [(i, i - 4) for i in range(4, wide - 4 * (hop...]
    ppermute x9, waiting for transfers between devices: 51.5 us -> 38.5 us  [swap(): return lax.ppermute(value, ('wide', 'narrow'), pairs)]
    ppermute x3 -> x6, starting transfers between devices: 8.2 us -> 14.9 us  [along_line(): lax.ppermute(up, 'wide', [(i, i + 4) for i in range(4 * (hop - 1), wide -...]
    ppermute x9, starting transfers between devices: 9.74 us -> 15.3 us  [swap(): return lax.ppermute(value, ('wide', 'narrow'), pairs)]
    ppermute x6 -> x3, starting transfers between devices: 10.7 us -> 6.11 us  [shifts(): lax.ppermute(value, 'wide', [(i, (i + 4 * hop) % wide) for i in range(wid...]
    ppermute x3 -> x6, starting transfers between devices: 3.85 us -> 7.69 us  [along_line(): lax.ppermute(down, 'wide', [(i, i - 4) for i in range(4, wide - 4 * (hop...]
    unnamed x69 -> x57, local copies, waits for them, and re-layouts: 8.63 us -> 8.19 us
  transfers between devices with their start and end apart: 37 -> 40, of which waited for: 19 -> 19; matrix products, arithmetic and copies ran while one was open for 6% -> 7% of each run, Pallas kernels for 14% -> 14%
where the time goes in v6:
time: 292 us; the launch traced here: 290 us
  waiting for transfers between devices  110 us (38%)
  Pallas kernels  75.7 us (26%)
  starting transfers between devices  69.2 us (24%)
  local copies, waits for them, and re-layouts  19 us (7%)
  other arithmetic  12.6 us (4%)
  matrix products  3.19 us (1%)
    ppermute x9, waiting for transfers between devices, swap(): return lax.ppermute(value, ('wide', 'narrow'), pairs)  38.5 us
    pallas_call x4, Pallas kernels, sparse_product(): pl.pallas_call(functools.partial(sparse_body, level, shapes, mirror), gri...  29.6 us
    all_to_all x3, starting transfers between devices, local(): got = lax.all_to_all(slots, 'wide', split_axis=0, concat_axis=0, tiled=True)  24.1 us
    ppermute x6, waiting for transfers between devices, along_line(): lax.ppermute(down, 'wide', [(i, i - 4) for i in range(4, wide - 4 * (hop...  23.5 us
    all_to_all x3, waiting for transfers between devices, local(): got = lax.all_to_all(slots, 'wide', split_axis=0, concat_axis=0, tiled=True)  19.8 us
    ppermute x3, waiting for transfers between devices, shifts(): lax.ppermute(value, 'wide', [(i, (i + 4 * hop) % wide) for i in range(wid...  18.4 us
    ppermute x9, starting transfers between devices, swap(): return lax.ppermute(value, ('wide', 'narrow'), pairs)  15.3 us
    ppermute x6, starting transfers between devices, along_line(): lax.ppermute(up, 'wide', [(i, i + 4) for i in range(4 * (hop - 1), wide -...  14.9 us
  transfers between devices with their start and end apart: 40, of which 19 were waited for; matrix products, arithmetic and copies ran while one was open for 7% of the time, Pallas kernels for 14%

profile of v6, /device:TPU:0, one launch (start us, length us, event | category | flops | bytes accessed | tf_op | source)
XLA Modules:
  0.0 290.3 jit_solution(15081417962768983784)
XLA Ops:
  2.1 6.2 %fusion.30 = (bf16[1,128,1,1024]{3,2,1,0:T(2,128)(2,1)S(1)}, bf16[1,128,1,1024]{3,2,1,0:T(2,128)(2,1)S(1)}, bf16[1,128,1,1024]{3,2,1,0:T(2,128)(2,1)S(1)}, bf16[...) fusion(bf16[4,128,4,1024]{3,2,1,0:T(4,128)(2,1)} %param.5), kind=kLoop, calls=%fused_computation.78 | loop fusion | bytes 3145728 | tf_op jit(solution)/shard_map/slice | solution.py:685
  8.4 5.1 %collective-permute-start.4 = (bf16[1,128,1024]{2,1,0:T(8,128)(2,1)S(1)}, bf16[1,128,1024]{2,1,0:T(8,128)(2,1)S(1)}, u32[]{:S(2)}, u32[]{:S(2)}) collective-permute-start(bf16[1,128,1024]{2,1,0:T(8,128)(2,1)S(1)} %bitcast_multiply_fusion), channel_id=1, source_target_pairs={{0,24},{2,26},{4,28},{6,30},{8,0},{10,2},{12,4},{14,6},{16,8},{18,... | collective-permute-start | bytes 786440 | tf_op jit(solution)/shard_map/ppermute | solution.py:68
  15.0 2.2 fusion
  17.4 2.8 collective-permute-done.4
  20.2 15.6 %collective-permute-done.3 = bf16[1,128,1024]{2,1,0:T(8,128)(2,1)S(1)} collective-permute-done((bf16[1,128,1024]{2,1,0:T(8,128)(2,1)S(1)}, bf16[1,128,1024]{2,1,0:T(8,128)(2,1)S(1)}, u32[]{:S(2)}, u32[]{:S(2)}) %collective-permute-start.3) | collective-permute-done | bytes 262176 | tf_op jit(solution)/shard_map/ppermute | solution.py:68
  36.0 1.6 collective-permute-start.12
  37.5 1.5 collective-permute-start.11
  40.4 2.4 shard_map.55.table_ref
  43.3 3.0 %shard_map.56 = (bf16[128,1536]{1,0:T(8,128)(2,1)}, bf16[128,1792]{1,0:T(8,128)(2,1)}) custom-call(s32[1]{0:T(128)} %bitcast.id_ref, s32[128]{0:T(128)} %shard_map.55.table_ref, bf16[5,128,1024]{2,1,0:T(8,128)(2,1)} %copy-done.7, bf16[5,128,1024]{2,1,0:T(8,128)(2,1)} %collective-permute-done.1.other_ref), custom_call_target="tpu_custom_call" | custom-call | flops 1 | bytes 1 | tf_op jit(solution)/shard_map/pallas_call | solution.py:418
  46.4 1.3 collective-permute-start.8
  47.7 4.6 %collective-permute-start.5 = (bf16[128,1536]{1,0:T(8,128)(2,1)}, bf16[128,1536]{1,0:T(8,128)(2,1)S(1)}, u32[]{:S(2)}, u32[]{:S(2)}) collective-permute-start(bf16[128,1536]{1,0:T(8,128)(2,1)} %get-tuple-element.46), channel_id=1, source_target_pairs={{0,8},{2,10},{4,12},{6,14},{8,16},{10,18},{12,20},{14,22},{16,24},... | collective-permute-start | bytes 1179656 | tf_op jit(solution)/shard_map/ppermute | solution.py:97
  52.7 8.6 %collective-permute-done.12.refs_5_ = bf16[4,1,128,1024]{3,2,1,0:T(8,128)(2,1)S(1)} collective-permute-done((bf16[4,1,128,1024]{3,2,1,0:T(8,128)(2,1)S(1)}, bf16[4,1,128,1024]{3,2,1,0:T(8,128)(2,1)S(1)}, u32[]{:S(2)}, u32[]{:S(2)}) %collective-permute-start.12) | collective-permute-done | bytes 1048608 | tf_op jit(solution)/shard_map/ppermute | solution.py:62
  61.3 1.5 collective-permute-start.13
  62.9 1.3 collective-permute-start.9
  64.2 1.4 collective-permute-start.6
  66.9 6.8 %collective-permute-done.9 = bf16[128,1536]{1,0:T(8,128)(2,1)S(1)} collective-permute-done((bf16[128,1536]{1,0:T(8,128)(2,1)S(1)}, bf16[128,1536]{1,0:T(8,128)(2,1)S(1)}, u32[]{:S(2)}, u32[]{:S(2)}) %collective-permute-start.9) | collective-permute-done | bytes 393248 | tf_op jit(solution)/shard_map/ppermute | solution.py:98
  73.6 1.3 collective-permute-start.10
  75.6 1.2 broadcast_select_fusion.7
  77.7 5.9 %collective-permute-done.10 = bf16[128,1536]{1,0:T(8,128)(2,1)S(1)} collective-permute-done((bf16[128,1536]{1,0:T(8,128)(2,1)S(1)}, bf16[128,1536]{1,0:T(8,128)(2,1)S(1)}, u32[]{:S(2)}, u32[]{:S(2)}) %collective-permute-start.10) | collective-permute-done | bytes 393248 | tf_op jit(solution)/shard_map/ppermute | solution.py:98
  83.5 4.8 %shard_map.57.own_ref = bf16[1,128,1024]{2,1,0:T(8,128)(2,1)} custom-call(s32[1,16]{1,0:T(1,128)} %add.73.refs_0_, s32[1,4]{1,0:T(1,128)} %fusion.25.refs_1_, bf16[128,2048]{1,0:T(8,128)(2,1)} %pad_maximum_fusion.5.refs_2_.refs_0_, bf16[4,1,128,1024]{3,2,1,0:T(8,128)(2,1)} %copy-done.2, bf16[4,1,128,1024]{3,2,1,0:T(8,128)(2,1)} %collective-permute-done.11.refs_4_, ...), custom_call_target="tpu_custom_call" | custom-call | flops 1 | bytes 1 | tf_op jit(solution)/shard_map/pallas_call | solution.py:228
  89.6 2.6 collective-permute-start.16
  92.2 3.0 %collective-permute-start.15 = (bf16[4,128,1536]{2,1,0:T(8,128)(2,1)S(1)}, bf16[4,128,1536]{2,1,0:T(8,128)(2,1)}, u32[]{:S(2)}, u32[]{:S(2)}) collective-permute-start(bf16[4,128,1536]{2,1,0:T(8,128)(2,1)S(1)} %pad_maximum_fusion.1.refs_4_.refs_1_), channel_id=1, source_target_pairs={{0,2},{1,5},{2,0},{3,7},{4,6},{5,1},{6,4},{7,3},{8,10},{9,13},{10,... | collective-permute-start | bytes 4718600 | tf_op jit(solution)/shard_map/ppermute | solution.py:62
  95.2 1.3 collective-permute-start.22
  96.5 5.3 %collective-permute-start.19 = (bf16[128,1792]{1,0:T(8,128)(2,1)S(1)}, bf16[128,1792]{1,0:T(8,128)(2,1)}, u32[]{:S(2)}, u32[]{:S(2)}) collective-permute-start(bf16[128,1792]{1,0:T(8,128)(2,1)S(1)} %copy-done.14), channel_id=1, source_target_pairs={{0,8},{2,10},{4,12},{6,14},{8,16},{10,18},{12,20},{14,22},{16,24},... | collective-permute-start | bytes 1376264 | tf_op jit(solution)/shard_map/ppermute | solution.py:97
  101.8 5.6 %collective-permute-done.22 = bf16[128,1792]{1,0:T(8,128)(2,1)} collective-permute-done((bf16[128,1792]{1,0:T(8,128)(2,1)S(1)}, bf16[128,1792]{1,0:T(8,128)(2,1)}, u32[]{:S(2)}, u32[]{:S(2)}) %collective-permute-start.22) | collective-permute-done | bytes 458784 | tf_op jit(solution)/shard_map/ppermute | solution.py:98
  107.4 1.3 collective-permute-start.23
  108.7 1.4 collective-permute-start.20
  110.9 2.0 shard_map.58
  112.9 9.1 %all-to-all-start = ((bf16[16,1,64,128]{3,2,1,0:T(8,128)(2,1)}), bf16[16,1,64,128]{3,2,1,0:T(8,128)(2,1)S(1)}, u32[]{:S(2)}, u32[]{:S(2)}) async-start(bf16[16,1,64,128]{3,2,1,0:T(8,128)(2,1)} %get-tuple-element.45), calls=%async_computation | async-start | bytes 524288 | tf_op jit(solution)/shard_map/all_to_all | solution.py:748
  122.0 1.3 collective-permute-start.24
  123.3 1.5 collective-permute-start.21
  124.9 5.6 %all-to-all-done.own_ref = bf16[16,1,64,128]{3,2,1,0:T(8,128)(2,1)S(1)} async-done(((bf16[16,1,64,128]{3,2,1,0:T(8,128)(2,1)}), bf16[16,1,64,128]{3,2,1,0:T(8,128)(2,1)S(1)}, u32[]{:S(2)}, u32[]{:S(2)}) %all-to-all-start) | async-done | bytes 262176 | tf_op jit(solution)/shard_map/all_to_all | solution.py:748
  131.3 5.2 %collective-permute-done.24 = bf16[128,1792]{1,0:T(8,128)(2,1)} collective-permute-done((bf16[128,1792]{1,0:T(8,128)(2,1)}, bf16[128,1792]{1,0:T(8,128)(2,1)}, u32[]{:S(2)}, u32[]{:S(2)}) %collective-permute-start.24) | collective-permute-done | bytes 458784 | tf_op jit(solution)/shard_map/ppermute | solution.py:98
  136.5 1.6 collective-permute-start.25
  138.8 2.1 shard_map.59.refs_1_.refs_3_
  140.9 5.1 %shard_map.60 = (f32[128,1024]{1,0:T(8,128)}, bf16[128,1024]{1,0:T(8,128)(2,1)}) custom-call(s32[1,16]{1,0:T(1,128)} %add.73.refs_0_, s32[1,4]{1,0:T(1,128)} %slice_convert_fusion.1.refs_1_, bf16[128,2048]{1,0:T(8,128)(2,1)} %bitcast.103, bf16[4,1,128,1024]{3,2,1,0:T(8,128)(2,1)} %copy-done.2, bf16[4,1,128,1024]{3,2,1,0:T(8,128)(2,1)} %collective-permute-done.11.refs_4_, ...), custom_call_target="tpu_custom_call" | custom-call | flops 1 | bytes 1 | tf_op jit(solution)/shard_map/pallas_call | solution.py:228
  146.0 1.1 select_bitcast_fusion.2
  147.1 1.1 select_bitcast_fusion.1
  148.3 1.1 select_bitcast_fusion
  149.4 1.5 pad_maximum_fusion.refs_7_.refs_1_
  151.3 1.5 collective-permute-start.27
  155.2 7.5 %collective-permute-done.25.refs_7_.refs_4_ = bf16[4,128,1536]{2,1,0:T(8,128)(2,1)} collective-permute-done((bf16[4,128,1536]{2,1,0:T(8,128)(2,1)}, bf16[4,128,1536]{2,1,0:T(8,128)(2,1)}, u32[]{:S(2)}, u32[]{:S(2)}) %collective-permute-start.25) | collective-permute-done | bytes 1572896 | tf_op jit(solution)/shard_map/ppermute | solution.py:62
  162.6 7.9 %shard_map.61.own_ref = bf16[2,128,1024]{2,1,0:T(8,128)(2,1)} custom-call(s32[128]{0:T(128)} %shard_map.55.table_ref, s32[16]{0:T(128)} %add.72.place_ref, bf16[128,2048]{1,0:T(8,128)(2,1)} %pad_maximum_fusion.5.refs_2_.refs_0_, bf16[1,128,2048]{2,1,0:T(8,128)(2,1)} %shard_map.59.refs_1_.refs_3_, bf16[128,2048]{1,0:T(8,128)(2,1)} %pad_maximum_fusion.6.refs_2_, ...), custom_call_target="tpu_custom_call" | custom-call | flops 1 | bytes 1 | tf_op jit(solution)/shard_map/pallas_call | solution.py:497
  170.6 2.1 collective-permute-done.26.other_ref
  173.5 2.8 shard_map.62
  176.3 8.3 %all-to-all-start.1 = ((bf16[16,2,64,128]{3,2,1,0:T(8,128)(2,1)}), bf16[16,2,64,128]{3,2,1,0:T(8,128)(2,1)S(1)}, u32[]{:S(2)}, u32[]{:S(2)}) async-start(bf16[16,2,64,128]{3,2,1,0:T(8,128)(2,1)} %get-tuple-element.59), calls=%async_computation.1 | async-start | bytes 1048576 | tf_op jit(solution)/shard_map/all_to_all | solution.py:748
  184.6 17.3 %collective-permute-done.28.refs_9_.refs_3_ = bf16[4,128,1792]{2,1,0:T(8,128)(2,1)} collective-permute-done((bf16[4,128,1792]{2,1,0:T(8,128)(2,1)}, bf16[4,128,1792]{2,1,0:T(8,128)(2,1)}, u32[]{:S(2)}, u32[]{:S(2)}) %collective-permute-start.28) | collective-permute-done | bytes 1835040 | tf_op jit(solution)/shard_map/ppermute | solution.py:62
  201.9 1.6 collective-permute-start.32
  205.1 1.4 collective-permute-done.29.other_ref
  207.3 2.5 shard_map.63.refs_0_.refs_3_.refs_4_
  210.0 5.3 %shard_map.64.own_ref = f32[128,256]{1,0:T(8,128)} custom-call(s32[128]{0:T(128)} %shard_map.55.table_ref, s32[16]{0:T(128)} %add.72.place_ref, bf16[2,128,2048]{2,1,0:T(8,128)(2,1)} %shard_map.63.refs_0_.refs_3_.refs_4_, bf16[4,128,1536]{2,1,0:T(8,128)(2,1)} %copy-done.1, bf16[4,128,1536]{2,1,0:T(8,128)(2,1)} %collective-permute-done.15.refs_5_.refs_2_, ...), custom_call_target="tpu_custom_call" | custom-call | flops 1 | bytes 1 | tf_op jit(solution)/shard_map/pallas_call | solution.py:497
  217.5 2.7 shard_map.65
  220.2 5.2 %collective-permute-done.32.refs_10_.refs_4_ = bf16[4,128,1792]{2,1,0:T(8,128)(2,1)} collective-permute-done((bf16[4,128,1792]{2,1,0:T(8,128)(2,1)}, bf16[4,128,1792]{2,1,0:T(8,128)(2,1)}, u32[]{:S(2)}, u32[]{:S(2)}) %collective-permute-start.32) | collective-permute-done | bytes 1835040 | tf_op jit(solution)/shard_map/ppermute | solution.py:62
  225.4 10.5 %shard_map.66.own_ref = bf16[3,128,1024]{2,1,0:T(8,128)(2,1)} custom-call(s32[128]{0:T(128)} %shard_map.55.table_ref, s32[16]{0:T(128)} %add.72.place_ref, bf16[128,2048]{1,0:T(8,128)(2,1)} %pad_maximum_fusion.5.refs_2_.refs_0_, bf16[1,128,2048]{2,1,0:T(8,128)(2,1)} %shard_map.59.refs_1_.refs_3_, bf16[128,2048]{1,0:T(8,128)(2,1)} %pad_maximum_fusion.6.refs_2_, ...), custom_call_target="tpu_custom_call" | custom-call | flops 1 | bytes 1 | tf_op jit(solution)/shard_map/pallas_call | solution.py:497
  235.9 2.5 collective-permute-done.33.other_ref
  239.3 3.4 %shard_map.67 = (bf16[16,3,64,128]{3,2,1,0:T(8,128)(2,1)}, bf16[3,128,2048]{2,1,0:T(8,128)(2,1)}) custom-call(s32[1]{0:T(128)} %bitcast.id_ref, s32[128]{0:T(128)} %shard_map.55.table_ref, bf16[3,128,1024]{2,1,0:T(8,128)(2,1)} %shard_map.66.own_ref, bf16[3,128,1024]{2,1,0:T(8,128)(2,1)} %copy-done.10), custom_call_target="tpu_custom_call" | custom-call | flops 1 | bytes 1 | tf_op jit(solution)/shard_map/pallas_call | solution.py:547
  242.7 6.7 %all-to-all-start.2 = ((bf16[16,3,64,128]{3,2,1,0:T(8,128)(2,1)}), bf16[16,3,64,128]{3,2,1,0:T(8,128)(2,1)S(1)}, u32[]{:S(2)}, u32[]{:S(2)}) async-start(bf16[16,3,64,128]{3,2,1,0:T(8,128)(2,1)} %get-tuple-element.72), calls=%async_computation.2 | async-start | bytes 1572864 | tf_op jit(solution)/shard_map/all_to_all | solution.py:748
  249.4 5.9 %shard_map.68.held_ref = f32[4,128,4,1024]{3,2,1,0:T(4,128)} custom-call(s32[1]{0:T(128)} %bitcast.id_ref, f32[4,128,1024]{2,1,0:T(8,128)} %first_ref.1, bf16[1,128,2048]{2,1,0:T(8,128)(2,1)} %get-tuple-element.55.refs_3_.refs_5_.refs_0_, bf16[2,128,2048]{2,1,0:T(8,128)(2,1)} %get-tuple-element.70.refs_6_.refs_1_, ...), custom_call_target="tpu_custom_call" | custom-call | bytes 41943040 | tf_op jit(solution)/shard_map/pallas_call | solution.py:622
  255.3 14.1 %all-to-all-done.2.own_ref = bf16[16,3,64,128]{3,2,1,0:T(8,128)(2,1)S(1)} async-done(((bf16[16,3,64,128]{3,2,1,0:T(8,128)(2,1)}), bf16[16,3,64,128]{3,2,1,0:T(8,128)(2,1)S(1)}, u32[]{:S(2)}, u32[]{:S(2)}) %all-to-all-start.2) | async-done | bytes 786464 | tf_op jit(solution)/shard_map/all_to_all | solution.py:748
  269.4 2.3 collective-permute-done.34.other_ref
  272.6 3.0 %shard_map.69.refs_0_.turn_ref = bf16[3,128,2048]{2,1,0:T(8,128)(2,1)} custom-call(s32[1]{0:T(128)} %bitcast.id_ref, bf16[16,3,64,128]{3,2,1,0:T(8,128)(2,1)} %copy-done.5, bf16[16,3,64,128]{3,2,1,0:T(8,128)(2,1)} %copy-done.11), custom_call_target="tpu_custom_call" | custom-call | flops 1 | bytes 1 | tf_op jit(solution)/shard_map/pallas_call | solution.py:303
  275.7 5.9 %shard_map.70.own_ref = f32[128,256]{1,0:T(8,128)} custom-call(s32[128]{0:T(128)} %shard_map.55.table_ref, s32[16]{0:T(128)} %add.72.place_ref, bf16[3,128,2048]{2,1,0:T(8,128)(2,1)} %shard_map.69.refs_0_.turn_ref, bf16[4,128,1792]{2,1,0:T(8,128)(2,1)} %pad_maximum_fusion.refs_7_.refs_1_, bf16[4,128,1792]{2,1,0:T(8,128)(2,1)} %collective-permute-done.27.refs_8_.refs_2_, ...), custom_call_target="tpu_custom_call" | custom-call | flops 1 | bytes 1 | tf_op jit(solution)/shard_map/pallas_call | solution.py:497
  283.8 2.6 shard_map.71
  286.4 3.8 %shard_map.72 = f32[4,128,4,1024]{3,2,1,0:T(4,128)} custom-call(s32[1]{0:T(128)} %bitcast.id_ref, bf16[3,128,2048]{2,1,0:T(8,128)(2,1)} %shard_map.69.refs_0_.turn_ref, f32[128,1024]{1,0:T(8,128)} %get-tuple-element.76.diag_ref, f32[4,128,4,1024]{3,2,1,0:T(4,128)} %shard_map.68.held_ref), custom_call_target="tpu_custom_call", output_to_operand_aliasing={{}: (3, {})} | custom-call | bytes 1 | tf_op jit(solution)/shard_map/pallas_call | solution.py:639
  (132 shorter events, 25.4 us)
Async XLA Ops:
  8.4 11.9 %collective-permute-start.4 = (bf16[1,128,1024]{2,1,0:T(8,128)(2,1)S(1)}, bf16[1,128,1024]{2,1,0:T(8,128)(2,1)S(1)}, u32[]{:S(2)}, u32[]{:S(2)}) collective-permute-start(bf16[1,128,1024]{2,1,0:T(8,128)(2,1)S(1)} %bitcast_multiply_fusion), channel_id=1, source_target_pairs={{0,24},{2,26},{4,28},{6,30},{8,0},{10,2},{12,4},{14,6},{16,8},{18,... | collective-permute-start | bytes 786440 | tf_op jit(solution)/shard_map/ppermute | solution.py:68
  13.5 22.3 %collective-permute-start.3 = (bf16[1,128,1024]{2,1,0:T(8,128)(2,1)S(1)}, bf16[1,128,1024]{2,1,0:T(8,128)(2,1)S(1)}, u32[]{:S(2)}, u32[]{:S(2)}) collective-permute-start(bf16[1,128,1024]{2,1,0:T(8,128)(2,1)S(1)} %bitcast_multiply_fusion), channel_id=1, source_target_pairs={{0,16},{2,18},{4,20},{6,22},{8,24},{10,26},{12,28},{14,30},{16,0},... | collective-permute-start | bytes 786440 | tf_op jit(solution)/shard_map/ppermute | solution.py:68
  13.5 22.3 %collective-permute-start.2 = (bf16[1,128,1024]{2,1,0:T(8,128)(2,1)S(1)}, bf16[1,128,1024]{2,1,0:T(8,128)(2,1)S(1)}, u32[]{:S(2)}, u32[]{:S(2)}) collective-permute-start(bf16[1,128,1024]{2,1,0:T(8,128)(2,1)S(1)} %bitcast_multiply_fusion), channel_id=1, source_target_pairs={{0,8},{2,10},{4,12},{6,14},{8,16},{10,18},{12,20},{14,22},{16,24},... | collective-permute-start | bytes 786440 | tf_op jit(solution)/shard_map/ppermute | solution.py:68
  15.0 21.0 %copy-start.7 = (bf16[5,128,1024]{2,1,0:T(8,128)(2,1)}, bf16[5,128,1024]{2,1,0:T(8,128)(2,1)S(1)}, u32[]{:S(2)}) copy-start(bf16[5,128,1024]{2,1,0:T(8,128)(2,1)S(1)} %fusion.1.own_ref) | copy-start | bytes 3932164
  15.0 28.4 %collective-permute-start.1 = (bf16[5,128,1024]{2,1,0:T(8,128)(2,1)S(1)}, bf16[5,128,1024]{2,1,0:T(8,128)(2,1)}, u32[]{:S(2)}, u32[]{:S(2)}) collective-permute-start(bf16[5,128,1024]{2,1,0:T(8,128)(2,1)S(1)} %fusion.1.own_ref), channel_id=1, source_target_pairs={{0,1},{1,0},{2,3},{3,2},{4,5},{5,4},{6,7},{7,6},{8,9},{9,8},{10,11... | collective-permute-start | bytes 3932168 | tf_op jit(solution)/shard_map/ppermute | solution.py:415
  17.2 22.4 %copy-start.22 = (s32[15,4,8]{0,2,1:T(8,128)S(1)}, s32[15,4,8]{0,2,1:T(8,128)}, u32[]{:S(2)}) copy-start(s32[15,4,8]{0,2,1:T(8,128)} %param.9) | copy-start | bytes 5764
  17.2 25.5 %copy-start.23 = (s32[4,8]{1,0:T(4,128)S(1)}, s32[4,8]{1,0:T(4,128)}, u32[]{:S(2)}) copy-start(s32[4,8]{1,0:T(4,128)} %node_ref.1) | copy-start | bytes 388
  17.2 25.7 %copy-start.24 = (s32[15]{0:T(128)S(1)}, s32[15]{0:T(128)}, u32[]{:S(2)}) copy-start(s32[15]{0:T(128)} %parent_ref.1) | copy-start | bytes 184
  17.2 58.4 %collective-permute-start = (bf16[128,1024]{1,0:T(8,128)(2,1)}, bf16[128,1024]{1,0:T(8,128)(2,1)}, u32[]{:S(2)}, u32[]{:S(2)}) collective-permute-start(bf16[128,1024]{1,0:T(8,128)(2,1)} %fusion), channel_id=1, source_target_pairs={{0,1},{1,0},{2,3},{3,2},{4,5},{5,4},{6,7},{7,6},{8,9},{9,8},{10,11... | collective-permute-start | bytes 786440 | tf_op jit(solution)/shard_map/ppermute | solution.py:42
  35.9 40.8 %copy-start.2 = (bf16[4,1,128,1024]{3,2,1,0:T(8,128)(2,1)}, bf16[4,1,128,1024]{3,2,1,0:T(8,128)(2,1)S(1)}, u32[]{:S(2)}) copy-start(bf16[4,1,128,1024]{3,2,1,0:T(8,128)(2,1)S(1)} %pad_maximum_fusion.2.refs_3_) | copy-start | bytes 3145732
  36.0 25.3 %collective-permute-start.12 = (bf16[4,1,128,1024]{3,2,1,0:T(8,128)(2,1)S(1)}, bf16[4,1,128,1024]{3,2,1,0:T(8,128)(2,1)S(1)}, u32[]{:S(2)}, u32[]{:S(2)}) collective-permute-start(bf16[4,1,128,1024]{3,2,1,0:T(8,128)(2,1)S(1)} %pad_maximum_fusion.2.refs_3_), channel_id=1, source_target_pairs={{0,4},{1,3},{2,6},{3,1},{4,0},{5,7},{6,2},{7,5},{8,12},{9,11},{10,... | collective-permute-start | bytes 3145736 | tf_op jit(solution)/shard_map/ppermute | solution.py:62
  37.5 23.7 %collective-permute-start.11 = (bf16[4,1,128,1024]{3,2,1,0:T(8,128)(2,1)S(1)}, bf16[4,1,128,1024]{3,2,1,0:T(8,128)(2,1)}, u32[]{:S(2)}, u32[]{:S(2)}) collective-permute-start(bf16[4,1,128,1024]{3,2,1,0:T(8,128)(2,1)S(1)} %pad_maximum_fusion.2.refs_3_), channel_id=1, source_target_pairs={{0,2},{1,5},{2,0},{3,7},{4,6},{5,1},{6,4},{7,3},{8,10},{9,13},{10,... | collective-permute-start | bytes 3145736 | tf_op jit(solution)/shard_map/ppermute | solution.py:62
  46.4 16.5 %collective-permute-start.8 = (bf16[128,1536]{1,0:T(8,128)(2,1)}, bf16[128,1536]{1,0:T(8,128)(2,1)S(1)}, u32[]{:S(2)}, u32[]{:S(2)}) collective-permute-start(bf16[128,1536]{1,0:T(8,128)(2,1)} %get-tuple-element.46), channel_id=1, source_target_pairs={{8,0},{10,2},{12,4},{14,6},{16,8},{18,10},{20,12},{22,14},{24,16},... | collective-permute-start | bytes 1179656 | tf_op jit(solution)/shard_map/ppermute | solution.py:98
  47.7 16.5 %collective-permute-start.5 = (bf16[128,1536]{1,0:T(8,128)(2,1)}, bf16[128,1536]{1,0:T(8,128)(2,1)S(1)}, u32[]{:S(2)}, u32[]{:S(2)}) collective-permute-start(bf16[128,1536]{1,0:T(8,128)(2,1)} %get-tuple-element.46), channel_id=1, source_target_pairs={{0,8},{2,10},{4,12},{6,14},{8,16},{10,18},{12,20},{14,22},{16,24},... | collective-permute-start | bytes 1179656 | tf_op jit(solution)/shard_map/ppermute | solution.py:97
  61.3 22.3 %copy-start.4 = (bf16[4,1,128,1024]{3,2,1,0:T(8,128)(2,1)}, bf16[4,1,128,1024]{3,2,1,0:T(8,128)(2,1)S(1)}, u32[]{:S(2)}) copy-start(bf16[4,1,128,1024]{3,2,1,0:T(8,128)(2,1)S(1)} %collective-permute-done.12.refs_5_) | copy-start | bytes 3145732
  61.3 22.3 %collective-permute-start.13 = (bf16[4,1,128,1024]{3,2,1,0:T(8,128)(2,1)}, bf16[4,1,128,1024]{3,2,1,0:T(8,128)(2,1)}, u32[]{:S(2)}, u32[]{:S(2)}) collective-permute-start(bf16[4,1,128,1024]{3,2,1,0:T(8,128)(2,1)} %collective-permute-done.11.refs_4_), channel_id=1, source_target_pairs={{0,4},{1,3},{2,6},{3,1},{4,0},{5,7},{6,2},{7,5},{8,12},{9,11},{10,... | collective-permute-start | bytes 3145736 | tf_op jit(solution)/shard_map/ppermute | solution.py:62
  62.9 10.7 %collective-permute-start.9 = (bf16[128,1536]{1,0:T(8,128)(2,1)S(1)}, bf16[128,1536]{1,0:T(8,128)(2,1)S(1)}, u32[]{:S(2)}, u32[]{:S(2)}) collective-permute-start(bf16[128,1536]{1,0:T(8,128)(2,1)S(1)} %collective-permute-done.8), channel_id=1, source_target_pairs={{8,0},{10,2},{12,4},{14,6},{16,8},{18,10},{20,12},{22,14},{9,1},{1... | collective-permute-start | bytes 1179656 | tf_op jit(solution)/shard_map/ppermute | solution.py:98
  64.2 10.7 %collective-permute-start.6 = (bf16[128,1536]{1,0:T(8,128)(2,1)S(1)}, bf16[128,1536]{1,0:T(8,128)(2,1)}, u32[]{:S(2)}, u32[]{:S(2)}) collective-permute-start(bf16[128,1536]{1,0:T(8,128)(2,1)S(1)} %collective-permute-done.5), channel_id=1, source_target_pairs={{8,16},{10,18},{12,20},{14,22},{16,24},{18,26},{20,28},{22,30},{9,... | collective-permute-start | bytes 1179656 | tf_op jit(solution)/shard_map/ppermute | solution.py:97
  73.6 9.9 %collective-permute-start.10 = (bf16[128,1536]{1,0:T(8,128)(2,1)S(1)}, bf16[128,1536]{1,0:T(8,128)(2,1)S(1)}, u32[]{:S(2)}, u32[]{:S(2)}) collective-permute-start(bf16[128,1536]{1,0:T(8,128)(2,1)S(1)} %collective-permute-done.9), channel_id=1, source_target_pairs={{8,0},{10,2},{12,4},{14,6},{9,1},{11,3},{13,5},{15,7}} | collective-permute-start | bytes 1179656 | tf_op jit(solution)/shard_map/ppermute | solution.py:98
  74.9 8.6 %collective-permute-start.7 = (bf16[128,1536]{1,0:T(8,128)(2,1)}, bf16[128,1536]{1,0:T(8,128)(2,1)S(1)}, u32[]{:S(2)}, u32[]{:S(2)}) collective-permute-start(bf16[128,1536]{1,0:T(8,128)(2,1)} %collective-permute-done.6), channel_id=1, source_target_pairs={{16,24},{18,26},{20,28},{22,30},{17,25},{19,27},{21,29},{23,31}} | collective-permute-start | bytes 1179656 | tf_op jit(solution)/shard_map/ppermute | solution.py:97
  88.4 1.0 copy-start.16
  89.4 5.8 %copy-start.14 = (bf16[128,1792]{1,0:T(8,128)(2,1)S(1)}, bf16[128,1792]{1,0:T(8,128)(2,1)}, u32[]{:S(2)}) copy-start(bf16[128,1792]{1,0:T(8,128)(2,1)} %get-tuple-element.61) | copy-start | bytes 1376260
  89.4 12.5 %copy-start.9 = (bf16[1,128,1024]{2,1,0:T(8,128)(2,1)S(1)}, bf16[1,128,1024]{2,1,0:T(8,128)(2,1)}, u32[]{:S(2)}) copy-start(bf16[1,128,1024]{2,1,0:T(8,128)(2,1)} %shard_map.57.own_ref) | copy-start | bytes 786436
  89.6 56.4 %copy-start.1 = (bf16[4,128,1536]{2,1,0:T(8,128)(2,1)}, bf16[4,128,1536]{2,1,0:T(8,128)(2,1)S(1)}, u32[]{:S(2)}) copy-start(bf16[4,128,1536]{2,1,0:T(8,128)(2,1)S(1)} %pad_maximum_fusion.1.refs_4_.refs_1_) | copy-start | bytes 4718596
  89.6 41.0 %collective-permute-start.16 = (bf16[4,128,1536]{2,1,0:T(8,128)(2,1)S(1)}, bf16[4,128,1536]{2,1,0:T(8,128)(2,1)S(1)}, u32[]{:S(2)}, u32[]{:S(2)}) collective-permute-start(bf16[4,128,1536]{2,1,0:T(8,128)(2,1)S(1)} %pad_maximum_fusion.1.refs_4_.refs_1_), channel_id=1, source_target_pairs={{0,4},{1,3},{2,6},{3,1},{4,0},{5,7},{6,2},{7,5},{8,12},{9,11},{10,... | collective-permute-start | bytes 4718600 | tf_op jit(solution)/shard_map/ppermute | solution.py:62
  92.2 38.4 %collective-permute-start.15 = (bf16[4,128,1536]{2,1,0:T(8,128)(2,1)S(1)}, bf16[4,128,1536]{2,1,0:T(8,128)(2,1)}, u32[]{:S(2)}, u32[]{:S(2)}) collective-permute-start(bf16[4,128,1536]{2,1,0:T(8,128)(2,1)S(1)} %pad_maximum_fusion.1.refs_4_.refs_1_), channel_id=1, source_target_pairs={{0,2},{1,5},{2,0},{3,7},{4,6},{5,1},{6,4},{7,3},{8,10},{9,13},{10,... | collective-permute-start | bytes 4718600 | tf_op jit(solution)/shard_map/ppermute | solution.py:62
  95.2 12.2 %collective-permute-start.22 = (bf16[128,1792]{1,0:T(8,128)(2,1)S(1)}, bf16[128,1792]{1,0:T(8,128)(2,1)}, u32[]{:S(2)}, u32[]{:S(2)}) collective-permute-start(bf16[128,1792]{1,0:T(8,128)(2,1)S(1)} %copy-done.14), channel_id=1, source_target_pairs={{8,0},{10,2},{12,4},{14,6},{16,8},{18,10},{20,12},{22,14},{24,16},... | collective-permute-start | bytes 1376264 | tf_op jit(solution)/shard_map/ppermute | solution.py:98
  96.5 12.2 %collective-permute-start.19 = (bf16[128,1792]{1,0:T(8,128)(2,1)S(1)}, bf16[128,1792]{1,0:T(8,128)(2,1)}, u32[]{:S(2)}, u32[]{:S(2)}) collective-permute-start(bf16[128,1792]{1,0:T(8,128)(2,1)S(1)} %copy-done.14), channel_id=1, source_target_pairs={{0,8},{2,10},{4,12},{6,14},{8,16},{10,18},{12,20},{14,22},{16,24},... | collective-permute-start | bytes 1376264 | tf_op jit(solution)/shard_map/ppermute | solution.py:97
  101.8 8.4 %collective-permute-start.14 = (bf16[1,128,1024]{2,1,0:T(8,128)(2,1)S(1)}, bf16[1,128,1024]{2,1,0:T(8,128)(2,1)S(1)}, u32[]{:S(2)}, u32[]{:S(2)}) collective-permute-start(bf16[1,128,1024]{2,1,0:T(8,128)(2,1)S(1)} %copy-done.9), channel_id=1, source_target_pairs={{0,1},{1,0},{2,3},{3,2},{4,5},{5,4},{6,7},{7,6},{8,9},{9,8},{10,11... | collective-permute-start | bytes 786440 | tf_op jit(solution)/shard_map/ppermute | solution.py:267
  107.4 14.5 %collective-permute-start.23 = (bf16[128,1792]{1,0:T(8,128)(2,1)}, bf16[128,1792]{1,0:T(8,128)(2,1)}, u32[]{:S(2)}, u32[]{:S(2)}) collective-permute-start(bf16[128,1792]{1,0:T(8,128)(2,1)} %collective-permute-done.22), channel_id=1, source_target_pairs={{8,0},{10,2},{12,4},{14,6},{16,8},{18,10},{20,12},{22,14},{9,1},{1... | collective-permute-start | bytes 1376264 | tf_op jit(solution)/shard_map/ppermute | solution.py:98
  108.7 14.5 %collective-permute-start.20 = (bf16[128,1792]{1,0:T(8,128)(2,1)}, bf16[128,1792]{1,0:T(8,128)(2,1)}, u32[]{:S(2)}, u32[]{:S(2)}) collective-permute-start(bf16[128,1792]{1,0:T(8,128)(2,1)} %collective-permute-done.19), channel_id=1, source_target_pairs={{8,16},{10,18},{12,20},{14,22},{16,24},{18,26},{20,28},{22,30},{9,... | collective-permute-start | bytes 1376264 | tf_op jit(solution)/shard_map/ppermute | solution.py:97
  110.2 0.7 copy-start.17
  112.9 17.6 %all-to-all-start = ((bf16[16,1,64,128]{3,2,1,0:T(8,128)(2,1)}), bf16[16,1,64,128]{3,2,1,0:T(8,128)(2,1)S(1)}, u32[]{:S(2)}, u32[]{:S(2)}) async-start(bf16[16,1,64,128]{3,2,1,0:T(8,128)(2,1)} %get-tuple-element.45), calls=%async_computation | async-start | bytes 524288 | tf_op jit(solution)/shard_map/all_to_all | solution.py:748
  122.0 14.6 %collective-permute-start.24 = (bf16[128,1792]{1,0:T(8,128)(2,1)}, bf16[128,1792]{1,0:T(8,128)(2,1)}, u32[]{:S(2)}, u32[]{:S(2)}) collective-permute-start(bf16[128,1792]{1,0:T(8,128)(2,1)} %collective-permute-done.23), channel_id=1, source_target_pairs={{8,0},{10,2},{12,4},{14,6},{9,1},{11,3},{13,5},{15,7}} | collective-permute-start | bytes 1376264 | tf_op jit(solution)/shard_map/ppermute | solution.py:98
  123.3 13.3 %collective-permute-start.21 = (bf16[128,1792]{1,0:T(8,128)(2,1)}, bf16[128,1792]{1,0:T(8,128)(2,1)}, u32[]{:S(2)}, u32[]{:S(2)}) collective-permute-start(bf16[128,1792]{1,0:T(8,128)(2,1)} %collective-permute-done.20), channel_id=1, source_target_pairs={{16,24},{18,26},{20,28},{22,30},{17,25},{19,27},{21,29},{23,31}} | collective-permute-start | bytes 1376264 | tf_op jit(solution)/shard_map/ppermute | solution.py:97
  130.5 7.6 %copy-start.8 = (bf16[16,1,64,128]{3,2,1,0:T(8,128)(2,1)}, bf16[16,1,64,128]{3,2,1,0:T(8,128)(2,1)S(1)}, u32[]{:S(2)}) copy-start(bf16[16,1,64,128]{3,2,1,0:T(8,128)(2,1)S(1)} %all-to-all-done.own_ref) | copy-start | bytes 786436
  130.6 15.5 %copy-start.3 = (bf16[4,128,1536]{2,1,0:T(8,128)(2,1)}, bf16[4,128,1536]{2,1,0:T(8,128)(2,1)S(1)}, u32[]{:S(2)}) copy-start(bf16[4,128,1536]{2,1,0:T(8,128)(2,1)S(1)} %collective-permute-done.16.refs_6_.refs_3_) | copy-start | bytes 4718596
  130.6 7.6 %collective-permute-start.17 = (bf16[16,1,64,128]{3,2,1,0:T(8,128)(2,1)S(1)}, bf16[16,1,64,128]{3,2,1,0:T(8,128)(2,1)S(1)}, u32[]{:S(2)}, u32[]{:S(2)}) collective-permute-start(bf16[16,1,64,128]{3,2,1,0:T(8,128)(2,1)S(1)} %all-to-all-done.own_ref), channel_id=1, source_target_pairs={{0,1},{1,0},{2,3},{3,2},{4,5},{5,4},{6,7},{7,6},{8,9},{9,8},{10,11... | collective-permute-start | bytes 786440 | tf_op jit(solution)/shard_map/ppermute | solution.py:301
  136.5 26.1 %collective-permute-start.25 = (bf16[4,128,1536]{2,1,0:T(8,128)(2,1)}, bf16[4,128,1536]{2,1,0:T(8,128)(2,1)}, u32[]{:S(2)}, u32[]{:S(2)}) collective-permute-start(bf16[4,128,1536]{2,1,0:T(8,128)(2,1)} %collective-permute-done.15.refs_5_.refs_2_), channel_id=1, source_target_pairs={{0,4},{1,3},{2,6},{3,1},{4,0},{5,7},{6,2},{7,5},{8,12},{9,11},{10,... | collective-permute-start | bytes 4718600 | tf_op jit(solution)/shard_map/ppermute | solution.py:62
  138.1 0.7 copy-start.19
  147.1 2.2 copy-start.15
  149.4 3.4 %copy-start.18 = (bf16[128,1024]{1,0:T(8,128)(2,1)S(1)}, bf16[128,1024]{1,0:T(8,128)(2,1)}, u32[]{:S(2)}) copy-start(bf16[128,1024]{1,0:T(8,128)(2,1)} %get-tuple-element.54) | copy-start | bytes 786436
  150.8 51.0 %collective-permute-start.28 = (bf16[4,128,1792]{2,1,0:T(8,128)(2,1)}, bf16[4,128,1792]{2,1,0:T(8,128)(2,1)}, u32[]{:S(2)}, u32[]{:S(2)}) collective-permute-start(bf16[4,128,1792]{2,1,0:T(8,128)(2,1)} %pad_maximum_fusion.refs_7_.refs_1_), channel_id=1, source_target_pairs={{0,4},{1,3},{2,6},{3,1},{4,0},{5,7},{6,2},{7,5},{8,12},{9,11},{10,... | collective-permute-start | bytes 5505032 | tf_op jit(solution)/shard_map/ppermute | solution.py:62
  151.3 50.6 %collective-permute-start.27 = (bf16[4,128,1792]{2,1,0:T(8,128)(2,1)}, bf16[4,128,1792]{2,1,0:T(8,128)(2,1)}, u32[]{:S(2)}, u32[]{:S(2)}) collective-permute-start(bf16[4,128,1792]{2,1,0:T(8,128)(2,1)} %pad_maximum_fusion.refs_7_.refs_1_), channel_id=1, source_target_pairs={{0,2},{1,5},{2,0},{3,7},{4,6},{5,1},{6,4},{7,3},{8,10},{9,13},{10,... | collective-permute-start | bytes 5505032 | tf_op jit(solution)/shard_map/ppermute | solution.py:62
  152.8 1.5 collective-permute-start.18
  170.5 32.9 %copy-start = (f32[4,128,1024]{2,1,0:T(8,128)S(1)}, f32[4,128,1024]{2,1,0:T(8,128)}, u32[]{:S(2)}) copy-start(f32[4,128,1024]{2,1,0:T(8,128)} %first_ref.1) | copy-start | bytes 6291460
  170.5 2.1 collective-permute-start.26
  172.7 0.8 copy-start.13
  176.3 28.2 %all-to-all-start.1 = ((bf16[16,2,64,128]{3,2,1,0:T(8,128)(2,1)}), bf16[16,2,64,128]{3,2,1,0:T(8,128)(2,1)S(1)}, u32[]{:S(2)}, u32[]{:S(2)}) async-start(bf16[16,2,64,128]{3,2,1,0:T(8,128)(2,1)} %get-tuple-element.59), calls=%async_computation.1 | async-start | bytes 1048576 | tf_op jit(solution)/shard_map/all_to_all | solution.py:748
  201.9 23.5 %collective-permute-start.32 = (bf16[4,128,1792]{2,1,0:T(8,128)(2,1)}, bf16[4,128,1792]{2,1,0:T(8,128)(2,1)}, u32[]{:S(2)}, u32[]{:S(2)}) collective-permute-start(bf16[4,128,1792]{2,1,0:T(8,128)(2,1)} %collective-permute-done.27.refs_8_.refs_2_), channel_id=1, source_target_pairs={{0,4},{1,3},{2,6},{3,1},{4,0},{5,7},{6,2},{7,5},{8,12},{9,11},{10,... | collective-permute-start | bytes 5505032 | tf_op jit(solution)/shard_map/ppermute | solution.py:62
  204.5 2.0 copy-start.6
  204.5 2.0 collective-permute-start.29
  204.5 5.3 %collective-permute-start.36 = (f32[128,1024]{1,0:T(8,128)}, f32[128,1024]{1,0:T(8,128)S(1)}, u32[]{:S(2)}, u32[]{:S(2)}) collective-permute-start(f32[128,1024]{1,0:T(8,128)} %get-tuple-element.89), channel_id=1, source_target_pairs={{0,1},{1,0},{2,3},{3,2},{4,5},{5,4},{6,7},{7,6},{8,9},{9,8},{10,11... | collective-permute-start | bytes 1572872 | tf_op jit(solution)/shard_map/ppermute | solution.py:42
  205.0 4.8 %collective-permute-start.31 = (f32[128,1024]{1,0:T(8,128)}, f32[128,1024]{1,0:T(8,128)S(1)}, u32[]{:S(2)}, u32[]{:S(2)}) collective-permute-start(f32[128,1024]{1,0:T(8,128)} %get-tuple-element.90), channel_id=1, source_target_pairs={{0,1},{1,0},{2,3},{3,2},{4,5},{5,4},{6,7},{7,6},{8,9},{9,8},{10,11... | collective-permute-start | bytes 1572872 | tf_op jit(solution)/shard_map/ppermute | solution.py:42
  206.5 0.8 copy-start.12
  215.3 1.6 collective-permute-start.30
  235.9 2.5 collective-permute-start.33
  238.4 0.9 copy-start.10
  242.7 26.8 %all-to-all-start.2 = ((bf16[16,3,64,128]{3,2,1,0:T(8,128)(2,1)}), bf16[16,3,64,128]{3,2,1,0:T(8,128)(2,1)S(1)}, u32[]{:S(2)}, u32[]{:S(2)}) async-start(bf16[16,3,64,128]{3,2,1,0:T(8,128)(2,1)} %get-tuple-element.72), calls=%async_computation.2 | async-start | bytes 1572864 | tf_op jit(solution)/shard_map/all_to_all | solution.py:748
  269.4 2.3 copy-start.5
  269.4 2.3 collective-permute-start.34
  271.7 0.9 copy-start.11
  281.6 1.6 collective-permute-start.35
  283.2 0.7 copy-start.20
  (1 other events, 0.7 us)

commit v7 on v6

--- a/solution.py
+++ b/solution.py
@@ -736,7 +736,7 @@
                     known.append([by_level[j] for j in range(level)])
             value = product(known, groups, above[:level, level])
             if compact:
-                held_line = lax.optimization_barrier(tuple(second[0] + second[1]) + (value,))
+                held_line = lax.optimization_barrier(tuple(second[0] + second[1]) + (one[-1],))
                 depth = len(second[0])
                 ahead = along_xy(line_pieces(held_line[:depth], held_line[depth:-1], second[2]), None)
                 third = along_line(after(shards[1], ahead[0]), None)

time: 292 us -> 291 us (level)
  starting transfers between devices: 69.2 us -> 62.2 us
  waiting for transfers between devices: 110 us -> 117 us
    ppermute x6, waiting for transfers between devices: 23.5 us -> 29.7 us  [along_line(): lax.ppermute(down, 'wide', [(i, i - 4) for i in range(4, wide - 4 * (hop...]
    all_to_all x3, starting transfers between devices: 24.1 us -> 19.5 us  [local(): got = lax.all_to_all(slots, 'wide', split_axis=0, concat_axis=0, tiled=True)]
    all_to_all x3, waiting for transfers between devices: 19.8 us -> 15.6 us  [local(): got = lax.all_to_all(slots, 'wide', split_axis=0, concat_axis=0, tiled=True)]
    ppermute x3, waiting for transfers between devices: 18.4 us -> 21.6 us  [shifts(): lax.ppermute(value, 'wide', [(i, (i + 4 * hop) % wide) for i in range(wid...]
  transfers between devices with their start and end apart: 40 -> 40, of which waited for: 19 -> 19; matrix products, arithmetic and copies ran while one was open for 7% -> 7% of each run, Pallas kernels for 14% -> 16%
where the time goes in v7:
time: 291 us; the launch traced here: 289 us
  waiting for transfers between devices  117 us (40%)
  Pallas kernels  75.6 us (26%)
  starting transfers between devices  62.2 us (21%)
  local copies, waits for them, and re-layouts  18.9 us (6%)
  other arithmetic  12.8 us (4%)
    ppermute x9, waiting for transfers between devices, swap(): return lax.ppermute(value, ('wide', 'narrow'), pairs)  40.6 us
    ppermute x6, waiting for transfers between devices, along_line(): lax.ppermute(down, 'wide', [(i, i - 4) for i in range(4, wide - 4 * (hop...  29.7 us
    pallas_call x4, Pallas kernels, sparse_product(): pl.pallas_call(functools.partial(sparse_body, level, shapes, mirror), gri...  29.6 us
    ppermute x3, waiting for transfers between devices, shifts(): lax.ppermute(value, 'wide', [(i, (i + 4 * hop) % wide) for i in range(wid...  21.6 us
    all_to_all x3, starting transfers between devices, local(): got = lax.all_to_all(slots, 'wide', split_axis=0, concat_axis=0, tiled=True)  19.5 us
    all_to_all x3, waiting for transfers between devices, local(): got = lax.all_to_all(slots, 'wide', split_axis=0, concat_axis=0, tiled=True)  15.6 us
    ppermute x6, starting transfers between devices, along_line(): lax.ppermute(up, 'wide', [(i, i + 4) for i in range(4 * (hop - 1), wide -...  14.2 us
    ppermute x9, starting transfers between devices, swap(): return lax.ppermute(value, ('wide', 'narrow'), pairs)  13.5 us
  transfers between devices with their start and end apart: 40, of which 19 were waited for; matrix products, arithmetic and copies ran while one was open for 7% of the time, Pallas kernels for 16%

profile of v7, /device:TPU:0, one launch (start us, length us, event | category | flops | bytes accessed | tf_op | source)
XLA Modules:
  0.0 289.2 jit_solution(11984994435077864751)
XLA Ops:
  0.0 6.1 %fusion.30 = (bf16[1,128,1,1024]{3,2,1,0:T(2,128)(2,1)S(1)}, bf16[1,128,1,1024]{3,2,1,0:T(2,128)(2,1)S(1)}, bf16[1,128,1,1024]{3,2,1,0:T(2,128)(2,1)S(1)}, bf16[...) fusion(bf16[4,128,4,1024]{3,2,1,0:T(4,128)(2,1)} %param.5), kind=kLoop, calls=%fused_computation.78 | loop fusion | bytes 3145728 | tf_op jit(solution)/shard_map/slice | solution.py:685
  8.0 4.9 %collective-permute-start.4 = (bf16[1,128,1024]{2,1,0:T(8,128)(2,1)S(1)}, bf16[1,128,1024]{2,1,0:T(8,128)(2,1)S(1)}, u32[]{:S(2)}, u32[]{:S(2)}) collective-permute-start(bf16[1,128,1024]{2,1,0:T(8,128)(2,1)S(1)} %bitcast_multiply_fusion), channel_id=1, source_target_pairs={{0,24},{2,26},{4,28},{6,30},{8,0},{10,2},{12,4},{14,6},{16,8},{18,... | collective-permute-start | bytes 786440 | tf_op jit(solution)/shard_map/ppermute | solution.py:68
  14.0 5.6 %collective-permute-done.4 = bf16[1,128,1024]{2,1,0:T(8,128)(2,1)S(1)} collective-permute-done((bf16[1,128,1024]{2,1,0:T(8,128)(2,1)S(1)}, bf16[1,128,1024]{2,1,0:T(8,128)(2,1)S(1)}, u32[]{:S(2)}, u32[]{:S(2)}) %collective-permute-start.4) | collective-permute-done | bytes 262176 | tf_op jit(solution)/shard_map/ppermute | solution.py:68
  19.6 16.0 %collective-permute-done.3 = bf16[1,128,1024]{2,1,0:T(8,128)(2,1)S(1)} collective-permute-done((bf16[1,128,1024]{2,1,0:T(8,128)(2,1)S(1)}, bf16[1,128,1024]{2,1,0:T(8,128)(2,1)S(1)}, u32[]{:S(2)}, u32[]{:S(2)}) %collective-permute-start.3) | collective-permute-done | bytes 262176 | tf_op jit(solution)/shard_map/ppermute | solution.py:68
  35.8 1.6 collective-permute-start.12
  37.4 1.5 collective-permute-start.11
  40.2 2.4 shard_map.55.table_ref
  42.6 3.0 %shard_map.56 = (bf16[128,1536]{1,0:T(8,128)(2,1)}, bf16[128,1792]{1,0:T(8,128)(2,1)}) custom-call(s32[1]{0:T(128)} %bitcast.id_ref, s32[128]{0:T(128)} %shard_map.55.table_ref, bf16[5,128,1024]{2,1,0:T(8,128)(2,1)} %copy-done.8, bf16[5,128,1024]{2,1,0:T(8,128)(2,1)} %collective-permute-done.1.other_ref), custom_call_target="tpu_custom_call" | custom-call | flops 1 | bytes 1 | tf_op jit(solution)/shard_map/pallas_call | solution.py:418
  45.7 1.3 collective-permute-start.8
  47.0 4.6 %collective-permute-start.5 = (bf16[128,1536]{1,0:T(8,128)(2,1)}, bf16[128,1536]{1,0:T(8,128)(2,1)S(1)}, u32[]{:S(2)}, u32[]{:S(2)}) collective-permute-start(bf16[128,1536]{1,0:T(8,128)(2,1)} %get-tuple-element.46), channel_id=1, source_target_pairs={{0,8},{2,10},{4,12},{6,14},{8,16},{10,18},{12,20},{14,22},{16,24},... | collective-permute-start | bytes 1179656 | tf_op jit(solution)/shard_map/ppermute | solution.py:97
  51.5 1.8 fusion
  53.3 8.3 %collective-permute-done.12.refs_5_ = bf16[4,1,128,1024]{3,2,1,0:T(8,128)(2,1)S(1)} collective-permute-done((bf16[4,1,128,1024]{3,2,1,0:T(8,128)(2,1)S(1)}, bf16[4,1,128,1024]{3,2,1,0:T(8,128)(2,1)S(1)}, u32[]{:S(2)}, u32[]{:S(2)}) %collective-permute-start.12) | collective-permute-done | bytes 1048608 | tf_op jit(solution)/shard_map/ppermute | solution.py:62
  61.6 1.5 collective-permute-start.13
  63.3 1.3 collective-permute-start.9
  65.7 8.8 %collective-permute-done.9 = bf16[128,1536]{1,0:T(8,128)(2,1)S(1)} collective-permute-done((bf16[128,1536]{1,0:T(8,128)(2,1)S(1)}, bf16[128,1536]{1,0:T(8,128)(2,1)S(1)}, u32[]{:S(2)}, u32[]{:S(2)}) %collective-permute-start.9) | collective-permute-done | bytes 393248 | tf_op jit(solution)/shard_map/ppermute | solution.py:98
  74.5 1.3 collective-permute-start.10
  77.0 7.8 %collective-permute-done.10 = bf16[128,1536]{1,0:T(8,128)(2,1)S(1)} collective-permute-done((bf16[128,1536]{1,0:T(8,128)(2,1)S(1)}, bf16[128,1536]{1,0:T(8,128)(2,1)S(1)}, u32[]{:S(2)}, u32[]{:S(2)}) %collective-permute-start.10) | collective-permute-done | bytes 393248 | tf_op jit(solution)/shard_map/ppermute | solution.py:98
  85.2 2.6 collective-permute-start.16
  87.8 3.1 %collective-permute-start.15 = (bf16[4,128,1536]{2,1,0:T(8,128)(2,1)S(1)}, bf16[4,128,1536]{2,1,0:T(8,128)(2,1)}, u32[]{:S(2)}, u32[]{:S(2)}) collective-permute-start(bf16[4,128,1536]{2,1,0:T(8,128)(2,1)S(1)} %pad_maximum_fusion.1.refs_4_.refs_1_), channel_id=1, source_target_pairs={{0,2},{1,5},{2,0},{3,7},{4,6},{5,1},{6,4},{7,3},{8,10},{9,13},{10,... | collective-permute-start | bytes 4718600 | tf_op jit(solution)/shard_map/ppermute | solution.py:62
  92.2 1.3 collective-permute-start.22
  93.5 5.3 %collective-permute-start.19 = (bf16[128,1792]{1,0:T(8,128)(2,1)}, bf16[128,1792]{1,0:T(8,128)(2,1)}, u32[]{:S(2)}, u32[]{:S(2)}) collective-permute-start(bf16[128,1792]{1,0:T(8,128)(2,1)} %get-tuple-element.61), channel_id=1, source_target_pairs={{0,8},{2,10},{4,12},{6,14},{8,16},{10,18},{12,20},{14,22},{16,24},... | collective-permute-start | bytes 1376264 | tf_op jit(solution)/shard_map/ppermute | solution.py:97
  98.9 1.2 broadcast_select_fusion.7
  100.9 4.8 %shard_map.57.own_ref = bf16[1,128,1024]{2,1,0:T(8,128)(2,1)} custom-call(s32[1,16]{1,0:T(1,128)} %add.73.refs_0_, s32[1,4]{1,0:T(1,128)} %fusion.25.refs_1_, bf16[128,2048]{1,0:T(8,128)(2,1)} %pad_maximum_fusion.5.refs_2_.refs_0_, bf16[4,1,128,1024]{3,2,1,0:T(8,128)(2,1)} %copy-done.2, bf16[4,1,128,1024]{3,2,1,0:T(8,128)(2,1)} %collective-permute-done.11.refs_4_, ...), custom_call_target="tpu_custom_call" | custom-call | flops 1 | bytes 1 | tf_op jit(solution)/shard_map/pallas_call | solution.py:228
  105.8 1.3 collective-permute-start.23
  107.1 1.4 collective-permute-start.20
  109.3 2.0 shard_map.58
  111.3 6.1 %all-to-all-start = ((bf16[16,1,64,128]{3,2,1,0:T(8,128)(2,1)}), bf16[16,1,64,128]{3,2,1,0:T(8,128)(2,1)S(1)}, u32[]{:S(2)}, u32[]{:S(2)}) async-start(bf16[16,1,64,128]{3,2,1,0:T(8,128)(2,1)} %get-tuple-element.45), calls=%async_computation | async-start | bytes 524288 | tf_op jit(solution)/shard_map/all_to_all | solution.py:748
  117.4 5.4 %collective-permute-done.23 = bf16[128,1792]{1,0:T(8,128)(2,1)} collective-permute-done((bf16[128,1792]{1,0:T(8,128)(2,1)}, bf16[128,1792]{1,0:T(8,128)(2,1)}, u32[]{:S(2)}, u32[]{:S(2)}) %collective-permute-start.23) | collective-permute-done | bytes 458784 | tf_op jit(solution)/shard_map/ppermute | solution.py:98
  122.8 1.3 collective-permute-start.24
  124.1 1.5 collective-permute-start.21
  125.8 1.4 all-to-all-done.own_ref
  128.0 7.6 %collective-permute-done.24 = bf16[128,1792]{1,0:T(8,128)(2,1)} collective-permute-done((bf16[128,1792]{1,0:T(8,128)(2,1)}, bf16[128,1792]{1,0:T(8,128)(2,1)}, u32[]{:S(2)}, u32[]{:S(2)}) %collective-permute-start.24) | collective-permute-done | bytes 458784 | tf_op jit(solution)/shard_map/ppermute | solution.py:98
  137.0 2.0 shard_map.59.refs_1_.refs_3_
  139.1 5.1 %shard_map.60 = (f32[128,1024]{1,0:T(8,128)}, bf16[128,1024]{1,0:T(8,128)(2,1)}) custom-call(s32[1,16]{1,0:T(1,128)} %add.73.refs_0_, s32[1,4]{1,0:T(1,128)} %slice_convert_fusion.1.refs_1_, bf16[128,2048]{1,0:T(8,128)(2,1)} %bitcast.103, bf16[4,1,128,1024]{3,2,1,0:T(8,128)(2,1)} %copy-done.2, bf16[4,1,128,1024]{3,2,1,0:T(8,128)(2,1)} %collective-permute-done.11.refs_4_, ...), custom_call_target="tpu_custom_call" | custom-call | flops 1 | bytes 1 | tf_op jit(solution)/shard_map/pallas_call | solution.py:228
  144.2 1.1 select_bitcast_fusion.2
  145.3 1.1 select_bitcast_fusion.1
  146.5 1.1 select_bitcast_fusion
  147.6 1.5 pad_maximum_fusion.refs_7_.refs_1_
  149.0 1.3 collective-permute-start.28
  153.2 8.3 %collective-permute-done.25.refs_7_.refs_4_ = bf16[4,128,1536]{2,1,0:T(8,128)(2,1)S(1)} collective-permute-done((bf16[4,128,1536]{2,1,0:T(8,128)(2,1)}, bf16[4,128,1536]{2,1,0:T(8,128)(2,1)S(1)}, u32[]{:S(2)}, u32[]{:S(2)}) %collective-permute-start.25) | collective-permute-done | bytes 1572896 | tf_op jit(solution)/shard_map/ppermute | solution.py:62
  161.5 1.2 copy-done.4
  162.7 7.9 %shard_map.61.own_ref = bf16[2,128,1024]{2,1,0:T(8,128)(2,1)} custom-call(s32[128]{0:T(128)} %shard_map.55.table_ref, s32[16]{0:T(128)} %add.72.place_ref, bf16[128,2048]{1,0:T(8,128)(2,1)} %pad_maximum_fusion.5.refs_2_.refs_0_, bf16[1,128,2048]{2,1,0:T(8,128)(2,1)} %shard_map.59.refs_1_.refs_3_, bf16[128,2048]{1,0:T(8,128)(2,1)} %pad_maximum_fusion.6.refs_2_, ...), custom_call_target="tpu_custom_call" | custom-call | flops 1 | bytes 1 | tf_op jit(solution)/shard_map/pallas_call | solution.py:497
  170.6 2.1 collective-permute-done.26.other_ref
  173.6 2.8 shard_map.62
  176.3 6.6 %all-to-all-start.1 = ((bf16[16,2,64,128]{3,2,1,0:T(8,128)(2,1)}), bf16[16,2,64,128]{3,2,1,0:T(8,128)(2,1)S(1)}, u32[]{:S(2)}, u32[]{:S(2)}) async-start(bf16[16,2,64,128]{3,2,1,0:T(8,128)(2,1)} %get-tuple-element.59), calls=%async_computation.1 | async-start | bytes 1048576 | tf_op jit(solution)/shard_map/all_to_all | solution.py:748
  183.0 17.9 %collective-permute-done.28.refs_9_.refs_3_ = bf16[4,128,1792]{2,1,0:T(8,128)(2,1)} collective-permute-done((bf16[4,128,1792]{2,1,0:T(8,128)(2,1)}, bf16[4,128,1792]{2,1,0:T(8,128)(2,1)}, u32[]{:S(2)}, u32[]{:S(2)}) %collective-permute-start.28) | collective-permute-done | bytes 1835040 | tf_op jit(solution)/shard_map/ppermute | solution.py:62
  201.6 1.1 slice_bitcast_fusion
  203.3 1.4 collective-permute-done.29.other_ref
  205.5 2.5 shard_map.63.refs_0_.refs_3_.refs_4_
  208.2 5.3 %shard_map.64.own_ref = f32[128,256]{1,0:T(8,128)} custom-call(s32[128]{0:T(128)} %shard_map.55.table_ref, s32[16]{0:T(128)} %add.72.place_ref, bf16[2,128,2048]{2,1,0:T(8,128)(2,1)} %shard_map.63.refs_0_.refs_3_.refs_4_, bf16[4,128,1536]{2,1,0:T(8,128)(2,1)} %copy-done.1, bf16[4,128,1536]{2,1,0:T(8,128)(2,1)} %collective-permute-done.15.refs_5_.refs_2_, ...), custom_call_target="tpu_custom_call" | custom-call | flops 1 | bytes 1 | tf_op jit(solution)/shard_map/pallas_call | solution.py:497
  215.7 2.6 shard_map.65
  218.4 6.1 %collective-permute-done.32.refs_10_.refs_4_ = bf16[4,128,1792]{2,1,0:T(8,128)(2,1)} collective-permute-done((bf16[4,128,1792]{2,1,0:T(8,128)(2,1)}, bf16[4,128,1792]{2,1,0:T(8,128)(2,1)}, u32[]{:S(2)}, u32[]{:S(2)}) %collective-permute-start.32) | collective-permute-done | bytes 1835040 | tf_op jit(solution)/shard_map/ppermute | solution.py:62
  224.5 10.4 %shard_map.66.own_ref = bf16[3,128,1024]{2,1,0:T(8,128)(2,1)} custom-call(s32[128]{0:T(128)} %shard_map.55.table_ref, s32[16]{0:T(128)} %add.72.place_ref, bf16[128,2048]{1,0:T(8,128)(2,1)} %pad_maximum_fusion.5.refs_2_.refs_0_, bf16[1,128,2048]{2,1,0:T(8,128)(2,1)} %shard_map.59.refs_1_.refs_3_, bf16[128,2048]{1,0:T(8,128)(2,1)} %pad_maximum_fusion.6.refs_2_, ...), custom_call_target="tpu_custom_call" | custom-call | flops 1 | bytes 1 | tf_op jit(solution)/shard_map/pallas_call | solution.py:497
  234.9 2.5 collective-permute-done.33.other_ref
  238.3 3.4 %shard_map.67 = (bf16[16,3,64,128]{3,2,1,0:T(8,128)(2,1)}, bf16[3,128,2048]{2,1,0:T(8,128)(2,1)}) custom-call(s32[1]{0:T(128)} %bitcast.id_ref, s32[128]{0:T(128)} %shard_map.55.table_ref, bf16[3,128,1024]{2,1,0:T(8,128)(2,1)} %shard_map.66.own_ref, bf16[3,128,1024]{2,1,0:T(8,128)(2,1)} %copy-done.10), custom_call_target="tpu_custom_call" | custom-call | flops 1 | bytes 1 | tf_op jit(solution)/shard_map/pallas_call | solution.py:547
  241.7 6.7 %all-to-all-start.2 = ((bf16[16,3,64,128]{3,2,1,0:T(8,128)(2,1)}), bf16[16,3,64,128]{3,2,1,0:T(8,128)(2,1)S(1)}, u32[]{:S(2)}, u32[]{:S(2)}) async-start(bf16[16,3,64,128]{3,2,1,0:T(8,128)(2,1)} %get-tuple-element.72), calls=%async_computation.2 | async-start | bytes 1572864 | tf_op jit(solution)/shard_map/all_to_all | solution.py:748
  248.4 5.9 %shard_map.68.held_ref = f32[4,128,4,1024]{3,2,1,0:T(4,128)} custom-call(s32[1]{0:T(128)} %bitcast.id_ref, f32[4,128,1024]{2,1,0:T(8,128)} %first_ref.1, bf16[1,128,2048]{2,1,0:T(8,128)(2,1)} %get-tuple-element.55.refs_3_.refs_5_.refs_0_, bf16[2,128,2048]{2,1,0:T(8,128)(2,1)} %get-tuple-element.70.refs_6_.refs_1_, ...), custom_call_target="tpu_custom_call" | custom-call | bytes 41943040 | tf_op jit(solution)/shard_map/pallas_call | solution.py:622
  254.3 14.1 %all-to-all-done.2.own_ref = bf16[16,3,64,128]{3,2,1,0:T(8,128)(2,1)S(1)} async-done(((bf16[16,3,64,128]{3,2,1,0:T(8,128)(2,1)}), bf16[16,3,64,128]{3,2,1,0:T(8,128)(2,1)S(1)}, u32[]{:S(2)}, u32[]{:S(2)}) %all-to-all-start.2) | async-done | bytes 786464 | tf_op jit(solution)/shard_map/all_to_all | solution.py:748
  268.4 2.3 collective-permute-done.34.other_ref
  271.6 3.0 %shard_map.69.refs_0_.turn_ref = bf16[3,128,2048]{2,1,0:T(8,128)(2,1)} custom-call(s32[1]{0:T(128)} %bitcast.id_ref, bf16[16,3,64,128]{3,2,1,0:T(8,128)(2,1)} %copy-done.6, bf16[16,3,64,128]{3,2,1,0:T(8,128)(2,1)} %copy-done.11), custom_call_target="tpu_custom_call" | custom-call | flops 1 | bytes 1 | tf_op jit(solution)/shard_map/pallas_call | solution.py:303
  274.6 5.9 %shard_map.70.own_ref = f32[128,256]{1,0:T(8,128)} custom-call(s32[128]{0:T(128)} %shard_map.55.table_ref, s32[16]{0:T(128)} %add.72.place_ref, bf16[3,128,2048]{2,1,0:T(8,128)(2,1)} %shard_map.69.refs_0_.turn_ref, bf16[4,128,1792]{2,1,0:T(8,128)(2,1)} %pad_maximum_fusion.refs_7_.refs_1_, bf16[4,128,1792]{2,1,0:T(8,128)(2,1)} %collective-permute-done.27.refs_8_.refs_2_, ...), custom_call_target="tpu_custom_call" | custom-call | flops 1 | bytes 1 | tf_op jit(solution)/shard_map/pallas_call | solution.py:497
  280.7 1.1 pad_maximum_fusion.4.diag_ref
  282.8 2.6 shard_map.71
  285.4 3.8 %shard_map.72 = f32[4,128,4,1024]{3,2,1,0:T(4,128)} custom-call(s32[1]{0:T(128)} %bitcast.id_ref, bf16[3,128,2048]{2,1,0:T(8,128)(2,1)} %shard_map.69.refs_0_.turn_ref, f32[128,1024]{1,0:T(8,128)} %get-tuple-element.76.diag_ref, f32[4,128,4,1024]{3,2,1,0:T(4,128)} %shard_map.68.held_ref), custom_call_target="tpu_custom_call", output_to_operand_aliasing={{}: (3, {})} | custom-call | bytes 1 | tf_op jit(solution)/shard_map/pallas_call | solution.py:639
  (131 shorter events, 23.7 us)
Async XLA Ops:
  6.2 0.9 copy-start.21
  6.2 1.0 copy-start.22
  6.6 29.2 %copy-start.8 = (bf16[5,128,1024]{2,1,0:T(8,128)(2,1)}, bf16[5,128,1024]{2,1,0:T(8,128)(2,1)S(1)}, u32[]{:S(2)}) copy-start(bf16[5,128,1024]{2,1,0:T(8,128)(2,1)S(1)} %fusion.1.own_ref) | copy-start | bytes 3932164
  6.6 36.0 %collective-permute-start.1 = (bf16[5,128,1024]{2,1,0:T(8,128)(2,1)S(1)}, bf16[5,128,1024]{2,1,0:T(8,128)(2,1)}, u32[]{:S(2)}, u32[]{:S(2)}) collective-permute-start(bf16[5,128,1024]{2,1,0:T(8,128)(2,1)S(1)} %fusion.1.own_ref), channel_id=1, source_target_pairs={{0,1},{1,0},{2,3},{3,2},{4,5},{5,4},{6,7},{7,6},{8,9},{9,8},{10,11... | collective-permute-start | bytes 3932168 | tf_op jit(solution)/shard_map/ppermute | solution.py:415
  8.0 11.6 %collective-permute-start.4 = (bf16[1,128,1024]{2,1,0:T(8,128)(2,1)S(1)}, bf16[1,128,1024]{2,1,0:T(8,128)(2,1)S(1)}, u32[]{:S(2)}, u32[]{:S(2)}) collective-permute-start(bf16[1,128,1024]{2,1,0:T(8,128)(2,1)S(1)} %bitcast_multiply_fusion), channel_id=1, source_target_pairs={{0,24},{2,26},{4,28},{6,30},{8,0},{10,2},{12,4},{14,6},{16,8},{18,... | collective-permute-start | bytes 786440 | tf_op jit(solution)/shard_map/ppermute | solution.py:68
  12.9 22.7 %collective-permute-start.3 = (bf16[1,128,1024]{2,1,0:T(8,128)(2,1)S(1)}, bf16[1,128,1024]{2,1,0:T(8,128)(2,1)S(1)}, u32[]{:S(2)}, u32[]{:S(2)}) collective-permute-start(bf16[1,128,1024]{2,1,0:T(8,128)(2,1)S(1)} %bitcast_multiply_fusion), channel_id=1, source_target_pairs={{0,16},{2,18},{4,20},{6,22},{8,24},{10,26},{12,28},{14,30},{16,0},... | collective-permute-start | bytes 786440 | tf_op jit(solution)/shard_map/ppermute | solution.py:68
  12.9 22.7 %collective-permute-start.2 = (bf16[1,128,1024]{2,1,0:T(8,128)(2,1)S(1)}, bf16[1,128,1024]{2,1,0:T(8,128)(2,1)S(1)}, u32[]{:S(2)}, u32[]{:S(2)}) collective-permute-start(bf16[1,128,1024]{2,1,0:T(8,128)(2,1)S(1)} %bitcast_multiply_fusion), channel_id=1, source_target_pairs={{0,8},{2,10},{4,12},{6,14},{8,16},{10,18},{12,20},{14,22},{16,24},... | collective-permute-start | bytes 786440 | tf_op jit(solution)/shard_map/ppermute | solution.py:68
  35.8 17.5 %copy-start.2 = (bf16[4,1,128,1024]{3,2,1,0:T(8,128)(2,1)}, bf16[4,1,128,1024]{3,2,1,0:T(8,128)(2,1)S(1)}, u32[]{:S(2)}) copy-start(bf16[4,1,128,1024]{3,2,1,0:T(8,128)(2,1)S(1)} %pad_maximum_fusion.2.refs_3_) | copy-start | bytes 3145732
  35.8 25.8 %collective-permute-start.12 = (bf16[4,1,128,1024]{3,2,1,0:T(8,128)(2,1)S(1)}, bf16[4,1,128,1024]{3,2,1,0:T(8,128)(2,1)S(1)}, u32[]{:S(2)}, u32[]{:S(2)}) collective-permute-start(bf16[4,1,128,1024]{3,2,1,0:T(8,128)(2,1)S(1)} %pad_maximum_fusion.2.refs_3_), channel_id=1, source_target_pairs={{0,4},{1,3},{2,6},{3,1},{4,0},{5,7},{6,2},{7,5},{8,12},{9,11},{10,... | collective-permute-start | bytes 3145736 | tf_op jit(solution)/shard_map/ppermute | solution.py:62
  37.4 24.2 %collective-permute-start.11 = (bf16[4,1,128,1024]{3,2,1,0:T(8,128)(2,1)S(1)}, bf16[4,1,128,1024]{3,2,1,0:T(8,128)(2,1)}, u32[]{:S(2)}, u32[]{:S(2)}) collective-permute-start(bf16[4,1,128,1024]{3,2,1,0:T(8,128)(2,1)S(1)} %pad_maximum_fusion.2.refs_3_), channel_id=1, source_target_pairs={{0,2},{1,5},{2,0},{3,7},{4,6},{5,1},{6,4},{7,3},{8,10},{9,13},{10,... | collective-permute-start | bytes 3145736 | tf_op jit(solution)/shard_map/ppermute | solution.py:62
  42.6 20.5 %copy-start.24 = (s32[15]{0:T(128)S(1)}, s32[15]{0:T(128)}, u32[]{:S(2)}) copy-start(s32[15]{0:T(128)} %parent_ref.1) | copy-start | bytes 184
  42.6 22.7 %copy-start.23 = (s32[4,8]{1,0:T(4,128)S(1)}, s32[4,8]{1,0:T(4,128)}, u32[]{:S(2)}) copy-start(s32[4,8]{1,0:T(4,128)} %node_ref.1) | copy-start | bytes 388
  45.7 17.6 %collective-permute-start.8 = (bf16[128,1536]{1,0:T(8,128)(2,1)}, bf16[128,1536]{1,0:T(8,128)(2,1)S(1)}, u32[]{:S(2)}, u32[]{:S(2)}) collective-permute-start(bf16[128,1536]{1,0:T(8,128)(2,1)} %get-tuple-element.46), channel_id=1, source_target_pairs={{8,0},{10,2},{12,4},{14,6},{16,8},{18,10},{20,12},{22,14},{24,16},... | collective-permute-start | bytes 1179656 | tf_op jit(solution)/shard_map/ppermute | solution.py:98
  47.0 17.6 %collective-permute-start.5 = (bf16[128,1536]{1,0:T(8,128)(2,1)}, bf16[128,1536]{1,0:T(8,128)(2,1)S(1)}, u32[]{:S(2)}, u32[]{:S(2)}) collective-permute-start(bf16[128,1536]{1,0:T(8,128)(2,1)} %get-tuple-element.46), channel_id=1, source_target_pairs={{0,8},{2,10},{4,12},{6,14},{8,16},{10,18},{12,20},{14,22},{16,24},... | collective-permute-start | bytes 1179656 | tf_op jit(solution)/shard_map/ppermute | solution.py:97
  53.3 45.5 %collective-permute-start = (bf16[128,1024]{1,0:T(8,128)(2,1)}, bf16[128,1024]{1,0:T(8,128)(2,1)}, u32[]{:S(2)}, u32[]{:S(2)}) collective-permute-start(bf16[128,1024]{1,0:T(8,128)(2,1)} %fusion), channel_id=1, source_target_pairs={{0,1},{1,0},{2,3},{3,2},{4,5},{5,4},{6,7},{7,6},{8,9},{9,8},{10,11... | collective-permute-start | bytes 786440 | tf_op jit(solution)/shard_map/ppermute | solution.py:42
  61.6 23.4 %copy-start.5 = (bf16[4,1,128,1024]{3,2,1,0:T(8,128)(2,1)}, bf16[4,1,128,1024]{3,2,1,0:T(8,128)(2,1)S(1)}, u32[]{:S(2)}) copy-start(bf16[4,1,128,1024]{3,2,1,0:T(8,128)(2,1)S(1)} %collective-permute-done.12.refs_5_) | copy-start | bytes 3145732
  61.6 15.4 %collective-permute-start.13 = (bf16[4,1,128,1024]{3,2,1,0:T(8,128)(2,1)}, bf16[4,1,128,1024]{3,2,1,0:T(8,128)(2,1)}, u32[]{:S(2)}, u32[]{:S(2)}) collective-permute-start(bf16[4,1,128,1024]{3,2,1,0:T(8,128)(2,1)} %collective-permute-done.11.refs_4_), channel_id=1, source_target_pairs={{0,4},{1,3},{2,6},{3,1},{4,0},{5,7},{6,2},{7,5},{8,12},{9,11},{10,... | collective-permute-start | bytes 3145736 | tf_op jit(solution)/shard_map/ppermute | solution.py:62
  63.3 11.2 %collective-permute-start.9 = (bf16[128,1536]{1,0:T(8,128)(2,1)S(1)}, bf16[128,1536]{1,0:T(8,128)(2,1)S(1)}, u32[]{:S(2)}, u32[]{:S(2)}) collective-permute-start(bf16[128,1536]{1,0:T(8,128)(2,1)S(1)} %collective-permute-done.8), channel_id=1, source_target_pairs={{8,0},{10,2},{12,4},{14,6},{16,8},{18,10},{20,12},{22,14},{9,1},{1... | collective-permute-start | bytes 1179656 | tf_op jit(solution)/shard_map/ppermute | solution.py:98
  64.6 11.2 %collective-permute-start.6 = (bf16[128,1536]{1,0:T(8,128)(2,1)S(1)}, bf16[128,1536]{1,0:T(8,128)(2,1)S(1)}, u32[]{:S(2)}, u32[]{:S(2)}) collective-permute-start(bf16[128,1536]{1,0:T(8,128)(2,1)S(1)} %collective-permute-done.5), channel_id=1, source_target_pairs={{8,16},{10,18},{12,20},{14,22},{16,24},{18,26},{20,28},{22,30},{9,... | collective-permute-start | bytes 1179656 | tf_op jit(solution)/shard_map/ppermute | solution.py:97
  74.5 10.4 %collective-permute-start.10 = (bf16[128,1536]{1,0:T(8,128)(2,1)S(1)}, bf16[128,1536]{1,0:T(8,128)(2,1)S(1)}, u32[]{:S(2)}, u32[]{:S(2)}) collective-permute-start(bf16[128,1536]{1,0:T(8,128)(2,1)S(1)} %collective-permute-done.9), channel_id=1, source_target_pairs={{8,0},{10,2},{12,4},{14,6},{9,1},{11,3},{13,5},{15,7}} | collective-permute-start | bytes 1179656 | tf_op jit(solution)/shard_map/ppermute | solution.py:98
  75.8 9.1 %collective-permute-start.7 = (bf16[128,1536]{1,0:T(8,128)(2,1)S(1)}, bf16[128,1536]{1,0:T(8,128)(2,1)S(1)}, u32[]{:S(2)}, u32[]{:S(2)}) collective-permute-start(bf16[128,1536]{1,0:T(8,128)(2,1)S(1)} %collective-permute-done.6), channel_id=1, source_target_pairs={{16,24},{18,26},{20,28},{22,30},{17,25},{19,27},{21,29},{23,31}} | collective-permute-start | bytes 1179656 | tf_op jit(solution)/shard_map/ppermute | solution.py:97
  77.0 8.0 %copy-start.15 = (bf16[128,1536]{1,0:T(8,128)(2,1)S(1)}, bf16[128,1536]{1,0:T(8,128)(2,1)}, u32[]{:S(2)}) copy-start(bf16[128,1536]{1,0:T(8,128)(2,1)} %get-tuple-element.46) | copy-start | bytes 1179652
  85.2 20.5 %copy-start.1 = (bf16[4,128,1536]{2,1,0:T(8,128)(2,1)}, bf16[4,128,1536]{2,1,0:T(8,128)(2,1)S(1)}, u32[]{:S(2)}) copy-start(bf16[4,128,1536]{2,1,0:T(8,128)(2,1)S(1)} %pad_maximum_fusion.1.refs_4_.refs_1_) | copy-start | bytes 4718596
  85.2 42.0 %collective-permute-start.16 = (bf16[4,128,1536]{2,1,0:T(8,128)(2,1)S(1)}, bf16[4,128,1536]{2,1,0:T(8,128)(2,1)S(1)}, u32[]{:S(2)}, u32[]{:S(2)}) collective-permute-start(bf16[4,128,1536]{2,1,0:T(8,128)(2,1)S(1)} %pad_maximum_fusion.1.refs_4_.refs_1_), channel_id=1, source_target_pairs={{0,4},{1,3},{2,6},{3,1},{4,0},{5,7},{6,2},{7,5},{8,12},{9,11},{10,... | collective-permute-start | bytes 4718600 | tf_op jit(solution)/shard_map/ppermute | solution.py:62
  87.8 39.4 %collective-permute-start.15 = (bf16[4,128,1536]{2,1,0:T(8,128)(2,1)S(1)}, bf16[4,128,1536]{2,1,0:T(8,128)(2,1)}, u32[]{:S(2)}, u32[]{:S(2)}) collective-permute-start(bf16[4,128,1536]{2,1,0:T(8,128)(2,1)S(1)} %pad_maximum_fusion.1.refs_4_.refs_1_), channel_id=1, source_target_pairs={{0,2},{1,5},{2,0},{3,7},{4,6},{5,1},{6,4},{7,3},{8,10},{9,13},{10,... | collective-permute-start | bytes 4718600 | tf_op jit(solution)/shard_map/ppermute | solution.py:62
  92.2 13.5 %collective-permute-start.22 = (bf16[128,1792]{1,0:T(8,128)(2,1)}, bf16[128,1792]{1,0:T(8,128)(2,1)}, u32[]{:S(2)}, u32[]{:S(2)}) collective-permute-start(bf16[128,1792]{1,0:T(8,128)(2,1)} %get-tuple-element.61), channel_id=1, source_target_pairs={{8,0},{10,2},{12,4},{14,6},{16,8},{18,10},{20,12},{22,14},{24,16},... | collective-permute-start | bytes 1376264 | tf_op jit(solution)/shard_map/ppermute | solution.py:98
  93.5 13.6 %collective-permute-start.19 = (bf16[128,1792]{1,0:T(8,128)(2,1)}, bf16[128,1792]{1,0:T(8,128)(2,1)}, u32[]{:S(2)}, u32[]{:S(2)}) collective-permute-start(bf16[128,1792]{1,0:T(8,128)(2,1)} %get-tuple-element.61), channel_id=1, source_target_pairs={{0,8},{2,10},{4,12},{6,14},{8,16},{10,18},{12,20},{14,22},{16,24},... | collective-permute-start | bytes 1376264 | tf_op jit(solution)/shard_map/ppermute | solution.py:97
  105.7 2.8 collective-permute-start.14
  105.8 17.0 %collective-permute-start.23 = (bf16[128,1792]{1,0:T(8,128)(2,1)}, bf16[128,1792]{1,0:T(8,128)(2,1)}, u32[]{:S(2)}, u32[]{:S(2)}) collective-permute-start(bf16[128,1792]{1,0:T(8,128)(2,1)} %collective-permute-done.22), channel_id=1, source_target_pairs={{8,0},{10,2},{12,4},{14,6},{16,8},{18,10},{20,12},{22,14},{9,1},{1... | collective-permute-start | bytes 1376264 | tf_op jit(solution)/shard_map/ppermute | solution.py:98
  107.1 17.0 %collective-permute-start.20 = (bf16[128,1792]{1,0:T(8,128)(2,1)}, bf16[128,1792]{1,0:T(8,128)(2,1)}, u32[]{:S(2)}, u32[]{:S(2)}) collective-permute-start(bf16[128,1792]{1,0:T(8,128)(2,1)} %collective-permute-done.19), channel_id=1, source_target_pairs={{8,16},{10,18},{12,20},{14,22},{16,24},{18,26},{20,28},{22,30},{9,... | collective-permute-start | bytes 1376264 | tf_op jit(solution)/shard_map/ppermute | solution.py:97
  108.5 0.7 copy-start.16
  111.3 15.9 %all-to-all-start = ((bf16[16,1,64,128]{3,2,1,0:T(8,128)(2,1)}), bf16[16,1,64,128]{3,2,1,0:T(8,128)(2,1)S(1)}, u32[]{:S(2)}, u32[]{:S(2)}) async-start(bf16[16,1,64,128]{3,2,1,0:T(8,128)(2,1)} %get-tuple-element.45), calls=%async_computation | async-start | bytes 524288 | tf_op jit(solution)/shard_map/all_to_all | solution.py:748
  122.8 12.8 %collective-permute-start.24 = (bf16[128,1792]{1,0:T(8,128)(2,1)}, bf16[128,1792]{1,0:T(8,128)(2,1)}, u32[]{:S(2)}, u32[]{:S(2)}) collective-permute-start(bf16[128,1792]{1,0:T(8,128)(2,1)} %collective-permute-done.23), channel_id=1, source_target_pairs={{8,0},{10,2},{12,4},{14,6},{9,1},{11,3},{13,5},{15,7}} | collective-permute-start | bytes 1376264 | tf_op jit(solution)/shard_map/ppermute | solution.py:98
  124.1 11.5 %collective-permute-start.21 = (bf16[128,1792]{1,0:T(8,128)(2,1)}, bf16[128,1792]{1,0:T(8,128)(2,1)}, u32[]{:S(2)}, u32[]{:S(2)}) collective-permute-start(bf16[128,1792]{1,0:T(8,128)(2,1)} %collective-permute-done.20), channel_id=1, source_target_pairs={{16,24},{18,26},{20,28},{22,30},{17,25},{19,27},{21,29},{23,31}} | collective-permute-start | bytes 1376264 | tf_op jit(solution)/shard_map/ppermute | solution.py:97
  127.2 9.1 %copy-start.9 = (bf16[16,1,64,128]{3,2,1,0:T(8,128)(2,1)}, bf16[16,1,64,128]{3,2,1,0:T(8,128)(2,1)S(1)}, u32[]{:S(2)}) copy-start(bf16[16,1,64,128]{3,2,1,0:T(8,128)(2,1)S(1)} %all-to-all-done.own_ref) | copy-start | bytes 786436
  127.2 17.0 %copy-start.3 = (bf16[4,128,1536]{2,1,0:T(8,128)(2,1)}, bf16[4,128,1536]{2,1,0:T(8,128)(2,1)S(1)}, u32[]{:S(2)}) copy-start(bf16[4,128,1536]{2,1,0:T(8,128)(2,1)S(1)} %collective-permute-done.16.refs_6_.refs_3_) | copy-start | bytes 4718596
  127.2 9.1 %collective-permute-start.17 = (bf16[16,1,64,128]{3,2,1,0:T(8,128)(2,1)S(1)}, bf16[16,1,64,128]{3,2,1,0:T(8,128)(2,1)S(1)}, u32[]{:S(2)}, u32[]{:S(2)}) collective-permute-start(bf16[16,1,64,128]{3,2,1,0:T(8,128)(2,1)S(1)} %all-to-all-done.own_ref), channel_id=1, source_target_pairs={{0,1},{1,0},{2,3},{3,2},{4,5},{5,4},{6,7},{7,6},{8,9},{9,8},{10,11... | collective-permute-start | bytes 786440 | tf_op jit(solution)/shard_map/ppermute | solution.py:301
  135.6 25.9 %collective-permute-start.25 = (bf16[4,128,1536]{2,1,0:T(8,128)(2,1)}, bf16[4,128,1536]{2,1,0:T(8,128)(2,1)S(1)}, u32[]{:S(2)}, u32[]{:S(2)}) collective-permute-start(bf16[4,128,1536]{2,1,0:T(8,128)(2,1)} %collective-permute-done.15.refs_5_.refs_2_), channel_id=1, source_target_pairs={{0,4},{1,3},{2,6},{3,1},{4,0},{5,7},{6,2},{7,5},{8,12},{9,11},{10,... | collective-permute-start | bytes 4718600 | tf_op jit(solution)/shard_map/ppermute | solution.py:62
  136.3 0.7 copy-start.18
  145.3 2.2 copy-start.14
  147.5 3.2 %copy-start.17 = (bf16[128,1024]{1,0:T(8,128)(2,1)S(1)}, bf16[128,1024]{1,0:T(8,128)(2,1)}, u32[]{:S(2)}) copy-start(bf16[128,1024]{1,0:T(8,128)(2,1)} %get-tuple-element.54) | copy-start | bytes 786436
  149.0 51.9 %collective-permute-start.28 = (bf16[4,128,1792]{2,1,0:T(8,128)(2,1)}, bf16[4,128,1792]{2,1,0:T(8,128)(2,1)}, u32[]{:S(2)}, u32[]{:S(2)}) collective-permute-start(bf16[4,128,1792]{2,1,0:T(8,128)(2,1)} %pad_maximum_fusion.refs_7_.refs_1_), channel_id=1, source_target_pairs={{0,4},{1,3},{2,6},{3,1},{4,0},{5,7},{6,2},{7,5},{8,12},{9,11},{10,... | collective-permute-start | bytes 5505032 | tf_op jit(solution)/shard_map/ppermute | solution.py:62
  150.3 50.6 %collective-permute-start.27 = (bf16[4,128,1792]{2,1,0:T(8,128)(2,1)}, bf16[4,128,1792]{2,1,0:T(8,128)(2,1)}, u32[]{:S(2)}, u32[]{:S(2)}) collective-permute-start(bf16[4,128,1792]{2,1,0:T(8,128)(2,1)} %pad_maximum_fusion.refs_7_.refs_1_), channel_id=1, source_target_pairs={{0,2},{1,5},{2,0},{3,7},{4,6},{5,1},{6,4},{7,3},{8,10},{9,13},{10,... | collective-permute-start | bytes 5505032 | tf_op jit(solution)/shard_map/ppermute | solution.py:62
  150.8 1.5 collective-permute-start.18
  161.5 1.2 copy-start.4
  170.6 31.0 %copy-start = (f32[4,128,1024]{2,1,0:T(8,128)S(1)}, f32[4,128,1024]{2,1,0:T(8,128)}, u32[]{:S(2)}) copy-start(f32[4,128,1024]{2,1,0:T(8,128)} %first_ref.1) | copy-start | bytes 6291460
  170.6 2.1 collective-permute-start.26
  172.8 0.8 copy-start.13
  176.3 26.4 %all-to-all-start.1 = ((bf16[16,2,64,128]{3,2,1,0:T(8,128)(2,1)}), bf16[16,2,64,128]{3,2,1,0:T(8,128)(2,1)S(1)}, u32[]{:S(2)}, u32[]{:S(2)}) async-start(bf16[16,2,64,128]{3,2,1,0:T(8,128)(2,1)} %get-tuple-element.59), calls=%async_computation.1 | async-start | bytes 1048576 | tf_op jit(solution)/shard_map/all_to_all | solution.py:748
  200.9 23.5 %collective-permute-start.32 = (bf16[4,128,1792]{2,1,0:T(8,128)(2,1)}, bf16[4,128,1792]{2,1,0:T(8,128)(2,1)}, u32[]{:S(2)}, u32[]{:S(2)}) collective-permute-start(bf16[4,128,1792]{2,1,0:T(8,128)(2,1)} %collective-permute-done.27.refs_8_.refs_2_), channel_id=1, source_target_pairs={{0,4},{1,3},{2,6},{3,1},{4,0},{5,7},{6,2},{7,5},{8,12},{9,11},{10,... | collective-permute-start | bytes 5505032 | tf_op jit(solution)/shard_map/ppermute | solution.py:62
  202.7 2.0 copy-start.7
  202.7 2.0 collective-permute-start.29
  202.7 5.3 %collective-permute-start.36 = (f32[128,1024]{1,0:T(8,128)}, f32[128,1024]{1,0:T(8,128)S(1)}, u32[]{:S(2)}, u32[]{:S(2)}) collective-permute-start(f32[128,1024]{1,0:T(8,128)} %get-tuple-element.89), channel_id=1, source_target_pairs={{0,1},{1,0},{2,3},{3,2},{4,5},{5,4},{6,7},{7,6},{8,9},{9,8},{10,11... | collective-permute-start | bytes 1572872 | tf_op jit(solution)/shard_map/ppermute | solution.py:42
  203.2 4.8 %collective-permute-start.31 = (f32[128,1024]{1,0:T(8,128)}, f32[128,1024]{1,0:T(8,128)S(1)}, u32[]{:S(2)}, u32[]{:S(2)}) collective-permute-start(f32[128,1024]{1,0:T(8,128)} %get-tuple-element.90), channel_id=1, source_target_pairs={{0,1},{1,0},{2,3},{3,2},{4,5},{5,4},{6,7},{7,6},{8,9},{9,8},{10,11... | collective-permute-start | bytes 1572872 | tf_op jit(solution)/shard_map/ppermute | solution.py:42
  204.7 0.8 copy-start.12
  213.5 1.6 collective-permute-start.30
  234.9 2.5 collective-permute-start.33
  237.4 0.9 copy-start.10
  241.7 26.7 %all-to-all-start.2 = ((bf16[16,3,64,128]{3,2,1,0:T(8,128)(2,1)}), bf16[16,3,64,128]{3,2,1,0:T(8,128)(2,1)S(1)}, u32[]{:S(2)}, u32[]{:S(2)}) async-start(bf16[16,3,64,128]{3,2,1,0:T(8,128)(2,1)} %get-tuple-element.72), calls=%async_computation.2 | async-start | bytes 1572864 | tf_op jit(solution)/shard_map/all_to_all | solution.py:748
  268.4 2.3 copy-start.6
  268.4 2.3 collective-permute-start.34
  270.7 0.9 copy-start.11
  280.6 1.6 collective-permute-start.35
  282.1 0.7 copy-start.19
  (1 other events, 0.6 us)
